TPU v7x, 1024 devices: a whole 8x8x8 slice. The times are simulated.
1024 devices in a mesh: outer: 128 (over y, z_lo, x), inner: 8 (over z_hi, core).
Axes of the slice: x: 8, y: 8, z: 8 (z_hi: 4, z_lo: 2; z = z_hi * 2 + z_lo), core: 2. Of those that a mesh axis runs over, the one named last changes fastest.
Arguments:
- photo_embedding_matrix: bfloat16 [131072, 1152], P(('outer', 'inner')), may hold values from -1 to 1
- sentence_embedding_matrix: bfloat16 [131072, 1152], P(('outer', 'inner')), may hold values from -1 to 1
- logit_stretch_factor: float32 [1], replicated, may hold values from 4 to 8
- logit_offset_term: float32 [1], replicated, may hold values from -4 to -2
Outputs:
- grad_image: float32 [131072, 1152], P(('outer', 'inner'))
- grad_text: float32 [131072, 1152], P(('outer', 'inner'))
All inputs are finite; a program needn't handle non-finite values.
Results may differ from a plain program's by a relative error of at most 0.0027.
Values may be sent and summed in bfloat16 or wider, within the bound.
No kernel may reach another device: no remote copies, remote signals or barrier semaphores. Data moves between devices by JAX's collectives and lax.ppermute only.
A program may use at most 32 MiB of HBM per device.

v0:
```python
import jax
import jax.numpy as jnp
from jax import lax
from jax.sharding import PartitionSpec as P


def shifted(block, axis, distance):
    devices = range(lax.axis_size(axis))
    route = [((i - distance) % len(devices), i) for i in devices]
    return lax.ppermute(block, axis, route)


def signed_multiplier(left_rows, right_rows, reciprocal_logit_temp, offset, positive):
    scores = (
        reciprocal_logit_temp
        * lax.dot_general(
            left_rows, right_rows, (((1,), (1,)), ((), ())), preferred_element_type=jnp.float32
        )
        + offset
    )
    signs = jnp.where(positive, 1.0, -1.0).astype(jnp.float32)
    return (-signs * jax.nn.sigmoid(-signs * scores) * reciprocal_logit_temp).astype(jnp.bfloat16)


def per_device(
    photo_embedding_matrix, sentence_embedding_matrix, logit_stretch_factor, logit_offset_term
):
    row_count = photo_embedding_matrix.shape[0]
    reciprocal_logit_temp = logit_stretch_factor[0]
    offset = logit_offset_term[0]
    group_text = lax.all_gather(sentence_embedding_matrix, "inner", axis=0, tiled=True)
    visiting_partner_blocks = shifted(photo_embedding_matrix, "outer", -1)
    block_rows = group_text.shape[0]
    leading_row_index = lax.axis_index("inner") * row_count
    row_index = lax.broadcasted_iota(jnp.int32, (row_count, block_rows), 0)
    column_position = lax.broadcasted_iota(jnp.int32, (row_count, block_rows), 1)
    positive = column_position == row_index + leading_row_index
    nothing = column_position < 0
    own_coef = signed_multiplier(
        photo_embedding_matrix, group_text, reciprocal_logit_temp, offset, positive
    )
    guest_coef = signed_multiplier(
        visiting_partner_blocks, group_text, reciprocal_logit_temp, offset, nothing
    )
    own_grad = jnp.dot(own_coef, group_text, preferred_element_type=jnp.float32)
    guest_grad = jnp.dot(guest_coef, group_text, preferred_element_type=jnp.float32)
    grad_image = own_grad + shifted(guest_grad, "outer", 1)
    partial_value = lax.dot_general(
        own_coef,
        photo_embedding_matrix,
        (((0,), (0,)), ((), ())),
        preferred_element_type=jnp.float32,
    )
    grad_text = lax.psum_scatter(
        partial_value
        + lax.dot_general(
            guest_coef,
            visiting_partner_blocks,
            (((0,), (0,)), ((), ())),
            preferred_element_type=jnp.float32,
        ),
        "inner",
        scatter_dimension=0,
        tiled=True,
    )
    return (grad_image, grad_text)


def solution(mesh):
    return jax.shard_map(
        per_device,
        mesh=mesh,
        in_specs=(P(("outer", "inner"), None), P(("outer", "inner"), None), P(), P()),
        out_specs=(P(("outer", "inner"), None), P(("outer", "inner"), None)),
        check_vma=False,
    )
```

profile of v0, /device:TPU:1, one launch (start us, length us, event | category | flops | bytes accessed | tf_op | source)
XLA Modules:
  0.0 149.4 jit_solution(12406149005713527695)
XLA Ops:
  7.2 0.0 all-gather.2.cloned.1.call-start
  7.2 0.7 all-gather.2.cloned.1.call-update
  7.9 0.0 reduce-scatter.2.cloned.1.call-start
  7.9 11.8 %collective-permute-start = (bf16[128,1152]{1,0:T(8,128)(2,1)}, bf16[128,1152]{1,0:T(8,128)(2,1)S(1)}, u32[]{:S(2)}, u32[]{:S(2)}) collective-permute-start(bf16[128,1152]{1,0:T(8,128)(2,1)} %param.4), channel_id=1, source_target_pairs={{8,0},{16,8},{24,16},{32,24},{40,32},{48,40},{56,48},{64,56},{72,6... | collective-permute-start | bytes 884744 | tf_op jit(solution)/shard_map/ppermute | solution.py:10
  21.0 47.5 %all-gather.2.cloned.1.call-done = bf16[1024,1152]{1,0:T(8,128)(2,1)} async-done(((bf16[128,1152]{1,0:T(8,128)(2,1)}), bf16[1024,1152]{1,0:T(8,128)(2,1)}) %all-gather.2.cloned.1.call-update) | async-done | bytes 2359312 | tf_op jit(solution)/shard_map/all_gather | solution.py:31
  68.5 0.0 copy-start.1
  68.5 2.8 %fusion.15 = bf16[128,1024]{1,0:T(8,128)(2,1)S(1)} fusion(bf16[128,1152]{1,0:T(8,128)(2,1)} %param.4, bf16[1024,1152]{1,0:T(8,128)(2,1)} %all-gather.2.cloned.1.call-done, f32[]{:T(128)} %bitcast.16, f32[]{:T(128)} %bitcast.15, s32[128]{0:T(128)S(1)} %iota_add_fusion), kind=kOutput, calls=%fused_computation.19 | convolution fusion | flops 303562752 | bytes 2916872 | tf_op jit(solution)/shard_map/dot_general | solution.py:16
  71.3 0.0 copy-done.1
  71.3 0.0 copy-start
  71.3 0.8 fusion.17
  72.2 0.0 collective-permute-done
  72.2 0.8 copy-done
  73.0 0.9 fusion.14
  73.9 2.9 %convolution_add_fusion = f32[1024,1152]{1,0:T(8,128)} fusion(f32[1024,1152]{1,0:T(8,128)S(1)} %fusion.17, bf16[128,1024]{1,0:T(8,128)(2,1)S(1)} %fusion.14, bf16[128,1152]{1,0:T(8,128)(2,1)S(1)} %collective-permute-done), kind=kOutput, calls=%fused_computation | convolution fusion | flops 303169536 | bytes 9994240 | tf_op jit(solution)/shard_map/dot_general | solution.py:56
  76.9 0.0 reduce-scatter.2.cloned.1.call-update
  76.9 0.5 fusion.16
  77.4 2.2 %collective-permute-start.1 = (f32[128,1152]{1,0:T(8,128)S(1)}, f32[128,1152]{1,0:T(8,128)S(1)}, u32[]{:S(2)}, u32[]{:S(2)}) collective-permute-start(f32[128,1152]{1,0:T(8,128)S(1)} %fusion.16), channel_id=1, source_target_pairs={{1016,0},{0,8},{8,16},{16,24},{24,32},{32,40},{40,48},{48,56},{56,... | collective-permute-start | bytes 1769480 | tf_op jit(solution)/shard_map/ppermute | solution.py:10
  79.6 20.5 %collective-permute-done.1 = f32[128,1152]{1,0:T(8,128)S(1)} collective-permute-done((f32[128,1152]{1,0:T(8,128)S(1)}, f32[128,1152]{1,0:T(8,128)S(1)}, u32[]{:S(2)}, u32[]{:S(2)}) %collective-permute-start.1) | collective-permute-done | bytes 589856 | tf_op jit(solution)/shard_map/ppermute | solution.py:10
  100.2 1.3 convolution_add_fusion.1
  101.5 41.1 %reduce-scatter.2.cloned.1.call-done = f32[128,1152]{1,0:T(8,128)} async-done(((f32[1024,1152]{1,0:T(8,128)}), f32[128,1152]{1,0:T(8,128)}) %reduce-scatter.2.cloned.1.call-update) | async-done | bytes 589840 | tf_op jit(solution)/shard_map/reduce_scatter | solution.py:54
  (1 shorter events, 0.0 us)
Async XLA Ops:
  7.2 61.4 %all-gather.2.cloned.1.call-start = ((), (), s32[]{:S(2)}) async-start(), calls=%async_computation.1 | async-start | bytes 2654208 | tf_op jit(solution)/shard_map/all_gather | solution.py:31
  7.9 134.7 %reduce-scatter.2.cloned.1.call-start = ((), (), s32[]{:S(2)}) async-start(), calls=%async_computation.2 | async-start | bytes 5308416 | tf_op jit(solution)/shard_map/reduce_scatter | solution.py:54
  7.9 64.2 %collective-permute-start = (bf16[128,1152]{1,0:T(8,128)(2,1)}, bf16[128,1152]{1,0:T(8,128)(2,1)S(1)}, u32[]{:S(2)}, u32[]{:S(2)}) collective-permute-start(bf16[128,1152]{1,0:T(8,128)(2,1)} %param.4), channel_id=1, source_target_pairs={{8,0},{16,8},{24,16},{32,24},{40,32},{48,40},{56,48},{64,56},{72,6... | collective-permute-start | bytes 884744 | tf_op jit(solution)/shard_map/ppermute | solution.py:10
  68.5 2.8 %copy-start.1 = (bf16[128,1152]{1,0:T(8,128)(2,1)S(1)}, bf16[128,1152]{1,0:T(8,128)(2,1)}, u32[]{:S(2)}) copy-start(bf16[128,1152]{1,0:T(8,128)(2,1)} %param.4) | copy-start | bytes 884740
  71.3 1.7 %copy-start = (bf16[1024,1152]{1,0:T(8,128)(2,1)S(1)}, bf16[1024,1152]{1,0:T(8,128)(2,1)}, u32[]{:S(2)}) copy-start(bf16[1024,1152]{1,0:T(8,128)(2,1)} %all-gather.2.cloned.1.call-done) | copy-start | bytes 7077892
  77.4 22.7 %collective-permute-start.1 = (f32[128,1152]{1,0:T(8,128)S(1)}, f32[128,1152]{1,0:T(8,128)S(1)}, u32[]{:S(2)}, u32[]{:S(2)}) collective-permute-start(f32[128,1152]{1,0:T(8,128)S(1)} %fusion.16), channel_id=1, source_target_pairs={{1016,0},{0,8},{8,16},{16,24},{24,32},{32,40},{40,48},{48,56},{56,... | collective-permute-start | bytes 1769480 | tf_op jit(solution)/shard_map/ppermute | solution.py:10
Sparse Core Ops, SparseCore 0:
  10.7 57.7 all-gather.1
  77.0 65.5 reduce-scatter.1
where the time goes:
time: 152 us; the launch traced here: 149 us
  waiting for transfers between devices  110 us (72%)
  between operations  15.4 us (10%)
  starting transfers between devices  14 us (9%)
  matrix products  9.32 us (6%)
    all_gather x1, waiting for transfers between devices, per_device(): lax.all_gather(sentence_embedding_matrix, 'inner', axis=0, tiled=True)  47.5 us
    reduce_scatter x1, waiting for transfers between devices, per_device(): lax.psum_scatter(partial_value + lax.dot_general(guest_coef, visiting_par...  41.1 us
    ppermute x2, waiting for transfers between devices, shifted(): return lax.ppermute(block, axis, route)  20.6 us
    ppermute x2, starting transfers between devices, shifted(): return lax.ppermute(block, axis, route)  13.9 us
    dot_general x2, matrix products, signed_multiplier(): lax.dot_general(left_rows, right_rows, (((1,), (1,)), ((), ())), preferre...  3.71 us
  transfers between devices with their start and end apart: 4, of which 3 were waited for; matrix products, arithmetic and copies ran while one was open for 4% of the time, Pallas kernels for 0%

commit v1 on v0

v1 whole, which is shorter than its diff:
```python
import jax
import jax.numpy as jnp
from jax import lax
from jax.sharding import PartitionSpec as P

F32 = jnp.float32
BF16 = jnp.bfloat16


def inner_route(move, devices):
    route = []
    for chip in range(devices // 2):
        for core in range(2):
            to_chip, to_core = move(chip, core)
            route.append((chip * 2 + core, to_chip * 2 + to_core))
    return route


def per_device(images, texts, stretch, offset_term):
    outer, inner = lax.axis_size("outer"), lax.axis_size("inner")
    chips = inner // 2
    rows = images.shape[0]
    scale, offset = stretch[0], offset_term[0]

    across = inner_route(lambda z, c: (chips - 1 - z, c), inner)
    beside = inner_route(lambda z, c: (z ^ 1, c), inner)
    other_core = inner_route(lambda z, c: (z, 1 - c), inner)
    to_previous = [(i, (i - 1) % outer) for i in range(outer)]
    to_next = [(i, (i + 1) % outer) for i in range(outer)]

    images_across = lax.ppermute(images, "inner", across)
    guests = lax.ppermute(images, "outer", to_previous)
    texts_beside = lax.ppermute(texts, "inner", beside)
    texts_core = lax.ppermute(texts, "inner", other_core)
    texts_beside_core = lax.ppermute(texts_beside, "inner", other_core)
    guests_across = lax.ppermute(images_across, "outer", to_previous)
    all_texts = jnp.concatenate([texts, texts_beside, texts_core, texts_beside_core], axis=0)

    row = lax.broadcasted_iota(jnp.int32, (rows, 4 * rows), 0)
    column = lax.broadcasted_iota(jnp.int32, (rows, 4 * rows), 1)

    def coefficients(left, positive):
        scores = scale * lax.dot_general(
            left, all_texts, (((1,), (1,)), ((), ())), preferred_element_type=F32
        ) + offset
        signs = jnp.where(positive, 1.0, -1.0).astype(F32)
        return (-signs * jax.nn.sigmoid(-signs * scores) * scale).astype(BF16)

    def image_part(coef):
        return jnp.dot(coef, all_texts, preferred_element_type=F32)

    def text_part(coef, left):
        return lax.dot_general(coef, left, (((0,), (0,)), ((), ())), preferred_element_type=F32)

    nothing = column < 0
    coef = coefficients(images, row == column)
    coef_across = coefficients(images_across, nothing)
    coef_guests = coefficients(guests, nothing)
    coef_guests_across = coefficients(guests_across, nothing)

    back_across = lax.ppermute(image_part(coef_guests_across).astype(BF16), "outer", to_next)
    back = lax.ppermute(image_part(coef_guests).astype(BF16), "outer", to_next)
    own = image_part(coef)
    own_across = image_part(coef_across)

    grad_texts = (
        text_part(coef, images)
        + text_part(coef_across, images_across)
        + text_part(coef_guests, guests)
        + text_part(coef_guests_across, guests_across)
    )
    mine, beside_mine, core, beside_core = (
        grad_texts[k * rows : (k + 1) * rows] for k in range(4)
    )
    beside_from_core = lax.ppermute(beside_core.astype(BF16), "inner", other_core)
    from_core = lax.ppermute(core.astype(BF16), "inner", other_core)
    from_beside = lax.ppermute(
        (beside_mine + beside_from_core.astype(F32)).astype(BF16), "inner", beside
    )
    from_across = lax.ppermute(
        (own_across + back_across.astype(F32)).astype(BF16), "inner", across
    )
    grad_image = own + back.astype(F32) + from_across.astype(F32)
    grad_text = mine + from_core.astype(F32) + from_beside.astype(F32)
    return grad_image, grad_text


def solution(mesh):
    block = P(("outer", "inner"), None)
    return jax.shard_map(
        per_device,
        mesh=mesh,
        in_specs=(block, block, P(), P()),
        out_specs=(block, block),
        check_vma=False,
    )
```

time: 152 us -> 88.7 us (0.58)
  waiting for transfers between devices: 110 us -> 14.4 us
  starting transfers between devices: 14 us -> 62.6 us
  between operations: 15.4 us -> 2.21 us
  matrix products: 9.32 us -> 6.1 us
    ppermute x2 -> x12, starting transfers between devices: 13.9 us -> 62.6 us  [the longest x1 10.4 us: per_device(): images_across = lax.ppermute(images, 'inner', across)]
    all_gather x1 -> x0, waiting for transfers between devices: 47.5 us -> none  [per_device(): lax.all_gather(sentence_embedding_matrix, 'inner', axis=0, tiled=True)]
    reduce_scatter x1 -> x0, waiting for transfers between devices: 41.1 us -> none  [per_device(): lax.psum_scatter(partial_value + lax.dot_general(guest_coef, visiting_par...]
    ppermute x2 -> x12, waiting for transfers between devices: 20.6 us -> 14.4 us  [the longest x1 8.41 us: per_device(): lax.ppermute((own_across + back_across.astype(F32)).astype(BF16), 'inner'...]
    dot_general x6 -> x12, matrix products: 9.32 us -> 6.1 us  [the longest x4 2.3 us: image_part(): return jnp.dot(coef, all_texts, preferred_element_type=F32)]
  transfers between devices with their start and end apart: 4 -> 12, of which waited for: 3 -> 3; matrix products, arithmetic and copies ran while one was open for 4% -> 8% of each run, Pallas kernels for 0% -> 0%
where the time goes in v1:
time: 88.7 us; the launch traced here: 87.3 us
  starting transfers between devices  62.6 us (71%)
  waiting for transfers between devices  14.4 us (16%)
  matrix products  6.1 us (7%)
  between operations  2.21 us (2%)
  local copies, waits for them, and re-layouts  1.13 us (1%)
  other arithmetic  0.95 us (1%)
    ppermute x1, starting transfers between devices, per_device(): images_across = lax.ppermute(images, 'inner', across)  10.4 us
    ppermute x1, starting transfers between devices, per_device(): lax.ppermute((own_across + back_across.astype(F32)).astype(BF16), 'inner'...  10.2 us
    ppermute x1, starting transfers between devices, per_device(): guests = lax.ppermute(images, 'outer', to_previous)  10 us
    ppermute x1, starting transfers between devices, per_device(): texts_beside = lax.ppermute(texts, 'inner', beside)  8.46 us
    ppermute x1, waiting for transfers between devices, per_device(): lax.ppermute((own_across + back_across.astype(F32)).astype(BF16), 'inner'...  8.41 us
    ppermute x1, starting transfers between devices, per_device(): guests_across = lax.ppermute(images_across, 'outer', to_previous)  6.55 us
    ppermute x1, waiting for transfers between devices, per_device(): guests_across = lax.ppermute(images_across, 'outer', to_previous)  5.31 us
    ppermute x1, starting transfers between devices, per_device(): lax.ppermute(beside_core.astype(BF16), 'inner', other_core)  3.68 us
  transfers between devices with their start and end apart: 12, of which 3 were waited for; matrix products, arithmetic and copies ran while one was open for 8% of the time, Pallas kernels for 0%

profile of v1, /device:TPU:1, one launch (start us, length us, event | category | flops | bytes accessed | tf_op | source)
XLA Modules:
  0.0 87.3 jit_solution(17400751590615333843)
XLA Ops:
  0.6 8.5 %collective-permute-start = (bf16[128,1152]{1,0:T(8,128)(2,1)}, bf16[128,1152]{1,0:T(8,128)(2,1)S(1)}, u32[]{:S(2)}, u32[]{:S(2)}) collective-permute-start(bf16[128,1152]{1,0:T(8,128)(2,1)} %param.5), channel_id=1, source_target_pairs={{0,2},{1,3},{2,0},{3,1},{4,6},{5,7},{6,4},{7,5},{8,10},{9,11},{10,... | collective-permute-start | bytes 884744 | tf_op jit(solution)/shard_map/ppermute | solution.py:33
  9.1 10.4 %collective-permute-start.5 = (bf16[128,1152]{1,0:T(8,128)(2,1)}, bf16[128,1152]{1,0:T(8,128)(2,1)S(1)}, u32[]{:S(2)}, u32[]{:S(2)}) collective-permute-start(bf16[128,1152]{1,0:T(8,128)(2,1)} %param.4), channel_id=1, source_target_pairs={{0,6},{1,7},{2,4},{3,5},{4,2},{5,3},{6,0},{7,1},{8,14},{9,15},{10,... | collective-permute-start | bytes 884744 | tf_op jit(solution)/shard_map/ppermute | solution.py:31
  19.5 2.9 %collective-permute-start.1 = (bf16[128,1152]{1,0:T(8,128)(2,1)}, bf16[128,1152]{1,0:T(8,128)(2,1)S(1)}, u32[]{:S(2)}, u32[]{:S(2)}) collective-permute-start(bf16[128,1152]{1,0:T(8,128)(2,1)} %param.5), channel_id=1, source_target_pairs={{0,1},{1,0},{2,3},{3,2},{4,5},{5,4},{6,7},{7,6},{8,9},{9,8},{10,11... | collective-permute-start | bytes 884744 | tf_op jit(solution)/shard_map/ppermute | solution.py:34
  22.4 10.0 %collective-permute-start.3 = (bf16[128,1152]{1,0:T(8,128)(2,1)}, bf16[128,1152]{1,0:T(8,128)(2,1)S(1)}, u32[]{:S(2)}, u32[]{:S(2)}) collective-permute-start(bf16[128,1152]{1,0:T(8,128)(2,1)} %param.4), channel_id=1, source_target_pairs={{0,1016},{8,0},{16,8},{24,16},{32,24},{40,32},{48,40},{56,48},{64,... | collective-permute-start | bytes 884744 | tf_op jit(solution)/shard_map/ppermute | solution.py:32
  32.4 1.0 %constant_dynamic-update-slice_fusion.3 = bf16[512,1152]{1,0:T(8,128)(2,1)S(1)} fusion(bf16[128,1152]{1,0:T(8,128)(2,1)} %param.5), kind=kLoop, calls=%fused_computation.52 | loop fusion | bytes 589824
  34.7 2.2 %collective-permute-start.2 = (bf16[128,1152]{1,0:T(8,128)(2,1)S(1)}, bf16[128,1152]{1,0:T(8,128)(2,1)S(1)}, u32[]{:S(2)}, u32[]{:S(2)}) collective-permute-start(bf16[128,1152]{1,0:T(8,128)(2,1)S(1)} %collective-permute-done), channel_id=1, source_target_pairs={{0,1},{1,0},{2,3},{3,2},{4,5},{5,4},{6,7},{7,6},{8,9},{9,8},{10,11... | collective-permute-start | bytes 884744 | tf_op jit(solution)/shard_map/ppermute | solution.py:35
  36.9 0.0 collective-permute-done.5
  36.9 6.6 %collective-permute-start.6 = (bf16[128,1152]{1,0:T(8,128)(2,1)S(1)}, bf16[128,1152]{1,0:T(8,128)(2,1)S(1)}, u32[]{:S(2)}, u32[]{:S(2)}) collective-permute-start(bf16[128,1152]{1,0:T(8,128)(2,1)S(1)} %collective-permute-done.5), channel_id=1, source_target_pairs={{0,1016},{8,0},{16,8},{24,16},{32,24},{40,32},{48,40},{56,48},{64,... | collective-permute-start | bytes 884744 | tf_op jit(solution)/shard_map/ppermute | solution.py:36
  43.6 5.3 %collective-permute-done.6 = bf16[128,1152]{1,0:T(8,128)(2,1)S(1)} collective-permute-done((bf16[128,1152]{1,0:T(8,128)(2,1)S(1)}, bf16[128,1152]{1,0:T(8,128)(2,1)S(1)}, u32[]{:S(2)}, u32[]{:S(2)}) %collective-permute-start.6) | collective-permute-done | bytes 294944 | tf_op jit(solution)/shard_map/ppermute | solution.py:36
  48.9 0.5 fusion.30
  49.4 0.0 copy-start
  49.4 0.4 convolution_convert_fusion
  49.8 1.9 %collective-permute-start.7 = (bf16[128,1152]{1,0:T(8,128)(2,1)S(1)}, bf16[128,1152]{1,0:T(8,128)(2,1)S(1)}, u32[]{:S(2)}, u32[]{:S(2)}) collective-permute-start(bf16[128,1152]{1,0:T(8,128)(2,1)S(1)} %convolution_convert_fusion), channel_id=1, source_target_pairs={{0,8},{8,16},{16,24},{24,32},{32,40},{40,48},{48,56},{56,64},{64,7... | collective-permute-start | bytes 884744 | tf_op jit(solution)/shard_map/ppermute | solution.py:61
  51.8 0.5 fusion.29
  52.3 0.4 fusion.37
  52.7 0.5 fusion.31
  53.2 0.5 convolution_add_fusion.2
  53.7 0.5 fusion.32
  54.2 0.5 convolution_add_fusion.1
  54.7 0.5 fusion.36
  55.2 3.7 %collective-permute-start.10 = (bf16[128,1152]{1,0:T(8,128)(2,1)S(1)}, bf16[128,1152]{1,0:T(8,128)(2,1)S(1)}, u32[]{:S(2)}, u32[]{:S(2)}) collective-permute-start(bf16[128,1152]{1,0:T(8,128)(2,1)S(1)} %get-tuple-element.3), channel_id=1, source_target_pairs={{0,1},{1,0},{2,3},{3,2},{4,5},{5,4},{6,7},{7,6},{8,9},{9,8},{10,11... | collective-permute-start | bytes 884744 | tf_op jit(solution)/shard_map/ppermute | solution.py:75
  58.9 0.4 convolution_convert_fusion.1
  59.2 1.9 %collective-permute-start.4 = (bf16[128,1152]{1,0:T(8,128)(2,1)S(1)}, bf16[128,1152]{1,0:T(8,128)(2,1)S(1)}, u32[]{:S(2)}, u32[]{:S(2)}) collective-permute-start(bf16[128,1152]{1,0:T(8,128)(2,1)S(1)} %convolution_convert_fusion.1), channel_id=1, source_target_pairs={{0,8},{8,16},{16,24},{24,32},{32,40},{40,48},{48,56},{56,64},{64,7... | collective-permute-start | bytes 884744 | tf_op jit(solution)/shard_map/ppermute | solution.py:62
  61.2 1.9 %collective-permute-start.9 = (bf16[128,1152]{1,0:T(8,128)(2,1)S(1)}, bf16[128,1152]{1,0:T(8,128)(2,1)S(1)}, u32[]{:S(2)}, u32[]{:S(2)}) collective-permute-start(bf16[128,1152]{1,0:T(8,128)(2,1)S(1)} %get-tuple-element.2), channel_id=1, source_target_pairs={{0,1},{1,0},{2,3},{3,2},{4,5},{5,4},{6,7},{7,6},{8,9},{9,8},{10,11... | collective-permute-start | bytes 884744 | tf_op jit(solution)/shard_map/ppermute | solution.py:76
  63.1 0.6 collective-permute-done.7
  63.7 0.4 fusion.1
  64.1 10.2 %collective-permute-start.8 = (bf16[128,1152]{1,0:T(8,128)(2,1)S(1)}, bf16[128,1152]{1,0:T(8,128)(2,1)S(1)}, u32[]{:S(2)}, u32[]{:S(2)}) collective-permute-start(bf16[128,1152]{1,0:T(8,128)(2,1)S(1)} %fusion.1), channel_id=1, source_target_pairs={{0,6},{1,7},{2,4},{3,5},{4,2},{5,3},{6,0},{7,1},{8,14},{9,15},{10,... | collective-permute-start | bytes 884744 | tf_op jit(solution)/shard_map/ppermute | solution.py:80
  74.3 0.1 fusion.33
  74.4 2.4 %collective-permute-start.11 = (bf16[128,1152]{1,0:T(8,128)(2,1)S(1)}, bf16[128,1152]{1,0:T(8,128)(2,1)S(1)}, u32[]{:S(2)}, u32[]{:S(2)}) collective-permute-start(bf16[128,1152]{1,0:T(8,128)(2,1)S(1)} %fusion.33), channel_id=1, source_target_pairs={{0,2},{1,3},{2,0},{3,1},{4,6},{5,7},{6,4},{7,5},{8,10},{9,11},{10,... | collective-permute-start | bytes 884744 | tf_op jit(solution)/shard_map/ppermute | solution.py:77
  76.8 8.4 %collective-permute-done.8 = bf16[128,1152]{1,0:T(8,128)(2,1)S(1)} collective-permute-done((bf16[128,1152]{1,0:T(8,128)(2,1)S(1)}, bf16[128,1152]{1,0:T(8,128)(2,1)S(1)}, u32[]{:S(2)}, u32[]{:S(2)}) %collective-permute-start.8) | collective-permute-done | bytes 294944 | tf_op jit(solution)/shard_map/ppermute | solution.py:80
  85.2 1.2 %fusion = f32[128,1152]{1,0:T(8,128)} fusion(bf16[128,512]{0,1:T(8,128)(2,1)S(1)} %fusion.29, bf16[512,1152]{1,0:T(8,128)(2,1)S(1)} %constant_dynamic-update-slice_fusion, bf16[128,1152]{1,0:T(8,128)(2,1)S(1)} %collective-permute-done.8, bf16[128,1152]{1,0:T(8,128)(2,1)S(1)} %collective-permute-done.4), kind=kOutput, calls=%fused_computation.5 | convolution fusion | flops 151584768 | bytes 2490368 | tf_op jit(solution)/shard_map/dot_general | solution.py:50
  86.4 0.9 %fusion.34 = f32[128,1152]{1,0:T(8,128)} fusion(f32[512,1152]{1,0:T(8,128)S(1)} %get-tuple-element.5, bf16[128,1152]{1,0:T(8,128)(2,1)S(1)} %collective-permute-done.11, bf16[128,1152]{1,0:T(8,128)(2,1)S(1)} %collective-permute-done.9), kind=kLoop, calls=%fused_computation.47 | loop fusion | flops 589824 | bytes 1769472 | tf_op jit(solution)/shard_map/add | solution.py:84
  (13 shorter events, 0.2 us)
Async XLA Ops:
  0.6 34.1 %collective-permute-start = (bf16[128,1152]{1,0:T(8,128)(2,1)}, bf16[128,1152]{1,0:T(8,128)(2,1)S(1)}, u32[]{:S(2)}, u32[]{:S(2)}) collective-permute-start(bf16[128,1152]{1,0:T(8,128)(2,1)} %param.5), channel_id=1, source_target_pairs={{0,2},{1,3},{2,0},{3,1},{4,6},{5,7},{6,4},{7,5},{8,10},{9,11},{10,... | collective-permute-start | bytes 884744 | tf_op jit(solution)/shard_map/ppermute | solution.py:33
  9.1 27.8 %collective-permute-start.5 = (bf16[128,1152]{1,0:T(8,128)(2,1)}, bf16[128,1152]{1,0:T(8,128)(2,1)S(1)}, u32[]{:S(2)}, u32[]{:S(2)}) collective-permute-start(bf16[128,1152]{1,0:T(8,128)(2,1)} %param.4), channel_id=1, source_target_pairs={{0,6},{1,7},{2,4},{3,5},{4,2},{5,3},{6,0},{7,1},{8,14},{9,15},{10,... | collective-permute-start | bytes 884744 | tf_op jit(solution)/shard_map/ppermute | solution.py:31
  19.5 24.0 %collective-permute-start.1 = (bf16[128,1152]{1,0:T(8,128)(2,1)}, bf16[128,1152]{1,0:T(8,128)(2,1)S(1)}, u32[]{:S(2)}, u32[]{:S(2)}) collective-permute-start(bf16[128,1152]{1,0:T(8,128)(2,1)} %param.5), channel_id=1, source_target_pairs={{0,1},{1,0},{2,3},{3,2},{4,5},{5,4},{6,7},{7,6},{8,9},{9,8},{10,11... | collective-permute-start | bytes 884744 | tf_op jit(solution)/shard_map/ppermute | solution.py:34
  22.4 31.3 %collective-permute-start.3 = (bf16[128,1152]{1,0:T(8,128)(2,1)}, bf16[128,1152]{1,0:T(8,128)(2,1)S(1)}, u32[]{:S(2)}, u32[]{:S(2)}) collective-permute-start(bf16[128,1152]{1,0:T(8,128)(2,1)} %param.4), channel_id=1, source_target_pairs={{0,1016},{8,0},{16,8},{24,16},{32,24},{40,32},{48,40},{56,48},{64,... | collective-permute-start | bytes 884744 | tf_op jit(solution)/shard_map/ppermute | solution.py:32
  34.7 8.9 %collective-permute-start.2 = (bf16[128,1152]{1,0:T(8,128)(2,1)S(1)}, bf16[128,1152]{1,0:T(8,128)(2,1)S(1)}, u32[]{:S(2)}, u32[]{:S(2)}) collective-permute-start(bf16[128,1152]{1,0:T(8,128)(2,1)S(1)} %collective-permute-done), channel_id=1, source_target_pairs={{0,1},{1,0},{2,3},{3,2},{4,5},{5,4},{6,7},{7,6},{8,9},{9,8},{10,11... | collective-permute-start | bytes 884744 | tf_op jit(solution)/shard_map/ppermute | solution.py:35
  36.9 12.0 %collective-permute-start.6 = (bf16[128,1152]{1,0:T(8,128)(2,1)S(1)}, bf16[128,1152]{1,0:T(8,128)(2,1)S(1)}, u32[]{:S(2)}, u32[]{:S(2)}) collective-permute-start(bf16[128,1152]{1,0:T(8,128)(2,1)S(1)} %collective-permute-done.5), channel_id=1, source_target_pairs={{0,1016},{8,0},{16,8},{24,16},{32,24},{40,32},{48,40},{56,48},{64,... | collective-permute-start | bytes 884744 | tf_op jit(solution)/shard_map/ppermute | solution.py:36
  49.4 2.3 %copy-start = (bf16[128,1152]{1,0:T(8,128)(2,1)S(1)}, bf16[128,1152]{1,0:T(8,128)(2,1)}, u32[]{:S(2)}) copy-start(bf16[128,1152]{1,0:T(8,128)(2,1)} %param.4) | copy-start | bytes 884740
  49.8 13.9 %collective-permute-start.7 = (bf16[128,1152]{1,0:T(8,128)(2,1)S(1)}, bf16[128,1152]{1,0:T(8,128)(2,1)S(1)}, u32[]{:S(2)}, u32[]{:S(2)}) collective-permute-start(bf16[128,1152]{1,0:T(8,128)(2,1)S(1)} %convolution_convert_fusion), channel_id=1, source_target_pairs={{0,8},{8,16},{16,24},{24,32},{32,40},{40,48},{48,56},{56,64},{64,7... | collective-permute-start | bytes 884744 | tf_op jit(solution)/shard_map/ppermute | solution.py:61
  55.2 19.2 %collective-permute-start.10 = (bf16[128,1152]{1,0:T(8,128)(2,1)S(1)}, bf16[128,1152]{1,0:T(8,128)(2,1)S(1)}, u32[]{:S(2)}, u32[]{:S(2)}) collective-permute-start(bf16[128,1152]{1,0:T(8,128)(2,1)S(1)} %get-tuple-element.3), channel_id=1, source_target_pairs={{0,1},{1,0},{2,3},{3,2},{4,5},{5,4},{6,7},{7,6},{8,9},{9,8},{10,11... | collective-permute-start | bytes 884744 | tf_op jit(solution)/shard_map/ppermute | solution.py:75
  59.2 17.6 %collective-permute-start.4 = (bf16[128,1152]{1,0:T(8,128)(2,1)S(1)}, bf16[128,1152]{1,0:T(8,128)(2,1)S(1)}, u32[]{:S(2)}, u32[]{:S(2)}) collective-permute-start(bf16[128,1152]{1,0:T(8,128)(2,1)S(1)} %convolution_convert_fusion.1), channel_id=1, source_target_pairs={{0,8},{8,16},{16,24},{24,32},{32,40},{40,48},{48,56},{56,64},{64,7... | collective-permute-start | bytes 884744 | tf_op jit(solution)/shard_map/ppermute | solution.py:62
  61.2 25.2 %collective-permute-start.9 = (bf16[128,1152]{1,0:T(8,128)(2,1)S(1)}, bf16[128,1152]{1,0:T(8,128)(2,1)S(1)}, u32[]{:S(2)}, u32[]{:S(2)}) collective-permute-start(bf16[128,1152]{1,0:T(8,128)(2,1)S(1)} %get-tuple-element.2), channel_id=1, source_target_pairs={{0,1},{1,0},{2,3},{3,2},{4,5},{5,4},{6,7},{7,6},{8,9},{9,8},{10,11... | collective-permute-start | bytes 884744 | tf_op jit(solution)/shard_map/ppermute | solution.py:76
  64.1 21.1 %collective-permute-start.8 = (bf16[128,1152]{1,0:T(8,128)(2,1)S(1)}, bf16[128,1152]{1,0:T(8,128)(2,1)S(1)}, u32[]{:S(2)}, u32[]{:S(2)}) collective-permute-start(bf16[128,1152]{1,0:T(8,128)(2,1)S(1)} %fusion.1), channel_id=1, source_target_pairs={{0,6},{1,7},{2,4},{3,5},{4,2},{5,3},{6,0},{7,1},{8,14},{9,15},{10,... | collective-permute-start | bytes 884744 | tf_op jit(solution)/shard_map/ppermute | solution.py:80
  74.4 12.0 %collective-permute-start.11 = (bf16[128,1152]{1,0:T(8,128)(2,1)S(1)}, bf16[128,1152]{1,0:T(8,128)(2,1)S(1)}, u32[]{:S(2)}, u32[]{:S(2)}) collective-permute-start(bf16[128,1152]{1,0:T(8,128)(2,1)S(1)} %fusion.33), channel_id=1, source_target_pairs={{0,2},{1,3},{2,0},{3,1},{4,6},{5,7},{6,4},{7,5},{8,10},{9,11},{10,... | collective-permute-start | bytes 884744 | tf_op jit(solution)/shard_map/ppermute | solution.py:77

commit v2 on v1

--- a/solution.py
+++ b/solution.py
@@ -29,11 +29,11 @@
     to_next = [(i, (i + 1) % outer) for i in range(outer)]
 
     images_across = lax.ppermute(images, "inner", across)
-    guests = lax.ppermute(images, "outer", to_previous)
     texts_beside = lax.ppermute(texts, "inner", beside)
     texts_core = lax.ppermute(texts, "inner", other_core)
+    guests = lax.ppermute(images, "outer", to_previous)
+    guests_across = lax.ppermute(images_across, "outer", to_previous)
     texts_beside_core = lax.ppermute(texts_beside, "inner", other_core)
-    guests_across = lax.ppermute(images_across, "outer", to_previous)
     all_texts = jnp.concatenate([texts, texts_beside, texts_core, texts_beside_core], axis=0)
 
     row = lax.broadcasted_iota(jnp.int32, (rows, 4 * rows), 0)
@@ -53,35 +53,33 @@
         return lax.dot_general(coef, left, (((0,), (0,)), ((), ())), preferred_element_type=F32)
 
     nothing = column < 0
+    coef_guests = coefficients(guests, nothing)
+    guests_part = image_part(coef_guests).astype(BF16)
+    back = lax.ppermute(guests_part, "outer", to_next)
+
+    coef_guests_across = coefficients(guests_across, nothing)
+    guests_across_part = image_part(coef_guests_across).astype(BF16)
+    back_across = lax.ppermute(guests_across_part, "outer", to_next)
+
     coef = coefficients(images, row == column)
     coef_across = coefficients(images_across, nothing)
-    coef_guests = coefficients(guests, nothing)
-    coef_guests_across = coefficients(guests_across, nothing)
-
-    back_across = lax.ppermute(image_part(coef_guests_across).astype(BF16), "outer", to_next)
-    back = lax.ppermute(image_part(coef_guests).astype(BF16), "outer", to_next)
-    own = image_part(coef)
-    own_across = image_part(coef_across)
-
     grad_texts = (
         text_part(coef, images)
         + text_part(coef_across, images_across)
         + text_part(coef_guests, guests)
         + text_part(coef_guests_across, guests_across)
     )
-    mine, beside_mine, core, beside_core = (
-        grad_texts[k * rows : (k + 1) * rows] for k in range(4)
-    )
-    beside_from_core = lax.ppermute(beside_core.astype(BF16), "inner", other_core)
-    from_core = lax.ppermute(core.astype(BF16), "inner", other_core)
-    from_beside = lax.ppermute(
-        (beside_mine + beside_from_core.astype(F32)).astype(BF16), "inner", beside
-    )
+    from_core = lax.ppermute(grad_texts[2 * rows :].astype(BF16), "inner", other_core)
+    own = image_part(coef)
+    own_across = image_part(coef_across)
+    both = grad_texts[: 2 * rows] + from_core.astype(F32)
+    own, own_across, back_across = lax.optimization_barrier((own, own_across, back_across))
+    from_beside = lax.ppermute(both[rows:].astype(BF16), "inner", beside)
     from_across = lax.ppermute(
         (own_across + back_across.astype(F32)).astype(BF16), "inner", across
     )
+    grad_text = both[:rows] + from_beside.astype(F32)
     grad_image = own + back.astype(F32) + from_across.astype(F32)
-    grad_text = mine + from_core.astype(F32) + from_beside.astype(F32)
     return grad_image, grad_text
 
 

time: 88.7 us -> 87.6 us (0.988); the launches traced: 87.3 us -> 87.1 us
  starting transfers between devices: 62.6 us -> 60.2 us
  waiting for transfers between devices: 14.4 us -> 16.3 us
  other arithmetic: 0.95 us -> 1.91 us
    ppermute x5 -> x4, starting transfers between devices: 11.8 us -> 9.44 us  [the longest x1 3.68 us: per_device(): lax.ppermute(grad_texts[2 * rows:].astype(BF16), 'inner', other_core)]
    ppermute x5 -> x4, waiting for transfers between devices: 0.63 us -> 1.77 us  [the longest x1 1.77 us: per_device(): back_across = lax.ppermute(guests_across_part, 'outer', to_next)]
    add x1 -> x3, other arithmetic: 0.9 us -> 1.86 us  [the longest x1 0.89 us: per_device(): grad_image = own + back.astype(F32) + from_across.astype(F32)]
  transfers between devices with their start and end apart: 12 -> 11, of which waited for: 3 -> 3; matrix products, arithmetic and copies ran while one was open for 8% -> 9% of each run, Pallas kernels for 0% -> 0%
where the time goes in v2:
time: 87.6 us; the launch traced here: 87.1 us
  starting transfers between devices  60.2 us (69%)
  waiting for transfers between devices  16.3 us (19%)
  matrix products  5.29 us (6%)
  between operations  2.22 us (3%)
  other arithmetic  1.91 us (2%)
  local copies, waits for them, and re-layouts  1.19 us (1%)
    ppermute x1, starting transfers between devices, per_device(): images_across = lax.ppermute(images, 'inner', across)  10.4 us
    ppermute x1, starting transfers between devices, per_device(): lax.ppermute((own_across + back_across.astype(F32)).astype(BF16), 'inner'...  10.2 us
    ppermute x1, starting transfers between devices, per_device(): guests = lax.ppermute(images, 'outer', to_previous)  10 us
    ppermute x1, waiting for transfers between devices, per_device(): lax.ppermute((own_across + back_across.astype(F32)).astype(BF16), 'inner'...  9.22 us
    ppermute x1, starting transfers between devices, per_device(): texts_beside = lax.ppermute(texts, 'inner', beside)  8.46 us
    ppermute x1, starting transfers between devices, per_device(): guests_across = lax.ppermute(images_across, 'outer', to_previous)  6.55 us
    ppermute x1, waiting for transfers between devices, per_device(): guests_across = lax.ppermute(images_across, 'outer', to_previous)  5.31 us
    ppermute x1, starting transfers between devices, per_device(): lax.ppermute(grad_texts[2 * rows:].astype(BF16), 'inner', other_core)  3.68 us
  transfers between devices with their start and end apart: 11, of which 3 were waited for; matrix products, arithmetic and copies ran while one was open for 9% of the time, Pallas kernels for 0%

profile of v2, /device:TPU:1, one launch (start us, length us, event | category | flops | bytes accessed | tf_op | source)
XLA Modules:
  0.0 87.1 jit_solution(639047246663200509)
XLA Ops:
  0.6 8.5 %collective-permute-start = (bf16[128,1152]{1,0:T(8,128)(2,1)}, bf16[128,1152]{1,0:T(8,128)(2,1)S(1)}, u32[]{:S(2)}, u32[]{:S(2)}) collective-permute-start(bf16[128,1152]{1,0:T(8,128)(2,1)} %param.5), channel_id=1, source_target_pairs={{0,2},{1,3},{2,0},{3,1},{4,6},{5,7},{6,4},{7,5},{8,10},{9,11},{10,... | collective-permute-start | bytes 884744 | tf_op jit(solution)/shard_map/ppermute | solution.py:32
  9.1 10.4 %collective-permute-start.3 = (bf16[128,1152]{1,0:T(8,128)(2,1)}, bf16[128,1152]{1,0:T(8,128)(2,1)S(1)}, u32[]{:S(2)}, u32[]{:S(2)}) collective-permute-start(bf16[128,1152]{1,0:T(8,128)(2,1)} %param.4), channel_id=1, source_target_pairs={{0,6},{1,7},{2,4},{3,5},{4,2},{5,3},{6,0},{7,1},{8,14},{9,15},{10,... | collective-permute-start | bytes 884744 | tf_op jit(solution)/shard_map/ppermute | solution.py:31
  19.5 2.9 %collective-permute-start.1 = (bf16[128,1152]{1,0:T(8,128)(2,1)}, bf16[128,1152]{1,0:T(8,128)(2,1)S(1)}, u32[]{:S(2)}, u32[]{:S(2)}) collective-permute-start(bf16[128,1152]{1,0:T(8,128)(2,1)} %param.5), channel_id=1, source_target_pairs={{0,1},{1,0},{2,3},{3,2},{4,5},{5,4},{6,7},{7,6},{8,9},{9,8},{10,11... | collective-permute-start | bytes 884744 | tf_op jit(solution)/shard_map/ppermute | solution.py:33
  22.4 10.0 %collective-permute-start.6 = (bf16[128,1152]{1,0:T(8,128)(2,1)}, bf16[128,1152]{1,0:T(8,128)(2,1)S(1)}, u32[]{:S(2)}, u32[]{:S(2)}) collective-permute-start(bf16[128,1152]{1,0:T(8,128)(2,1)} %param.4), channel_id=1, source_target_pairs={{0,1016},{8,0},{16,8},{24,16},{32,24},{40,32},{48,40},{56,48},{64,... | collective-permute-start | bytes 884744 | tf_op jit(solution)/shard_map/ppermute | solution.py:34
  32.4 1.0 %constant_dynamic-update-slice_fusion.3 = bf16[512,1152]{1,0:T(8,128)(2,1)S(1)} fusion(bf16[128,1152]{1,0:T(8,128)(2,1)} %param.5), kind=kLoop, calls=%fused_computation.50 | loop fusion | bytes 589824
  34.7 2.2 %collective-permute-start.2 = (bf16[128,1152]{1,0:T(8,128)(2,1)S(1)}, bf16[128,1152]{1,0:T(8,128)(2,1)S(1)}, u32[]{:S(2)}, u32[]{:S(2)}) collective-permute-start(bf16[128,1152]{1,0:T(8,128)(2,1)S(1)} %collective-permute-done), channel_id=1, source_target_pairs={{0,1},{1,0},{2,3},{3,2},{4,5},{5,4},{6,7},{7,6},{8,9},{9,8},{10,11... | collective-permute-start | bytes 884744 | tf_op jit(solution)/shard_map/ppermute | solution.py:36
  36.9 6.6 %collective-permute-start.4 = (bf16[128,1152]{1,0:T(8,128)(2,1)S(1)}, bf16[128,1152]{1,0:T(8,128)(2,1)S(1)}, u32[]{:S(2)}, u32[]{:S(2)}) collective-permute-start(bf16[128,1152]{1,0:T(8,128)(2,1)S(1)} %collective-permute-done.3), channel_id=1, source_target_pairs={{0,1016},{8,0},{16,8},{24,16},{32,24},{40,32},{48,40},{56,48},{64,... | collective-permute-start | bytes 884744 | tf_op jit(solution)/shard_map/ppermute | solution.py:35
  43.6 5.3 %collective-permute-done.4 = bf16[128,1152]{1,0:T(8,128)(2,1)S(1)} collective-permute-done((bf16[128,1152]{1,0:T(8,128)(2,1)S(1)}, bf16[128,1152]{1,0:T(8,128)(2,1)S(1)}, u32[]{:S(2)}, u32[]{:S(2)}) %collective-permute-start.4) | collective-permute-done | bytes 294944 | tf_op jit(solution)/shard_map/ppermute | solution.py:35
  48.9 0.5 fusion.29
  49.4 0.4 convolution_convert_fusion.1
  49.8 1.9 %collective-permute-start.5 = (bf16[128,1152]{1,0:T(8,128)(2,1)S(1)}, bf16[128,1152]{1,0:T(8,128)(2,1)S(1)}, u32[]{:S(2)}, u32[]{:S(2)}) collective-permute-start(bf16[128,1152]{1,0:T(8,128)(2,1)S(1)} %convolution_convert_fusion.1), channel_id=1, source_target_pairs={{0,8},{8,16},{16,24},{24,32},{32,40},{40,48},{48,56},{56,64},{64,7... | collective-permute-start | bytes 884744 | tf_op jit(solution)/shard_map/ppermute | solution.py:62
  51.8 0.5 fusion.27
  52.3 0.4 fusion.33
  52.7 0.5 fusion.30
  53.2 0.5 convolution_add_fusion.2
  53.7 0.4 fusion.31
  54.1 0.5 fusion.28
  54.6 0.5 convolution_add_fusion.1
  55.0 0.5 convolution_add_fusion
  55.5 0.4 fusion.32
  55.9 0.1 slice.26
  56.0 3.7 %collective-permute-start.9 = (bf16[256,1152]{1,0:T(8,128)(2,1)S(1)}, bf16[256,1152]{1,0:T(8,128)(2,1)S(1)}, u32[]{:S(2)}, u32[]{:S(2)}) collective-permute-start(bf16[256,1152]{1,0:T(8,128)(2,1)S(1)} %slice.26), channel_id=1, source_target_pairs={{0,1},{1,0},{2,3},{3,2},{4,5},{5,4},{6,7},{7,6},{8,9},{9,8},{10,11... | collective-permute-start | bytes 1769480 | tf_op jit(solution)/shard_map/ppermute | solution.py:72
  59.6 0.4 convolution_convert_fusion
  60.0 1.9 %collective-permute-start.7 = (bf16[128,1152]{1,0:T(8,128)(2,1)S(1)}, bf16[128,1152]{1,0:T(8,128)(2,1)S(1)}, u32[]{:S(2)}, u32[]{:S(2)}) collective-permute-start(bf16[128,1152]{1,0:T(8,128)(2,1)S(1)} %convolution_convert_fusion), channel_id=1, source_target_pairs={{0,8},{8,16},{16,24},{24,32},{32,40},{40,48},{48,56},{56,64},{64,7... | collective-permute-start | bytes 884744 | tf_op jit(solution)/shard_map/ppermute | solution.py:58
  62.0 1.8 %collective-permute-done.5 = bf16[128,1152]{1,0:T(8,128)(2,1)S(1)} collective-permute-done((bf16[128,1152]{1,0:T(8,128)(2,1)S(1)}, bf16[128,1152]{1,0:T(8,128)(2,1)S(1)}, u32[]{:S(2)}, u32[]{:S(2)}) %collective-permute-start.5) | collective-permute-done | bytes 294944 | tf_op jit(solution)/shard_map/ppermute | solution.py:62
  63.7 0.1 add_convert_fusion
  63.8 10.2 %collective-permute-start.8 = (bf16[128,1152]{1,0:T(8,128)(2,1)S(1)}, bf16[128,1152]{1,0:T(8,128)(2,1)S(1)}, u32[]{:S(2)}, u32[]{:S(2)}) collective-permute-start(bf16[128,1152]{1,0:T(8,128)(2,1)S(1)} %add_convert_fusion), channel_id=1, source_target_pairs={{0,6},{1,7},{2,4},{3,5},{4,2},{5,3},{6,0},{7,1},{8,14},{9,15},{10,... | collective-permute-start | bytes 884744 | tf_op jit(solution)/shard_map/ppermute | solution.py:78
  74.0 0.1 slice_add_fusion
  74.2 1.9 %collective-permute-start.10 = (bf16[128,1152]{1,0:T(8,128)(2,1)S(1)}, bf16[128,1152]{1,0:T(8,128)(2,1)S(1)}, u32[]{:S(2)}, u32[]{:S(2)}) collective-permute-start(bf16[128,1152]{1,0:T(8,128)(2,1)S(1)} %slice.27), channel_id=1, source_target_pairs={{0,2},{1,3},{2,0},{3,1},{4,6},{5,7},{6,4},{7,5},{8,10},{9,11},{10,... | collective-permute-start | bytes 884744 | tf_op jit(solution)/shard_map/ppermute | solution.py:77
  76.1 9.2 %collective-permute-done.8 = bf16[128,1152]{1,0:T(8,128)(2,1)S(1)} collective-permute-done((bf16[128,1152]{1,0:T(8,128)(2,1)S(1)}, bf16[128,1152]{1,0:T(8,128)(2,1)S(1)}, u32[]{:S(2)}, u32[]{:S(2)}) %collective-permute-start.8) | collective-permute-done | bytes 294944 | tf_op jit(solution)/shard_map/ppermute | solution.py:78
  85.3 0.9 %convert_add_fusion = f32[128,1152]{1,0:T(8,128)} fusion(bf16[128,1152]{1,0:T(8,128)(2,1)S(1)} %collective-permute-done.8, f32[128,1152]{1,0:T(8,128)S(1)} %fusion.31, bf16[128,1152]{1,0:T(8,128)(2,1)S(1)} %collective-permute-done.7), kind=kLoop, calls=%fused_computation.44 | loop fusion | flops 589824 | bytes 1769472 | tf_op jit(solution)/shard_map/add | solution.py:82
  86.2 0.9 slice_add_fusion.1
  (14 shorter events, 0.2 us)
Async XLA Ops:
  0.6 34.1 %collective-permute-start = (bf16[128,1152]{1,0:T(8,128)(2,1)}, bf16[128,1152]{1,0:T(8,128)(2,1)S(1)}, u32[]{:S(2)}, u32[]{:S(2)}) collective-permute-start(bf16[128,1152]{1,0:T(8,128)(2,1)} %param.5), channel_id=1, source_target_pairs={{0,2},{1,3},{2,0},{3,1},{4,6},{5,7},{6,4},{7,5},{8,10},{9,11},{10,... | collective-permute-start | bytes 884744 | tf_op jit(solution)/shard_map/ppermute | solution.py:32
  9.1 27.8 %collective-permute-start.3 = (bf16[128,1152]{1,0:T(8,128)(2,1)}, bf16[128,1152]{1,0:T(8,128)(2,1)S(1)}, u32[]{:S(2)}, u32[]{:S(2)}) collective-permute-start(bf16[128,1152]{1,0:T(8,128)(2,1)} %param.4), channel_id=1, source_target_pairs={{0,6},{1,7},{2,4},{3,5},{4,2},{5,3},{6,0},{7,1},{8,14},{9,15},{10,... | collective-permute-start | bytes 884744 | tf_op jit(solution)/shard_map/ppermute | solution.py:31
  19.5 24.0 %collective-permute-start.1 = (bf16[128,1152]{1,0:T(8,128)(2,1)}, bf16[128,1152]{1,0:T(8,128)(2,1)S(1)}, u32[]{:S(2)}, u32[]{:S(2)}) collective-permute-start(bf16[128,1152]{1,0:T(8,128)(2,1)} %param.5), channel_id=1, source_target_pairs={{0,1},{1,0},{2,3},{3,2},{4,5},{5,4},{6,7},{7,6},{8,9},{9,8},{10,11... | collective-permute-start | bytes 884744 | tf_op jit(solution)/shard_map/ppermute | solution.py:33
  22.4 31.7 %collective-permute-start.6 = (bf16[128,1152]{1,0:T(8,128)(2,1)}, bf16[128,1152]{1,0:T(8,128)(2,1)S(1)}, u32[]{:S(2)}, u32[]{:S(2)}) collective-permute-start(bf16[128,1152]{1,0:T(8,128)(2,1)} %param.4), channel_id=1, source_target_pairs={{0,1016},{8,0},{16,8},{24,16},{32,24},{40,32},{48,40},{56,48},{64,... | collective-permute-start | bytes 884744 | tf_op jit(solution)/shard_map/ppermute | solution.py:34
  34.7 8.9 %collective-permute-start.2 = (bf16[128,1152]{1,0:T(8,128)(2,1)S(1)}, bf16[128,1152]{1,0:T(8,128)(2,1)S(1)}, u32[]{:S(2)}, u32[]{:S(2)}) collective-permute-start(bf16[128,1152]{1,0:T(8,128)(2,1)S(1)} %collective-permute-done), channel_id=1, source_target_pairs={{0,1},{1,0},{2,3},{3,2},{4,5},{5,4},{6,7},{7,6},{8,9},{9,8},{10,11... | collective-permute-start | bytes 884744 | tf_op jit(solution)/shard_map/ppermute | solution.py:36
  36.9 12.0 %collective-permute-start.4 = (bf16[128,1152]{1,0:T(8,128)(2,1)S(1)}, bf16[128,1152]{1,0:T(8,128)(2,1)S(1)}, u32[]{:S(2)}, u32[]{:S(2)}) collective-permute-start(bf16[128,1152]{1,0:T(8,128)(2,1)S(1)} %collective-permute-done.3), channel_id=1, source_target_pairs={{0,1016},{8,0},{16,8},{24,16},{32,24},{40,32},{48,40},{56,48},{64,... | collective-permute-start | bytes 884744 | tf_op jit(solution)/shard_map/ppermute | solution.py:35
  49.4 2.3 %copy-start = (bf16[128,1152]{1,0:T(8,128)(2,1)S(1)}, bf16[128,1152]{1,0:T(8,128)(2,1)}, u32[]{:S(2)}) copy-start(bf16[128,1152]{1,0:T(8,128)(2,1)} %param.4) | copy-start | bytes 884740
  49.8 13.9 %collective-permute-start.5 = (bf16[128,1152]{1,0:T(8,128)(2,1)S(1)}, bf16[128,1152]{1,0:T(8,128)(2,1)S(1)}, u32[]{:S(2)}, u32[]{:S(2)}) collective-permute-start(bf16[128,1152]{1,0:T(8,128)(2,1)S(1)} %convolution_convert_fusion.1), channel_id=1, source_target_pairs={{0,8},{8,16},{16,24},{24,32},{32,40},{40,48},{48,56},{56,64},{64,7... | collective-permute-start | bytes 884744 | tf_op jit(solution)/shard_map/ppermute | solution.py:62
  56.0 18.1 %collective-permute-start.9 = (bf16[256,1152]{1,0:T(8,128)(2,1)S(1)}, bf16[256,1152]{1,0:T(8,128)(2,1)S(1)}, u32[]{:S(2)}, u32[]{:S(2)}) collective-permute-start(bf16[256,1152]{1,0:T(8,128)(2,1)S(1)} %slice.26), channel_id=1, source_target_pairs={{0,1},{1,0},{2,3},{3,2},{4,5},{5,4},{6,7},{7,6},{8,9},{9,8},{10,11... | collective-permute-start | bytes 1769480 | tf_op jit(solution)/shard_map/ppermute | solution.py:72
  60.0 16.1 %collective-permute-start.7 = (bf16[128,1152]{1,0:T(8,128)(2,1)S(1)}, bf16[128,1152]{1,0:T(8,128)(2,1)S(1)}, u32[]{:S(2)}, u32[]{:S(2)}) collective-permute-start(bf16[128,1152]{1,0:T(8,128)(2,1)S(1)} %convolution_convert_fusion), channel_id=1, source_target_pairs={{0,8},{8,16},{16,24},{24,32},{32,40},{40,48},{48,56},{56,64},{64,7... | collective-permute-start | bytes 884744 | tf_op jit(solution)/shard_map/ppermute | solution.py:58
  63.8 21.6 %collective-permute-start.8 = (bf16[128,1152]{1,0:T(8,128)(2,1)S(1)}, bf16[128,1152]{1,0:T(8,128)(2,1)S(1)}, u32[]{:S(2)}, u32[]{:S(2)}) collective-permute-start(bf16[128,1152]{1,0:T(8,128)(2,1)S(1)} %add_convert_fusion), channel_id=1, source_target_pairs={{0,6},{1,7},{2,4},{3,5},{4,2},{5,3},{6,0},{7,1},{8,14},{9,15},{10,... | collective-permute-start | bytes 884744 | tf_op jit(solution)/shard_map/ppermute | solution.py:78
  74.2 12.1 %collective-permute-start.10 = (bf16[128,1152]{1,0:T(8,128)(2,1)S(1)}, bf16[128,1152]{1,0:T(8,128)(2,1)S(1)}, u32[]{:S(2)}, u32[]{:S(2)}) collective-permute-start(bf16[128,1152]{1,0:T(8,128)(2,1)S(1)} %slice.27), channel_id=1, source_target_pairs={{0,2},{1,3},{2,0},{3,1},{4,6},{5,7},{6,4},{7,5},{8,10},{9,11},{10,... | collective-permute-start | bytes 884744 | tf_op jit(solution)/shard_map/ppermute | solution.py:77

commit v3 on v2

v3 whole, which is shorter than its diff:
```python
import jax
import jax.numpy as jnp
from jax import lax
from jax.experimental import pallas as pl
from jax.experimental.pallas import tpu as pltpu
from jax.sharding import PartitionSpec as P

F32 = jnp.float32
BF16 = jnp.bfloat16
BY_COLUMN = (((0,), (0,)), ((), ()))
BY_ROW = (((1,), (1,)), ((), ()))


def inner_route(move, devices):
    route = []
    for chip in range(devices // 2):
        for core in range(2):
            to_chip, to_core = move(chip, core)
            route.append((chip * 2 + core, to_chip * 2 + to_core))
    return route


def coefficients(left, right, scale, offset, has_diagonal=False):
    scores = scale * lax.dot_general(left, right, BY_ROW, preferred_element_type=F32) + offset
    coef = scale * jax.nn.sigmoid(scores)
    if has_diagonal:
        shape = scores.shape
        same = lax.broadcasted_iota(jnp.int32, shape, 0) == lax.broadcasted_iota(jnp.int32, shape, 1)
        coef = jnp.where(same, -scale * jax.nn.sigmoid(-scores), coef)
    return coef.astype(BF16)


def last_guests_kernel(stretch, offset_term, left, t0, t1, t2, t3, coef, part):
    scale, offset = stretch[0], offset_term[0]
    rows = left.shape[0]
    total = None
    for k, text in enumerate((t0, t1, t2, t3)):
        c = coefficients(left[...], text[...], scale, offset)
        coef[:, k * rows : (k + 1) * rows] = c
        term = jnp.dot(c, text[...], preferred_element_type=F32)
        total = term if total is None else total + term
    part[...] = total.astype(BF16)


def rest_kernel(
    stretch, offset_term, images, across, guests, last, last_coef, t0, t1, t2, t3,
    own, own_across, guests_part, mine, far, for_core,
):
    scale, offset = stretch[0], offset_term[0]
    rows = images.shape[0]
    sums = [None, None, None]
    lefts = (images[...], across[...], guests[...])
    for k, text in enumerate((t0, t1, t2, t3)):
        right = text[...]
        grad = lax.dot_general(
            last_coef[:, k * rows : (k + 1) * rows], last[...], BY_COLUMN, preferred_element_type=F32
        )
        for i, left in enumerate(lefts):
            c = coefficients(left, right, scale, offset, has_diagonal=(i == 0 and k == 0))
            term = jnp.dot(c, right, preferred_element_type=F32)
            sums[i] = term if sums[i] is None else sums[i] + term
            grad = grad + lax.dot_general(c, left, BY_COLUMN, preferred_element_type=F32)
        if k == 0:
            mine[...] = grad
        elif k == 1:
            for_core[rows:, :] = grad.astype(BF16)
        elif k == 2:
            far[...] = grad
        else:
            for_core[:rows, :] = grad.astype(BF16)
    own[...] = sums[0]
    own_across[...] = sums[1]
    guests_part[...] = sums[2].astype(BF16)


def local_call(kernel, outs, flops, stretch, offset_term, *arrays):
    vmem = pl.BlockSpec(memory_space=pltpu.VMEM)
    return pl.pallas_call(
        kernel,
        out_shape=[jax.ShapeDtypeStruct(shape, dtype) for shape, dtype in outs],
        in_specs=[pl.BlockSpec(memory_space=pltpu.SMEM)] * 2 + [vmem] * len(arrays),
        out_specs=[vmem] * len(outs),
        compiler_params=pltpu.CompilerParams(vmem_limit_bytes=24 * 1024 * 1024),
        cost_estimate=pl.CostEstimate(flops=flops, bytes_accessed=0, transcendentals=0),
    )(stretch, offset_term, *arrays)


def per_device(images, texts, stretch, offset_term):
    outer, inner = lax.axis_size("outer"), lax.axis_size("inner")
    chips = inner // 2
    rows, width = images.shape

    across = inner_route(lambda z, c: (chips - 1 - z, c), inner)
    beside = inner_route(lambda z, c: (z ^ 1, c), inner)
    other_core = inner_route(lambda z, c: (z, 1 - c), inner)
    to_previous = [(i, (i - 1) % outer) for i in range(outer)]
    to_next = [(i, (i + 1) % outer) for i in range(outer)]

    images_across = lax.ppermute(images, "inner", across)
    texts_core = lax.ppermute(texts, "inner", other_core)
    texts_beside = lax.ppermute(texts, "inner", beside)
    guests = lax.ppermute(images, "outer", to_previous)
    guests_across = lax.ppermute(images_across, "outer", to_previous)
    texts_beside_core = lax.ppermute(texts_beside, "inner", other_core)
    all_texts = (texts, texts_core, texts_beside, texts_beside_core)

    block = rows * width * 4 * rows * 2
    last_coef, last_part = local_call(
        last_guests_kernel,
        [((rows, 4 * rows), BF16), ((rows, width), BF16)],
        2 * block,
        stretch, offset_term, guests_across, *all_texts,
    )
    back_across = lax.ppermute(last_part, "outer", to_next)
    own, own_across, guests_part, mine, far, for_core = local_call(
        rest_kernel,
        [
            ((rows, width), F32), ((rows, width), F32), ((rows, width), BF16),
            ((rows, width), F32), ((rows, width), F32), ((2 * rows, width), BF16),
        ],
        10 * block,
        stretch, offset_term, images, images_across, guests, guests_across, last_coef, *all_texts,
    )
    from_core = lax.ppermute(for_core, "inner", other_core)
    back = lax.ppermute(guests_part, "outer", to_next)
    own, own_across, back_across = lax.optimization_barrier((own, own_across, back_across))
    mine = mine + from_core[rows:].astype(F32)
    sent = (far + from_core[:rows].astype(F32)).astype(BF16)
    from_beside = lax.ppermute(sent, "inner", beside)
    from_across = lax.ppermute(
        (own_across + back_across.astype(F32)).astype(BF16), "inner", across
    )
    grad_text = mine + from_beside.astype(F32)
    grad_image = own + back.astype(F32) + from_across.astype(F32)
    return grad_image, grad_text


def solution(mesh):
    block = P(("outer", "inner"), None)
    return jax.shard_map(
        per_device,
        mesh=mesh,
        in_specs=(block, block, P(), P()),
        out_specs=(block, block),
        check_vma=False,
    )
```

time: 87.6 us -> 86.8 us (level)
  starting transfers between devices: 60.2 us -> 53.4 us
  Pallas kernels: 0 us -> 6.72 us
  matrix products: 5.29 us -> 0 us
  waiting for transfers between devices: 16.3 us -> 20.8 us
    ppermute x1, waiting for transfers between devices: 0.01 us -> 8.01 us  [per_device(): back = lax.ppermute(guests_part, 'outer', to_next)]
    ppermute x1, starting transfers between devices: 10 us -> 3.06 us  [per_device(): guests = lax.ppermute(images, 'outer', to_previous)]
    pallas_call x0 -> x2, Pallas kernels: none -> 6.72 us  [local_call(): pl.pallas_call(kernel, out_shape=[jax.ShapeDtypeStruct(shape, dtype) for...]
    ppermute x1, starting transfers between devices: 8.46 us -> 1.92 us  [per_device(): texts_beside = lax.ppermute(texts, 'inner', beside)]
    ppermute x1, starting transfers between devices: 10.4 us -> 16.9 us  [per_device(): images_across = lax.ppermute(images, 'inner', across)]
    ppermute x1, starting transfers between devices: 6.55 us -> 12.7 us  [per_device(): guests_across = lax.ppermute(images_across, 'outer', to_previous)]
    ppermute x1, starting transfers between devices: 10.2 us -> 4.46 us  [per_device(): lax.ppermute((own_across + back_across.astype(F32)).astype(BF16), 'inner'...]
    ppermute x1, waiting for transfers between devices: 0.01 us -> 5.64 us  [per_device(): images_across = lax.ppermute(images, 'inner', across)]
  transfers between devices with their start and end apart: 11 -> 11, of which waited for: 3 -> 4; matrix products, arithmetic and copies ran while one was open for 9% -> 1% of each run, Pallas kernels for 0% -> 8%
where the time goes in v3:
time: 86.8 us; the launch traced here: 86 us
  starting transfers between devices  53.4 us (62%)
  waiting for transfers between devices  20.8 us (24%)
  Pallas kernels  6.72 us (8%)
  between operations  2.1 us (2%)
  other arithmetic  1.9 us (2%)
  local copies, waits for them, and re-layouts  0.96 us (1%)
    ppermute x1, starting transfers between devices, per_device(): images_across = lax.ppermute(images, 'inner', across)  16.9 us
    ppermute x1, starting transfers between devices, per_device(): guests_across = lax.ppermute(images_across, 'outer', to_previous)  12.7 us
    ppermute x1, waiting for transfers between devices, per_device(): back = lax.ppermute(guests_part, 'outer', to_next)  8.01 us
    pallas_call x2, Pallas kernels, local_call(): pl.pallas_call(kernel, out_shape=[jax.ShapeDtypeStruct(shape, dtype) for...  6.72 us
    ppermute x1, waiting for transfers between devices, per_device(): images_across = lax.ppermute(images, 'inner', across)  5.64 us
    ppermute x1, waiting for transfers between devices, per_device(): lax.ppermute((own_across + back_across.astype(F32)).astype(BF16), 'inner'...  5.34 us
    ppermute x1, starting transfers between devices, per_device(): lax.ppermute((own_across + back_across.astype(F32)).astype(BF16), 'inner'...  4.46 us
    ppermute x1, starting transfers between devices, per_device(): guests = lax.ppermute(images, 'outer', to_previous)  3.06 us
  transfers between devices with their start and end apart: 11, of which 4 were waited for; matrix products, arithmetic and copies ran while one was open for 1% of the time, Pallas kernels for 8%

profile of v3, /device:TPU:1, one launch (start us, length us, event | category | flops | bytes accessed | tf_op | source)
XLA Modules:
  0.0 86.0 jit_solution(10439358093946059058)
XLA Ops:
  0.6 16.9 %collective-permute-start = (bf16[128,1152]{1,0:T(8,128)(2,1)}, bf16[128,1152]{1,0:T(8,128)(2,1)S(1)}, u32[]{:S(2)}, u32[]{:S(2)}) collective-permute-start(bf16[128,1152]{1,0:T(8,128)(2,1)} %images.1), channel_id=1, source_target_pairs={{0,6},{1,7},{2,4},{3,5},{4,2},{5,3},{6,0},{7,1},{8,14},{9,15},{10,... | collective-permute-start | bytes 884744 | tf_op jit(solution)/shard_map/ppermute | solution.py:99
  17.6 1.9 %collective-permute-start.4 = (bf16[128,1152]{1,0:T(8,128)(2,1)}, bf16[128,1152]{1,0:T(8,128)(2,1)S(1)}, u32[]{:S(2)}, u32[]{:S(2)}) collective-permute-start(bf16[128,1152]{1,0:T(8,128)(2,1)} %t0.3), channel_id=1, source_target_pairs={{0,2},{1,3},{2,0},{3,1},{4,6},{5,7},{6,4},{7,5},{8,10},{9,11},{10,... | collective-permute-start | bytes 884744 | tf_op jit(solution)/shard_map/ppermute | solution.py:101
  19.5 2.9 %collective-permute-start.3 = (bf16[128,1152]{1,0:T(8,128)(2,1)}, bf16[128,1152]{1,0:T(8,128)(2,1)S(1)}, u32[]{:S(2)}, u32[]{:S(2)}) collective-permute-start(bf16[128,1152]{1,0:T(8,128)(2,1)} %t0.3), channel_id=1, source_target_pairs={{0,1},{1,0},{2,3},{3,2},{4,5},{5,4},{6,7},{7,6},{8,9},{9,8},{10,11... | collective-permute-start | bytes 884744 | tf_op jit(solution)/shard_map/ppermute | solution.py:100
  22.4 5.6 %collective-permute-done.across = bf16[128,1152]{1,0:T(8,128)(2,1)S(1)} collective-permute-done((bf16[128,1152]{1,0:T(8,128)(2,1)}, bf16[128,1152]{1,0:T(8,128)(2,1)S(1)}, u32[]{:S(2)}, u32[]{:S(2)}) %collective-permute-start) | collective-permute-done | bytes 294944 | tf_op jit(solution)/shard_map/ppermute | solution.py:99
  28.0 12.7 %collective-permute-start.2 = (bf16[128,1152]{1,0:T(8,128)(2,1)S(1)}, bf16[128,1152]{1,0:T(8,128)(2,1)S(1)}, u32[]{:S(2)}, u32[]{:S(2)}) collective-permute-start(bf16[128,1152]{1,0:T(8,128)(2,1)S(1)} %collective-permute-done.across), channel_id=1, source_target_pairs={{0,1016},{8,0},{16,8},{24,16},{32,24},{40,32},{48,40},{56,48},{64,... | collective-permute-start | bytes 884744 | tf_op jit(solution)/shard_map/ppermute | solution.py:103
  40.7 0.0 collective-permute-done.4.t2
  40.7 2.7 %collective-permute-start.5 = (bf16[128,1152]{1,0:T(8,128)(2,1)S(1)}, bf16[128,1152]{1,0:T(8,128)(2,1)S(1)}, u32[]{:S(2)}, u32[]{:S(2)}) collective-permute-start(bf16[128,1152]{1,0:T(8,128)(2,1)S(1)} %collective-permute-done.4.t2), channel_id=1, source_target_pairs={{0,1},{1,0},{2,3},{3,2},{4,5},{5,4},{6,7},{7,6},{8,9},{9,8},{10,11... | collective-permute-start | bytes 884744 | tf_op jit(solution)/shard_map/ppermute | solution.py:104
  43.5 3.1 %collective-permute-start.1 = (bf16[128,1152]{1,0:T(8,128)(2,1)}, bf16[128,1152]{1,0:T(8,128)(2,1)S(1)}, u32[]{:S(2)}, u32[]{:S(2)}) collective-permute-start(bf16[128,1152]{1,0:T(8,128)(2,1)} %images.1), channel_id=1, source_target_pairs={{0,1016},{8,0},{16,8},{24,16},{32,24},{40,32},{48,40},{56,48},{64,... | collective-permute-start | bytes 884744 | tf_op jit(solution)/shard_map/ppermute | solution.py:102
  47.8 0.0 collective-permute-done.3.t1
  47.8 0.0 collective-permute-done.2.left.last
  47.8 0.0 collective-permute-done.5.t3
  47.9 0.0 copy-start
  47.9 1.0 %copy-done = bf16[128,1152]{1,0:T(8,128)(2,1)S(1)} copy-done((bf16[128,1152]{1,0:T(8,128)(2,1)S(1)}, bf16[128,1152]{1,0:T(8,128)(2,1)}, u32[]{:S(2)}) %copy-start) | copy-done | bytes 294936
  48.8 0.0 copy-start.1
  48.8 1.3 %shard_map.59 = (bf16[128,512]{1,0:T(8,128)(2,1)S(1)}, bf16[128,1152]{1,0:T(8,128)(2,1)S(1)}) custom-call(f32[1]{0:T(128)S(6)} %copy.6.stretch, f32[1]{0:T(128)S(6)} %copy.7.offset_term, bf16[128,1152]{1,0:T(8,128)(2,1)S(1)} %collective-permute-done.2.left.last, bf16[128,1152]{1,0:T(8,128)(2,1)S(1)} %copy-done, ...), custom_call_target="tpu_custom_call" | custom-call | flops 301989888 | tf_op jit(solution)/shard_map/pallas_call | solution.py:78
  50.1 2.2 %collective-permute-start.6 = (bf16[128,1152]{1,0:T(8,128)(2,1)S(1)}, bf16[128,1152]{1,0:T(8,128)(2,1)S(1)}, u32[]{:S(2)}, u32[]{:S(2)}) collective-permute-start(bf16[128,1152]{1,0:T(8,128)(2,1)S(1)} %get-tuple-element.16), channel_id=1, source_target_pairs={{0,8},{8,16},{16,24},{24,32},{32,40},{40,48},{48,56},{56,64},{64,7... | collective-permute-start | bytes 884744 | tf_op jit(solution)/shard_map/ppermute | solution.py:114
  52.4 1.8 %collective-permute-done.1.guests = bf16[128,1152]{1,0:T(8,128)(2,1)S(1)} collective-permute-done((bf16[128,1152]{1,0:T(8,128)(2,1)}, bf16[128,1152]{1,0:T(8,128)(2,1)S(1)}, u32[]{:S(2)}, u32[]{:S(2)}) %collective-permute-start.1) | collective-permute-done | bytes 294944 | tf_op jit(solution)/shard_map/ppermute | solution.py:102
  54.2 0.0 copy-done.1
  54.2 5.4 %shard_map.60 = (f32[128,1152]{1,0:T(8,128)S(1)}, f32[128,1152]{1,0:T(8,128)S(1)}, bf16[128,1152]{1,0:T(8,128)(2,1)S(1)}, f32[128,1152]{1,0:T(8,128)S(1)}, f32[1...) custom-call(f32[1]{0:T(128)S(6)} %copy.6.stretch, f32[1]{0:T(128)S(6)} %copy.7.offset_term, ...), custom_call_target="tpu_custom_call" | custom-call | flops 1509949440 | tf_op jit(solution)/shard_map/pallas_call | solution.py:78
  59.6 2.7 %collective-permute-start.9 = (bf16[256,1152]{1,0:T(8,128)(2,1)S(1)}, bf16[256,1152]{1,0:T(8,128)(2,1)S(1)}, u32[]{:S(2)}, u32[]{:S(2)}) collective-permute-start(bf16[256,1152]{1,0:T(8,128)(2,1)S(1)} %get-tuple-element.22), channel_id=1, source_target_pairs={{0,1},{1,0},{2,3},{3,2},{4,5},{5,4},{6,7},{7,6},{8,9},{9,8},{10,11... | collective-permute-start | bytes 1769480 | tf_op jit(solution)/shard_map/ppermute | solution.py:124
  62.3 1.9 %collective-permute-start.7 = (bf16[128,1152]{1,0:T(8,128)(2,1)S(1)}, bf16[128,1152]{1,0:T(8,128)(2,1)S(1)}, u32[]{:S(2)}, u32[]{:S(2)}) collective-permute-start(bf16[128,1152]{1,0:T(8,128)(2,1)S(1)} %get-tuple-element.18), channel_id=1, source_target_pairs={{0,8},{8,16},{16,24},{24,32},{32,40},{40,48},{48,56},{56,64},{64,7... | collective-permute-start | bytes 884744 | tf_op jit(solution)/shard_map/ppermute | solution.py:125
  64.3 0.0 collective-permute-done.6
  64.3 0.1 add_convert_fusion.1
  64.3 4.5 %collective-permute-start.8 = (bf16[128,1152]{1,0:T(8,128)(2,1)S(1)}, bf16[128,1152]{1,0:T(8,128)(2,1)S(1)}, u32[]{:S(2)}, u32[]{:S(2)}) collective-permute-start(bf16[128,1152]{1,0:T(8,128)(2,1)S(1)} %add_convert_fusion.1), channel_id=1, source_target_pairs={{0,6},{1,7},{2,4},{3,5},{4,2},{5,3},{6,0},{7,1},{8,14},{9,15},{10,... | collective-permute-start | bytes 884744 | tf_op jit(solution)/shard_map/ppermute | solution.py:130
  68.8 0.0 collective-permute-done.9
  68.8 0.1 add_convert_fusion
  68.9 1.9 %collective-permute-start.10 = (bf16[128,1152]{1,0:T(8,128)(2,1)S(1)}, bf16[128,1152]{1,0:T(8,128)(2,1)S(1)}, u32[]{:S(2)}, u32[]{:S(2)}) collective-permute-start(bf16[128,1152]{1,0:T(8,128)(2,1)S(1)} %add_convert_fusion), channel_id=1, source_target_pairs={{0,2},{1,3},{2,0},{3,1},{4,6},{5,7},{6,4},{7,5},{8,10},{9,11},{10,... | collective-permute-start | bytes 884744 | tf_op jit(solution)/shard_map/ppermute | solution.py:129
  70.8 8.0 %collective-permute-done.7 = bf16[128,1152]{1,0:T(8,128)(2,1)S(1)} collective-permute-done((bf16[128,1152]{1,0:T(8,128)(2,1)S(1)}, bf16[128,1152]{1,0:T(8,128)(2,1)S(1)}, u32[]{:S(2)}, u32[]{:S(2)}) %collective-permute-start.7) | collective-permute-done | bytes 294944 | tf_op jit(solution)/shard_map/ppermute | solution.py:125
  78.8 5.3 %collective-permute-done.8 = bf16[128,1152]{1,0:T(8,128)(2,1)S(1)} collective-permute-done((bf16[128,1152]{1,0:T(8,128)(2,1)S(1)}, bf16[128,1152]{1,0:T(8,128)(2,1)S(1)}, u32[]{:S(2)}, u32[]{:S(2)}) %collective-permute-start.8) | collective-permute-done | bytes 294944 | tf_op jit(solution)/shard_map/ppermute | solution.py:130
  84.2 0.9 %convert_add_fusion.1 = f32[128,1152]{1,0:T(8,128)} fusion(bf16[128,1152]{1,0:T(8,128)(2,1)S(1)} %collective-permute-done.8, f32[128,1152]{1,0:T(8,128)S(1)} %get-tuple-element.17, bf16[128,1152]{1,0:T(8,128)(2,1)S(1)} %collective-permute-done.7), kind=kLoop, calls=%fused_computation.2 | loop fusion | flops 589824 | bytes 1769472 | tf_op jit(solution)/shard_map/add | solution.py:134
  85.1 0.0 collective-permute-done.10
  85.1 0.9 %convert_add_fusion = f32[128,1152]{1,0:T(8,128)} fusion(bf16[128,1152]{1,0:T(8,128)(2,1)S(1)} %collective-permute-done.10, f32[128,1152]{1,0:T(8,128)S(1)} %get-tuple-element.21, bf16[256,1152]{1,0:T(8,128)(2,1)S(1)} %collective-permute-done.9), kind=kLoop, calls=%fused_computation | loop fusion | flops 589824 | bytes 1769472 | tf_op jit(solution)/shard_map/add | solution.py:133
Async XLA Ops:
  0.6 27.4 %collective-permute-start = (bf16[128,1152]{1,0:T(8,128)(2,1)}, bf16[128,1152]{1,0:T(8,128)(2,1)S(1)}, u32[]{:S(2)}, u32[]{:S(2)}) collective-permute-start(bf16[128,1152]{1,0:T(8,128)(2,1)} %images.1), channel_id=1, source_target_pairs={{0,6},{1,7},{2,4},{3,5},{4,2},{5,3},{6,0},{7,1},{8,14},{9,15},{10,... | collective-permute-start | bytes 884744 | tf_op jit(solution)/shard_map/ppermute | solution.py:99
  17.6 23.1 %collective-permute-start.4 = (bf16[128,1152]{1,0:T(8,128)(2,1)}, bf16[128,1152]{1,0:T(8,128)(2,1)S(1)}, u32[]{:S(2)}, u32[]{:S(2)}) collective-permute-start(bf16[128,1152]{1,0:T(8,128)(2,1)} %t0.3), channel_id=1, source_target_pairs={{0,2},{1,3},{2,0},{3,1},{4,6},{5,7},{6,4},{7,5},{8,10},{9,11},{10,... | collective-permute-start | bytes 884744 | tf_op jit(solution)/shard_map/ppermute | solution.py:101
  19.5 28.3 %collective-permute-start.3 = (bf16[128,1152]{1,0:T(8,128)(2,1)}, bf16[128,1152]{1,0:T(8,128)(2,1)S(1)}, u32[]{:S(2)}, u32[]{:S(2)}) collective-permute-start(bf16[128,1152]{1,0:T(8,128)(2,1)} %t0.3), channel_id=1, source_target_pairs={{0,1},{1,0},{2,3},{3,2},{4,5},{5,4},{6,7},{7,6},{8,9},{9,8},{10,11... | collective-permute-start | bytes 884744 | tf_op jit(solution)/shard_map/ppermute | solution.py:100
  28.0 19.8 %collective-permute-start.2 = (bf16[128,1152]{1,0:T(8,128)(2,1)S(1)}, bf16[128,1152]{1,0:T(8,128)(2,1)S(1)}, u32[]{:S(2)}, u32[]{:S(2)}) collective-permute-start(bf16[128,1152]{1,0:T(8,128)(2,1)S(1)} %collective-permute-done.across), channel_id=1, source_target_pairs={{0,1016},{8,0},{16,8},{24,16},{32,24},{40,32},{48,40},{56,48},{64,... | collective-permute-start | bytes 884744 | tf_op jit(solution)/shard_map/ppermute | solution.py:103
  40.7 7.1 %collective-permute-start.5 = (bf16[128,1152]{1,0:T(8,128)(2,1)S(1)}, bf16[128,1152]{1,0:T(8,128)(2,1)S(1)}, u32[]{:S(2)}, u32[]{:S(2)}) collective-permute-start(bf16[128,1152]{1,0:T(8,128)(2,1)S(1)} %collective-permute-done.4.t2), channel_id=1, source_target_pairs={{0,1},{1,0},{2,3},{3,2},{4,5},{5,4},{6,7},{7,6},{8,9},{9,8},{10,11... | collective-permute-start | bytes 884744 | tf_op jit(solution)/shard_map/ppermute | solution.py:104
  43.5 10.7 %collective-permute-start.1 = (bf16[128,1152]{1,0:T(8,128)(2,1)}, bf16[128,1152]{1,0:T(8,128)(2,1)S(1)}, u32[]{:S(2)}, u32[]{:S(2)}) collective-permute-start(bf16[128,1152]{1,0:T(8,128)(2,1)} %images.1), channel_id=1, source_target_pairs={{0,1016},{8,0},{16,8},{24,16},{32,24},{40,32},{48,40},{56,48},{64,... | collective-permute-start | bytes 884744 | tf_op jit(solution)/shard_map/ppermute | solution.py:102
  47.9 1.0 %copy-start = (bf16[128,1152]{1,0:T(8,128)(2,1)S(1)}, bf16[128,1152]{1,0:T(8,128)(2,1)}, u32[]{:S(2)}) copy-start(bf16[128,1152]{1,0:T(8,128)(2,1)} %t0.3) | copy-start | bytes 884740
  48.8 5.4 %copy-start.1 = (bf16[128,1152]{1,0:T(8,128)(2,1)S(1)}, bf16[128,1152]{1,0:T(8,128)(2,1)}, u32[]{:S(2)}) copy-start(bf16[128,1152]{1,0:T(8,128)(2,1)} %images.1) | copy-start | bytes 884740
  50.1 14.1 %collective-permute-start.6 = (bf16[128,1152]{1,0:T(8,128)(2,1)S(1)}, bf16[128,1152]{1,0:T(8,128)(2,1)S(1)}, u32[]{:S(2)}, u32[]{:S(2)}) collective-permute-start(bf16[128,1152]{1,0:T(8,128)(2,1)S(1)} %get-tuple-element.16), channel_id=1, source_target_pairs={{0,8},{8,16},{16,24},{24,32},{32,40},{40,48},{48,56},{56,64},{64,7... | collective-permute-start | bytes 884744 | tf_op jit(solution)/shard_map/ppermute | solution.py:114
  59.6 9.2 %collective-permute-start.9 = (bf16[256,1152]{1,0:T(8,128)(2,1)S(1)}, bf16[256,1152]{1,0:T(8,128)(2,1)S(1)}, u32[]{:S(2)}, u32[]{:S(2)}) collective-permute-start(bf16[256,1152]{1,0:T(8,128)(2,1)S(1)} %get-tuple-element.22), channel_id=1, source_target_pairs={{0,1},{1,0},{2,3},{3,2},{4,5},{5,4},{6,7},{7,6},{8,9},{9,8},{10,11... | collective-permute-start | bytes 1769480 | tf_op jit(solution)/shard_map/ppermute | solution.py:124
  62.3 16.5 %collective-permute-start.7 = (bf16[128,1152]{1,0:T(8,128)(2,1)S(1)}, bf16[128,1152]{1,0:T(8,128)(2,1)S(1)}, u32[]{:S(2)}, u32[]{:S(2)}) collective-permute-start(bf16[128,1152]{1,0:T(8,128)(2,1)S(1)} %get-tuple-element.18), channel_id=1, source_target_pairs={{0,8},{8,16},{16,24},{24,32},{32,40},{40,48},{48,56},{56,64},{64,7... | collective-permute-start | bytes 884744 | tf_op jit(solution)/shard_map/ppermute | solution.py:125
  64.3 19.8 %collective-permute-start.8 = (bf16[128,1152]{1,0:T(8,128)(2,1)S(1)}, bf16[128,1152]{1,0:T(8,128)(2,1)S(1)}, u32[]{:S(2)}, u32[]{:S(2)}) collective-permute-start(bf16[128,1152]{1,0:T(8,128)(2,1)S(1)} %add_convert_fusion.1), channel_id=1, source_target_pairs={{0,6},{1,7},{2,4},{3,5},{4,2},{5,3},{6,0},{7,1},{8,14},{9,15},{10,... | collective-permute-start | bytes 884744 | tf_op jit(solution)/shard_map/ppermute | solution.py:130
  68.9 16.2 %collective-permute-start.10 = (bf16[128,1152]{1,0:T(8,128)(2,1)S(1)}, bf16[128,1152]{1,0:T(8,128)(2,1)S(1)}, u32[]{:S(2)}, u32[]{:S(2)}) collective-permute-start(bf16[128,1152]{1,0:T(8,128)(2,1)S(1)} %add_convert_fusion), channel_id=1, source_target_pairs={{0,2},{1,3},{2,0},{3,1},{4,6},{5,7},{6,4},{7,5},{8,10},{9,11},{10,... | collective-permute-start | bytes 884744 | tf_op jit(solution)/shard_map/ppermute | solution.py:129

commit v4 on v3

v4 whole, which is shorter than its diff:
```python
import jax
import jax.numpy as jnp
from jax import lax
from jax.experimental import pallas as pl
from jax.experimental.pallas import tpu as pltpu
from jax.sharding import PartitionSpec as P

F32 = jnp.float32
BF16 = jnp.bfloat16
BY_COLUMN = (((0,), (0,)), ((), ()))
BY_ROW = (((1,), (1,)), ((), ()))


def inner_route(move, devices):
    route = []
    for chip in range(devices // 2):
        for core in range(2):
            to_chip, to_core = move(chip, core)
            route.append((chip * 2 + core, to_chip * 2 + to_core))
    return route


def stack(*refs):
    return jnp.concatenate([ref[...] for ref in refs], axis=0)


def scores_of(left, right, stretch, offset_term):
    product = lax.dot_general(left, right, BY_ROW, preferred_element_type=F32)
    return stretch[0] * product + offset_term[0]


def guests_kernel(stretch, offset_term, left, t0, t1, t2, t3, coef, part):
    texts = stack(t0, t1, t2, t3)
    scores = scores_of(left[...], texts, stretch, offset_term)
    c = (stretch[0] * jax.nn.sigmoid(scores)).astype(BF16)
    coef[...] = c
    part[...] = jnp.dot(c, texts, preferred_element_type=F32).astype(BF16)


def rest_kernel(
    stretch, offset_term, images, across, guests, last, guests_coef, last_coef, t0, t1, t2, t3,
    own, own_across, mine, far, for_core,
):
    rows = images.shape[0]
    texts = stack(t0, t1, t2, t3)
    scores = scores_of(stack(images, across), texts, stretch, offset_term)
    row = lax.broadcasted_iota(jnp.int32, scores.shape, 0)
    column = lax.broadcasted_iota(jnp.int32, scores.shape, 1)
    same = (row == column) & (row < rows)
    coef = jnp.where(
        same,
        (-stretch[0] * jax.nn.sigmoid(-scores)).astype(BF16),
        (stretch[0] * jax.nn.sigmoid(scores)).astype(BF16),
    )
    image_grads = jnp.dot(coef, texts, preferred_element_type=F32)
    own[...] = image_grads[:rows]
    own_across[...] = image_grads[rows:]
    text_grads = lax.dot_general(
        jnp.concatenate([coef, guests_coef[...], last_coef[...]], axis=0),
        stack(images, across, guests, last),
        BY_COLUMN,
        preferred_element_type=F32,
    )
    mine[...] = text_grads[:rows]
    far[...] = text_grads[2 * rows : 3 * rows]
    for_core[rows:, :] = text_grads[rows : 2 * rows].astype(BF16)
    for_core[:rows, :] = text_grads[3 * rows :].astype(BF16)


def local_call(kernel, outs, flops, stretch, offset_term, *arrays):
    vmem = pl.BlockSpec(memory_space=pltpu.VMEM)
    return pl.pallas_call(
        kernel,
        out_shape=[jax.ShapeDtypeStruct(shape, dtype) for shape, dtype in outs],
        in_specs=[pl.BlockSpec(memory_space=pltpu.SMEM)] * 2 + [vmem] * len(arrays),
        out_specs=[vmem] * len(outs),
        compiler_params=pltpu.CompilerParams(vmem_limit_bytes=24 * 1024 * 1024),
        cost_estimate=pl.CostEstimate(flops=flops, bytes_accessed=0, transcendentals=0),
    )(stretch, offset_term, *arrays)


def per_device(images, texts, stretch, offset_term):
    outer, inner = lax.axis_size("outer"), lax.axis_size("inner")
    chips = inner // 2
    rows, width = images.shape

    across = inner_route(lambda z, c: (chips - 1 - z, c), inner)
    beside = inner_route(lambda z, c: (z ^ 1, c), inner)
    other_core = inner_route(lambda z, c: (z, 1 - c), inner)
    to_previous = [(i, (i - 1) % outer) for i in range(outer)]
    to_next = [(i, (i + 1) % outer) for i in range(outer)]

    images_across = lax.ppermute(images, "inner", across)
    texts_core = lax.ppermute(texts, "inner", other_core)
    texts_out = texts
    texts_beside = lax.ppermute(texts_out, "inner", beside)
    guests = lax.ppermute(images, "outer", to_previous)
    guests_across = lax.ppermute(images_across, "outer", to_previous)
    texts_beside_core = lax.ppermute(texts_beside, "inner", other_core)
    all_texts = (texts, texts_core, texts_beside, texts_beside_core)

    block = rows * width * 4 * rows * 2
    guests_outs = [((rows, 4 * rows), BF16), ((rows, width), BF16)]
    guests_coef, guests_part = local_call(
        guests_kernel, guests_outs, 2 * block, stretch, offset_term, guests, *all_texts
    )
    back = lax.ppermute(guests_part, "outer", to_next)
    last_coef, last_part = local_call(
        guests_kernel, guests_outs, 2 * block, stretch, offset_term, guests_across, *all_texts
    )
    back_across = lax.ppermute(last_part, "outer", to_next)
    own, own_across, mine, far, for_core = local_call(
        rest_kernel,
        [((rows, width), F32)] * 4 + [((2 * rows, width), BF16)],
        8 * block,
        stretch, offset_term, images, images_across, guests, guests_across,
        guests_coef, last_coef, *all_texts,
    )
    from_core = lax.ppermute(for_core, "inner", other_core)
    own = own + back.astype(F32)
    own_across, back_across = lax.optimization_barrier((own_across, back_across))
    mine = mine + from_core[rows:].astype(F32)
    sent = (far + from_core[:rows].astype(F32)).astype(BF16)
    own, sent = lax.optimization_barrier((own, sent))
    from_beside = lax.ppermute(sent, "inner", beside)
    from_across = lax.ppermute(
        (own_across + back_across.astype(F32)).astype(BF16), "inner", across
    )
    grad_text = mine + from_beside.astype(F32)
    grad_image = own + from_across.astype(F32)
    return grad_image, grad_text


def solution(mesh):
    block = P(("outer", "inner"), None)
    return jax.shard_map(
        per_device,
        mesh=mesh,
        in_specs=(block, block, P(), P()),
        out_specs=(block, block),
        check_vma=False,
    )
```

time: 86.8 us -> 86.9 us (level)
  waiting for transfers between devices: 20.8 us -> 24.2 us
  Pallas kernels: 6.72 us -> 3.4 us
    ppermute x1, waiting for transfers between devices: 8.01 us -> 1.93 us  [per_device(): back = lax.ppermute(guests_part, 'outer', to_next)]
    ppermute x1, waiting for transfers between devices: 0.01 us -> 4.63 us  [per_device(): from_beside = lax.ppermute(sent, 'inner', beside)]
    pallas_call x2 -> x3, Pallas kernels: 6.72 us -> 3.4 us  [local_call(): pl.pallas_call(kernel, out_shape=[jax.ShapeDtypeStruct(shape, dtype) for...]
    ppermute x1, waiting for transfers between devices: 0.01 us -> 2.24 us  [per_device(): back_across = lax.ppermute(last_part, 'outer', to_next)]
    ppermute x1, waiting for transfers between devices: 5.34 us -> 7.53 us  [per_device(): lax.ppermute((own_across + back_across.astype(F32)).astype(BF16), 'inner'...]
  transfers between devices with their start and end apart: 11 -> 11, of which waited for: 4 -> 6; matrix products, arithmetic and copies ran while one was open for 1% -> 1% of each run, Pallas kernels for 8% -> 4%
where the time goes in v4:
time: 86.9 us; the launch traced here: 86.4 us
  starting transfers between devices  53.8 us (62%)
  waiting for transfers between devices  24.2 us (28%)
  Pallas kernels  3.4 us (4%)
  between operations  2.11 us (2%)
  other arithmetic  1.92 us (2%)
  local copies, waits for them, and re-layouts  0.96 us (1%)
    ppermute x1, starting transfers between devices, per_device(): images_across = lax.ppermute(images, 'inner', across)  16.9 us
    ppermute x1, starting transfers between devices, per_device(): guests_across = lax.ppermute(images_across, 'outer', to_previous)  12.7 us
    ppermute x1, waiting for transfers between devices, per_device(): lax.ppermute((own_across + back_across.astype(F32)).astype(BF16), 'inner'...  7.53 us
    ppermute x1, waiting for transfers between devices, per_device(): images_across = lax.ppermute(images, 'inner', across)  5.64 us
    ppermute x1, starting transfers between devices, per_device(): lax.ppermute((own_across + back_across.astype(F32)).astype(BF16), 'inner'...  4.72 us
    ppermute x1, waiting for transfers between devices, per_device(): from_beside = lax.ppermute(sent, 'inner', beside)  4.63 us
    pallas_call x3, Pallas kernels, local_call(): pl.pallas_call(kernel, out_shape=[jax.ShapeDtypeStruct(shape, dtype) for...  3.4 us
    ppermute x1, starting transfers between devices, per_device(): guests = lax.ppermute(images, 'outer', to_previous)  3.06 us
  transfers between devices with their start and end apart: 11, of which 6 were waited for; matrix products, arithmetic and copies ran while one was open for 1% of the time, Pallas kernels for 4%

profile of v4, /device:TPU:1, one launch (start us, length us, event | category | flops | bytes accessed | tf_op | source)
XLA Modules:
  0.0 86.4 jit_solution(7180496689827097074)
XLA Ops:
  0.6 16.9 %collective-permute-start = (bf16[128,1152]{1,0:T(8,128)(2,1)}, bf16[128,1152]{1,0:T(8,128)(2,1)S(1)}, u32[]{:S(2)}, u32[]{:S(2)}) collective-permute-start(bf16[128,1152]{1,0:T(8,128)(2,1)} %images.1), channel_id=1, source_target_pairs={{0,6},{1,7},{2,4},{3,5},{4,2},{5,3},{6,0},{7,1},{8,14},{9,15},{10,... | collective-permute-start | bytes 884744 | tf_op jit(solution)/shard_map/ppermute | solution.py:93
  17.6 1.9 %collective-permute-start.4 = (bf16[128,1152]{1,0:T(8,128)(2,1)}, bf16[128,1152]{1,0:T(8,128)(2,1)S(1)}, u32[]{:S(2)}, u32[]{:S(2)}) collective-permute-start(bf16[128,1152]{1,0:T(8,128)(2,1)} %t0.5), channel_id=1, source_target_pairs={{0,2},{1,3},{2,0},{3,1},{4,6},{5,7},{6,4},{7,5},{8,10},{9,11},{10,... | collective-permute-start | bytes 884744 | tf_op jit(solution)/shard_map/ppermute | solution.py:96
  19.5 2.9 %collective-permute-start.3 = (bf16[128,1152]{1,0:T(8,128)(2,1)}, bf16[128,1152]{1,0:T(8,128)(2,1)S(1)}, u32[]{:S(2)}, u32[]{:S(2)}) collective-permute-start(bf16[128,1152]{1,0:T(8,128)(2,1)} %t0.5), channel_id=1, source_target_pairs={{0,1},{1,0},{2,3},{3,2},{4,5},{5,4},{6,7},{7,6},{8,9},{9,8},{10,11... | collective-permute-start | bytes 884744 | tf_op jit(solution)/shard_map/ppermute | solution.py:94
  22.4 5.6 %collective-permute-done.across = bf16[128,1152]{1,0:T(8,128)(2,1)S(1)} collective-permute-done((bf16[128,1152]{1,0:T(8,128)(2,1)}, bf16[128,1152]{1,0:T(8,128)(2,1)S(1)}, u32[]{:S(2)}, u32[]{:S(2)}) %collective-permute-start) | collective-permute-done | bytes 294944 | tf_op jit(solution)/shard_map/ppermute | solution.py:93
  28.0 12.7 %collective-permute-start.2 = (bf16[128,1152]{1,0:T(8,128)(2,1)S(1)}, bf16[128,1152]{1,0:T(8,128)(2,1)S(1)}, u32[]{:S(2)}, u32[]{:S(2)}) collective-permute-start(bf16[128,1152]{1,0:T(8,128)(2,1)S(1)} %collective-permute-done.across), channel_id=1, source_target_pairs={{0,1016},{8,0},{16,8},{24,16},{32,24},{40,32},{48,40},{56,48},{64,... | collective-permute-start | bytes 884744 | tf_op jit(solution)/shard_map/ppermute | solution.py:98
  40.7 0.0 collective-permute-done.4.t2
  40.7 2.7 %collective-permute-start.5 = (bf16[128,1152]{1,0:T(8,128)(2,1)S(1)}, bf16[128,1152]{1,0:T(8,128)(2,1)S(1)}, u32[]{:S(2)}, u32[]{:S(2)}) collective-permute-start(bf16[128,1152]{1,0:T(8,128)(2,1)S(1)} %collective-permute-done.4.t2), channel_id=1, source_target_pairs={{0,1},{1,0},{2,3},{3,2},{4,5},{5,4},{6,7},{7,6},{8,9},{9,8},{10,11... | collective-permute-start | bytes 884744 | tf_op jit(solution)/shard_map/ppermute | solution.py:99
  43.5 3.1 %collective-permute-start.1 = (bf16[128,1152]{1,0:T(8,128)(2,1)}, bf16[128,1152]{1,0:T(8,128)(2,1)S(1)}, u32[]{:S(2)}, u32[]{:S(2)}) collective-permute-start(bf16[128,1152]{1,0:T(8,128)(2,1)} %images.1), channel_id=1, source_target_pairs={{0,1016},{8,0},{16,8},{24,16},{32,24},{40,32},{48,40},{56,48},{64,... | collective-permute-start | bytes 884744 | tf_op jit(solution)/shard_map/ppermute | solution.py:97
  47.8 0.0 collective-permute-done.3.t1
  47.8 0.0 collective-permute-done.2.left.last
  47.9 0.0 collective-permute-done.5.t3
  47.9 1.0 %copy-done = bf16[128,1152]{1,0:T(8,128)(2,1)S(1)} copy-done((bf16[128,1152]{1,0:T(8,128)(2,1)S(1)}, bf16[128,1152]{1,0:T(8,128)(2,1)}, u32[]{:S(2)}) %copy-start) | copy-done | bytes 294936
  48.8 0.8 shard_map.60
  49.7 0.0 copy-start.2
  49.7 2.4 %collective-permute-start.8 = (bf16[128,1152]{1,0:T(8,128)(2,1)S(1)}, bf16[128,1152]{1,0:T(8,128)(2,1)S(1)}, u32[]{:S(2)}, u32[]{:S(2)}) collective-permute-start(bf16[128,1152]{1,0:T(8,128)(2,1)S(1)} %get-tuple-element.23), channel_id=1, source_target_pairs={{0,8},{8,16},{16,24},{24,32},{32,40},{40,48},{48,56},{56,64},{64,7... | collective-permute-start | bytes 884744 | tf_op jit(solution)/shard_map/ppermute | solution.py:111
  52.0 2.2 %collective-permute-done.1.left.guests = bf16[128,1152]{1,0:T(8,128)(2,1)S(1)} collective-permute-done((bf16[128,1152]{1,0:T(8,128)(2,1)}, bf16[128,1152]{1,0:T(8,128)(2,1)S(1)}, u32[]{:S(2)}, u32[]{:S(2)}) %collective-permute-start.1) | collective-permute-done | bytes 294944 | tf_op jit(solution)/shard_map/ppermute | solution.py:97
  54.2 0.8 shard_map.59
  55.0 1.9 %collective-permute-start.6 = (bf16[128,1152]{1,0:T(8,128)(2,1)S(1)}, bf16[128,1152]{1,0:T(8,128)(2,1)S(1)}, u32[]{:S(2)}, u32[]{:S(2)}) collective-permute-start(bf16[128,1152]{1,0:T(8,128)(2,1)S(1)} %get-tuple-element.18), channel_id=1, source_target_pairs={{0,8},{8,16},{16,24},{24,32},{32,40},{40,48},{48,56},{56,64},{64,7... | collective-permute-start | bytes 884744 | tf_op jit(solution)/shard_map/ppermute | solution.py:107
  57.0 1.8 %shard_map.61 = (f32[128,1152]{1,0:T(8,128)S(1)}, f32[128,1152]{1,0:T(8,128)S(1)}, f32[128,1152]{1,0:T(8,128)S(1)}, f32[128,1152]{1,0:T(8,128)S(1)}, bf16[256,1152]{1,0:T(8,128)(2,1)S(1)}) custom-call(f32[1]{0:T(128)S(6)} %copy.6.stretch, f32[1]{0:T(128)S(6)} %copy.7.offset_term, bf16[128,1152]{1,0:T(8,128)(2,1)S(1)} %copy-done.2, ...), custom_call_target="tpu_custom_call" | custom-call | flops 1207959552 | tf_op jit(solution)/shard_map/pallas_call | solution.py:72
  58.7 2.7 %collective-permute-start.7 = (bf16[256,1152]{1,0:T(8,128)(2,1)S(1)}, bf16[256,1152]{1,0:T(8,128)(2,1)S(1)}, u32[]{:S(2)}, u32[]{:S(2)}) collective-permute-start(bf16[256,1152]{1,0:T(8,128)(2,1)S(1)} %get-tuple-element.20), channel_id=1, source_target_pairs={{0,1},{1,0},{2,3},{3,2},{4,5},{5,4},{6,7},{7,6},{8,9},{9,8},{10,11... | collective-permute-start | bytes 1769480 | tf_op jit(solution)/shard_map/ppermute | solution.py:119
  61.5 2.2 %collective-permute-done.8 = bf16[128,1152]{1,0:T(8,128)(2,1)S(1)} collective-permute-done((bf16[128,1152]{1,0:T(8,128)(2,1)S(1)}, bf16[128,1152]{1,0:T(8,128)(2,1)S(1)}, u32[]{:S(2)}, u32[]{:S(2)}) %collective-permute-start.8) | collective-permute-done | bytes 294944 | tf_op jit(solution)/shard_map/ppermute | solution.py:111
  63.7 0.1 add_convert_fusion
  63.7 4.7 %collective-permute-start.9 = (bf16[128,1152]{1,0:T(8,128)(2,1)S(1)}, bf16[128,1152]{1,0:T(8,128)(2,1)S(1)}, u32[]{:S(2)}, u32[]{:S(2)}) collective-permute-start(bf16[128,1152]{1,0:T(8,128)(2,1)S(1)} %add_convert_fusion), channel_id=1, source_target_pairs={{0,6},{1,7},{2,4},{3,5},{4,2},{5,3},{6,0},{7,1},{8,14},{9,15},{10,... | collective-permute-start | bytes 884744 | tf_op jit(solution)/shard_map/ppermute | solution.py:126
  68.5 1.9 %collective-permute-done.6 = bf16[128,1152]{1,0:T(8,128)(2,1)S(1)} collective-permute-done((bf16[128,1152]{1,0:T(8,128)(2,1)S(1)}, bf16[128,1152]{1,0:T(8,128)(2,1)S(1)}, u32[]{:S(2)}, u32[]{:S(2)}) %collective-permute-start.6) | collective-permute-done | bytes 294944 | tf_op jit(solution)/shard_map/ppermute | solution.py:107
  70.4 0.1 convert_add_fusion.2
  70.5 0.0 collective-permute-done.7
  70.5 0.1 add_convert_fusion.1
  70.5 1.9 %collective-permute-start.10 = (bf16[128,1152]{1,0:T(8,128)(2,1)S(1)}, bf16[128,1152]{1,0:T(8,128)(2,1)S(1)}, u32[]{:S(2)}, u32[]{:S(2)}) collective-permute-start(bf16[128,1152]{1,0:T(8,128)(2,1)S(1)} %add_convert_fusion.1), channel_id=1, source_target_pairs={{0,2},{1,3},{2,0},{3,1},{4,6},{5,7},{6,4},{7,5},{8,10},{9,11},{10,... | collective-permute-start | bytes 884744 | tf_op jit(solution)/shard_map/ppermute | solution.py:125
  72.5 7.5 %collective-permute-done.9 = bf16[128,1152]{1,0:T(8,128)(2,1)S(1)} collective-permute-done((bf16[128,1152]{1,0:T(8,128)(2,1)S(1)}, bf16[128,1152]{1,0:T(8,128)(2,1)S(1)}, u32[]{:S(2)}, u32[]{:S(2)}) %collective-permute-start.9) | collective-permute-done | bytes 294944 | tf_op jit(solution)/shard_map/ppermute | solution.py:126
  80.0 0.9 %convert_add_fusion.1 = f32[128,1152]{1,0:T(8,128)} fusion(f32[128,1152]{1,0:T(8,128)S(1)} %convert_add_fusion.2, bf16[128,1152]{1,0:T(8,128)(2,1)S(1)} %collective-permute-done.9), kind=kLoop, calls=%fused_computation.1 | loop fusion | flops 294912 | bytes 1474560 | tf_op jit(solution)/shard_map/add | solution.py:130
  80.9 4.6 %collective-permute-done.10 = bf16[128,1152]{1,0:T(8,128)(2,1)S(1)} collective-permute-done((bf16[128,1152]{1,0:T(8,128)(2,1)S(1)}, bf16[128,1152]{1,0:T(8,128)(2,1)S(1)}, u32[]{:S(2)}, u32[]{:S(2)}) %collective-permute-start.10) | collective-permute-done | bytes 294944 | tf_op jit(solution)/shard_map/ppermute | solution.py:125
  85.5 0.9 %convert_add_fusion = f32[128,1152]{1,0:T(8,128)} fusion(bf16[128,1152]{1,0:T(8,128)(2,1)S(1)} %collective-permute-done.10, f32[128,1152]{1,0:T(8,128)S(1)} %get-tuple-element.26, bf16[256,1152]{1,0:T(8,128)(2,1)S(1)} %collective-permute-done.7), kind=kLoop, calls=%fused_computation | loop fusion | flops 589824 | bytes 1769472 | tf_op jit(solution)/shard_map/add | solution.py:129
  (4 shorter events, 0.0 us)
Async XLA Ops:
  0.6 27.4 %collective-permute-start = (bf16[128,1152]{1,0:T(8,128)(2,1)}, bf16[128,1152]{1,0:T(8,128)(2,1)S(1)}, u32[]{:S(2)}, u32[]{:S(2)}) collective-permute-start(bf16[128,1152]{1,0:T(8,128)(2,1)} %images.1), channel_id=1, source_target_pairs={{0,6},{1,7},{2,4},{3,5},{4,2},{5,3},{6,0},{7,1},{8,14},{9,15},{10,... | collective-permute-start | bytes 884744 | tf_op jit(solution)/shard_map/ppermute | solution.py:93
  17.6 23.1 %collective-permute-start.4 = (bf16[128,1152]{1,0:T(8,128)(2,1)}, bf16[128,1152]{1,0:T(8,128)(2,1)S(1)}, u32[]{:S(2)}, u32[]{:S(2)}) collective-permute-start(bf16[128,1152]{1,0:T(8,128)(2,1)} %t0.5), channel_id=1, source_target_pairs={{0,2},{1,3},{2,0},{3,1},{4,6},{5,7},{6,4},{7,5},{8,10},{9,11},{10,... | collective-permute-start | bytes 884744 | tf_op jit(solution)/shard_map/ppermute | solution.py:96
  19.5 28.3 %collective-permute-start.3 = (bf16[128,1152]{1,0:T(8,128)(2,1)}, bf16[128,1152]{1,0:T(8,128)(2,1)S(1)}, u32[]{:S(2)}, u32[]{:S(2)}) collective-permute-start(bf16[128,1152]{1,0:T(8,128)(2,1)} %t0.5), channel_id=1, source_target_pairs={{0,1},{1,0},{2,3},{3,2},{4,5},{5,4},{6,7},{7,6},{8,9},{9,8},{10,11... | collective-permute-start | bytes 884744 | tf_op jit(solution)/shard_map/ppermute | solution.py:94
  28.0 19.8 %collective-permute-start.2 = (bf16[128,1152]{1,0:T(8,128)(2,1)S(1)}, bf16[128,1152]{1,0:T(8,128)(2,1)S(1)}, u32[]{:S(2)}, u32[]{:S(2)}) collective-permute-start(bf16[128,1152]{1,0:T(8,128)(2,1)S(1)} %collective-permute-done.across), channel_id=1, source_target_pairs={{0,1016},{8,0},{16,8},{24,16},{32,24},{40,32},{48,40},{56,48},{64,... | collective-permute-start | bytes 884744 | tf_op jit(solution)/shard_map/ppermute | solution.py:98
  40.7 7.1 %collective-permute-start.5 = (bf16[128,1152]{1,0:T(8,128)(2,1)S(1)}, bf16[128,1152]{1,0:T(8,128)(2,1)S(1)}, u32[]{:S(2)}, u32[]{:S(2)}) collective-permute-start(bf16[128,1152]{1,0:T(8,128)(2,1)S(1)} %collective-permute-done.4.t2), channel_id=1, source_target_pairs={{0,1},{1,0},{2,3},{3,2},{4,5},{5,4},{6,7},{7,6},{8,9},{9,8},{10,11... | collective-permute-start | bytes 884744 | tf_op jit(solution)/shard_map/ppermute | solution.py:99
  43.5 10.7 %collective-permute-start.1 = (bf16[128,1152]{1,0:T(8,128)(2,1)}, bf16[128,1152]{1,0:T(8,128)(2,1)S(1)}, u32[]{:S(2)}, u32[]{:S(2)}) collective-permute-start(bf16[128,1152]{1,0:T(8,128)(2,1)} %images.1), channel_id=1, source_target_pairs={{0,1016},{8,0},{16,8},{24,16},{32,24},{40,32},{48,40},{56,48},{64,... | collective-permute-start | bytes 884744 | tf_op jit(solution)/shard_map/ppermute | solution.py:97
  47.9 1.0 %copy-start = (bf16[128,1152]{1,0:T(8,128)(2,1)S(1)}, bf16[128,1152]{1,0:T(8,128)(2,1)}, u32[]{:S(2)}) copy-start(bf16[128,1152]{1,0:T(8,128)(2,1)} %t0.5) | copy-start | bytes 884740
  48.8 5.4 %copy-start.1 = (bf16[128,1152]{1,0:T(8,128)(2,1)S(1)}, bf16[128,1152]{1,0:T(8,128)(2,1)}, u32[]{:S(2)}) copy-start(bf16[128,1152]{1,0:T(8,128)(2,1)} %t0.5) | copy-start | bytes 884740
  49.7 7.3 %copy-start.2 = (bf16[128,1152]{1,0:T(8,128)(2,1)S(1)}, bf16[128,1152]{1,0:T(8,128)(2,1)}, u32[]{:S(2)}) copy-start(bf16[128,1152]{1,0:T(8,128)(2,1)} %images.1) | copy-start | bytes 884740
  49.7 14.0 %collective-permute-start.8 = (bf16[128,1152]{1,0:T(8,128)(2,1)S(1)}, bf16[128,1152]{1,0:T(8,128)(2,1)S(1)}, u32[]{:S(2)}, u32[]{:S(2)}) collective-permute-start(bf16[128,1152]{1,0:T(8,128)(2,1)S(1)} %get-tuple-element.23), channel_id=1, source_target_pairs={{0,8},{8,16},{16,24},{24,32},{32,40},{40,48},{48,56},{56,64},{64,7... | collective-permute-start | bytes 884744 | tf_op jit(solution)/shard_map/ppermute | solution.py:111
  55.0 15.4 %collective-permute-start.6 = (bf16[128,1152]{1,0:T(8,128)(2,1)S(1)}, bf16[128,1152]{1,0:T(8,128)(2,1)S(1)}, u32[]{:S(2)}, u32[]{:S(2)}) collective-permute-start(bf16[128,1152]{1,0:T(8,128)(2,1)S(1)} %get-tuple-element.18), channel_id=1, source_target_pairs={{0,8},{8,16},{16,24},{24,32},{32,40},{40,48},{48,56},{56,64},{64,7... | collective-permute-start | bytes 884744 | tf_op jit(solution)/shard_map/ppermute | solution.py:107
  58.7 11.7 %collective-permute-start.7 = (bf16[256,1152]{1,0:T(8,128)(2,1)S(1)}, bf16[256,1152]{1,0:T(8,128)(2,1)S(1)}, u32[]{:S(2)}, u32[]{:S(2)}) collective-permute-start(bf16[256,1152]{1,0:T(8,128)(2,1)S(1)} %get-tuple-element.20), channel_id=1, source_target_pairs={{0,1},{1,0},{2,3},{3,2},{4,5},{5,4},{6,7},{7,6},{8,9},{9,8},{10,11... | collective-permute-start | bytes 1769480 | tf_op jit(solution)/shard_map/ppermute | solution.py:119
  63.7 16.2 %collective-permute-start.9 = (bf16[128,1152]{1,0:T(8,128)(2,1)S(1)}, bf16[128,1152]{1,0:T(8,128)(2,1)S(1)}, u32[]{:S(2)}, u32[]{:S(2)}) collective-permute-start(bf16[128,1152]{1,0:T(8,128)(2,1)S(1)} %add_convert_fusion), channel_id=1, source_target_pairs={{0,6},{1,7},{2,4},{3,5},{4,2},{5,3},{6,0},{7,1},{8,14},{9,15},{10,... | collective-permute-start | bytes 884744 | tf_op jit(solution)/shard_map/ppermute | solution.py:126
  70.5 15.0 %collective-permute-start.10 = (bf16[128,1152]{1,0:T(8,128)(2,1)S(1)}, bf16[128,1152]{1,0:T(8,128)(2,1)S(1)}, u32[]{:S(2)}, u32[]{:S(2)}) collective-permute-start(bf16[128,1152]{1,0:T(8,128)(2,1)S(1)} %add_convert_fusion.1), channel_id=1, source_target_pairs={{0,2},{1,3},{2,0},{3,1},{4,6},{5,7},{6,4},{7,5},{8,10},{9,11},{10,... | collective-permute-start | bytes 884744 | tf_op jit(solution)/shard_map/ppermute | solution.py:125

commit v5 on v4

--- a/solution.py
+++ b/solution.py
@@ -105,6 +105,7 @@
         guests_kernel, guests_outs, 2 * block, stretch, offset_term, guests, *all_texts
     )
     back = lax.ppermute(guests_part, "outer", to_next)
+    guests_across, guests_part = lax.optimization_barrier((guests_across, guests_part))
     last_coef, last_part = local_call(
         guests_kernel, guests_outs, 2 * block, stretch, offset_term, guests_across, *all_texts
     )
@@ -117,17 +118,15 @@
         guests_coef, last_coef, *all_texts,
     )
     from_core = lax.ppermute(for_core, "inner", other_core)
-    own = own + back.astype(F32)
-    own_across, back_across = lax.optimization_barrier((own_across, back_across))
+    back, own_across, back_across = lax.optimization_barrier((back, own_across, back_across))
     mine = mine + from_core[rows:].astype(F32)
     sent = (far + from_core[:rows].astype(F32)).astype(BF16)
-    own, sent = lax.optimization_barrier((own, sent))
     from_beside = lax.ppermute(sent, "inner", beside)
     from_across = lax.ppermute(
         (own_across + back_across.astype(F32)).astype(BF16), "inner", across
     )
     grad_text = mine + from_beside.astype(F32)
-    grad_image = own + from_across.astype(F32)
+    grad_image = own + back.astype(F32) + from_across.astype(F32)
     return grad_image, grad_text
 
 

time: 86.9 us -> 88.9 us (1.023)
  starting transfers between devices: 53.8 us -> 64.5 us
  waiting for transfers between devices: 24.2 us -> 15.6 us
    ppermute x1, starting transfers between devices: 3.06 us -> 10 us  [per_device(): guests = lax.ppermute(images, 'outer', to_previous)]
    ppermute x1, starting transfers between devices: 1.92 us -> 8.46 us  [per_device(): texts_beside = lax.ppermute(texts_out, 'inner', beside)]
    ppermute x1, starting transfers between devices: 16.9 us -> 10.4 us  [per_device(): images_across = lax.ppermute(images, 'inner', across)]
    ppermute x1, waiting for transfers between devices: 5.64 us -> 0.01 us  [per_device(): images_across = lax.ppermute(images, 'inner', across)]
    ppermute x1, waiting for transfers between devices: 7.53 us -> 3.08 us  [per_device(): lax.ppermute((own_across + back_across.astype(F32)).astype(BF16), 'inner'...]
    ppermute x1, waiting for transfers between devices: 2.24 us -> 6.32 us  [per_device(): back_across = lax.ppermute(last_part, 'outer', to_next)]
    ppermute x1, starting transfers between devices: 4.72 us -> 7.67 us  [per_device(): lax.ppermute((own_across + back_across.astype(F32)).astype(BF16), 'inner'...]
    ppermute x1, waiting for transfers between devices: 2.17 us -> 0.01 us  [per_device(): guests = lax.ppermute(images, 'outer', to_previous)]
  transfers between devices with their start and end apart: 11 -> 11, of which waited for: 6 -> 5; matrix products, arithmetic and copies ran while one was open for 1% -> 1% of each run, Pallas kernels for 4% -> 4%
where the time goes in v5:
time: 88.9 us; the launch traced here: 88.5 us
  starting transfers between devices  64.5 us (73%)
  waiting for transfers between devices  15.6 us (18%)
  Pallas kernels  3.4 us (4%)
  between operations  2.11 us (2%)
  other arithmetic  1.89 us (2%)
  local copies, waits for them, and re-layouts  0.96 us (1%)
    ppermute x1, starting transfers between devices, per_device(): guests_across = lax.ppermute(images_across, 'outer', to_previous)  12.3 us
    ppermute x1, starting transfers between devices, per_device(): images_across = lax.ppermute(images, 'inner', across)  10.4 us
    ppermute x1, starting transfers between devices, per_device(): guests = lax.ppermute(images, 'outer', to_previous)  10 us
    ppermute x1, starting transfers between devices, per_device(): texts_beside = lax.ppermute(texts_out, 'inner', beside)  8.46 us
    ppermute x1, starting transfers between devices, per_device(): lax.ppermute((own_across + back_across.astype(F32)).astype(BF16), 'inner'...  7.67 us
    ppermute x1, waiting for transfers between devices, per_device(): back_across = lax.ppermute(last_part, 'outer', to_next)  6.32 us
    ppermute x1, starting transfers between devices, per_device(): from_core = lax.ppermute(for_core, 'inner', other_core)  3.67 us
    pallas_call x3, Pallas kernels, local_call(): pl.pallas_call(kernel, out_shape=[jax.ShapeDtypeStruct(shape, dtype) for...  3.4 us
  transfers between devices with their start and end apart: 11, of which 5 were waited for; matrix products, arithmetic and copies ran while one was open for 1% of the time, Pallas kernels for 4%

profile of v5, /device:TPU:1, one launch (start us, length us, event | category | flops | bytes accessed | tf_op | source)
XLA Modules:
  0.0 88.5 jit_solution(9184873680115609086)
XLA Ops:
  0.6 8.5 %collective-permute-start.4 = (bf16[128,1152]{1,0:T(8,128)(2,1)}, bf16[128,1152]{1,0:T(8,128)(2,1)S(1)}, u32[]{:S(2)}, u32[]{:S(2)}) collective-permute-start(bf16[128,1152]{1,0:T(8,128)(2,1)} %t0.5), channel_id=1, source_target_pairs={{0,2},{1,3},{2,0},{3,1},{4,6},{5,7},{6,4},{7,5},{8,10},{9,11},{10,... | collective-permute-start | bytes 884744 | tf_op jit(solution)/shard_map/ppermute | solution.py:96
  9.1 10.4 %collective-permute-start = (bf16[128,1152]{1,0:T(8,128)(2,1)}, bf16[128,1152]{1,0:T(8,128)(2,1)S(1)}, u32[]{:S(2)}, u32[]{:S(2)}) collective-permute-start(bf16[128,1152]{1,0:T(8,128)(2,1)} %images.1), channel_id=1, source_target_pairs={{0,6},{1,7},{2,4},{3,5},{4,2},{5,3},{6,0},{7,1},{8,14},{9,15},{10,... | collective-permute-start | bytes 884744 | tf_op jit(solution)/shard_map/ppermute | solution.py:93
  19.5 10.0 %collective-permute-start.1 = (bf16[128,1152]{1,0:T(8,128)(2,1)}, bf16[128,1152]{1,0:T(8,128)(2,1)S(1)}, u32[]{:S(2)}, u32[]{:S(2)}) collective-permute-start(bf16[128,1152]{1,0:T(8,128)(2,1)} %images.1), channel_id=1, source_target_pairs={{0,1016},{8,0},{16,8},{24,16},{32,24},{40,32},{48,40},{56,48},{64,... | collective-permute-start | bytes 884744 | tf_op jit(solution)/shard_map/ppermute | solution.py:97
  29.5 3.1 %collective-permute-start.3 = (bf16[128,1152]{1,0:T(8,128)(2,1)}, bf16[128,1152]{1,0:T(8,128)(2,1)S(1)}, u32[]{:S(2)}, u32[]{:S(2)}) collective-permute-start(bf16[128,1152]{1,0:T(8,128)(2,1)} %t0.5), channel_id=1, source_target_pairs={{0,1},{1,0},{2,3},{3,2},{4,5},{5,4},{6,7},{7,6},{8,9},{9,8},{10,11... | collective-permute-start | bytes 884744 | tf_op jit(solution)/shard_map/ppermute | solution.py:94
  32.7 0.0 collective-permute-done.4.t2
  32.7 1.9 %collective-permute-start.5 = (bf16[128,1152]{1,0:T(8,128)(2,1)S(1)}, bf16[128,1152]{1,0:T(8,128)(2,1)S(1)}, u32[]{:S(2)}, u32[]{:S(2)}) collective-permute-start(bf16[128,1152]{1,0:T(8,128)(2,1)S(1)} %collective-permute-done.4.t2), channel_id=1, source_target_pairs={{0,1},{1,0},{2,3},{3,2},{4,5},{5,4},{6,7},{7,6},{8,9},{9,8},{10,11... | collective-permute-start | bytes 884744 | tf_op jit(solution)/shard_map/ppermute | solution.py:99
  34.6 0.0 collective-permute-done.across
  34.6 12.3 %collective-permute-start.2 = (bf16[128,1152]{1,0:T(8,128)(2,1)S(1)}, bf16[128,1152]{1,0:T(8,128)(2,1)S(1)}, u32[]{:S(2)}, u32[]{:S(2)}) collective-permute-start(bf16[128,1152]{1,0:T(8,128)(2,1)S(1)} %collective-permute-done.across), channel_id=1, source_target_pairs={{0,1016},{8,0},{16,8},{24,16},{32,24},{40,32},{48,40},{56,48},{64,... | collective-permute-start | bytes 884744 | tf_op jit(solution)/shard_map/ppermute | solution.py:98
  48.2 0.0 collective-permute-done.1.left.guests
  48.2 0.0 collective-permute-done.3.t1
  48.2 0.0 collective-permute-done.5.t3
  48.3 0.0 copy-start
  48.3 1.0 %copy-done = bf16[128,1152]{1,0:T(8,128)(2,1)S(1)} copy-done((bf16[128,1152]{1,0:T(8,128)(2,1)S(1)}, bf16[128,1152]{1,0:T(8,128)(2,1)}, u32[]{:S(2)}) %copy-start) | copy-done | bytes 294936
  49.2 0.8 shard_map.59
  50.0 0.0 copy-start.2
  50.1 2.1 %collective-permute-start.6 = (bf16[128,1152]{1,0:T(8,128)(2,1)S(1)}, bf16[128,1152]{1,0:T(8,128)(2,1)S(1)}, u32[]{:S(2)}, u32[]{:S(2)}) collective-permute-start(bf16[128,1152]{1,0:T(8,128)(2,1)S(1)} %get-tuple-element.15), channel_id=1, source_target_pairs={{0,8},{8,16},{16,24},{24,32},{32,40},{40,48},{48,56},{56,64},{64,7... | collective-permute-start | bytes 884744 | tf_op jit(solution)/shard_map/ppermute | solution.py:107
  52.1 0.3 collective-permute-done.2.left.last
  52.4 0.8 shard_map.60
  53.2 1.9 %collective-permute-start.7 = (bf16[128,1152]{1,0:T(8,128)(2,1)S(1)}, bf16[128,1152]{1,0:T(8,128)(2,1)S(1)}, u32[]{:S(2)}, u32[]{:S(2)}) collective-permute-start(bf16[128,1152]{1,0:T(8,128)(2,1)S(1)} %get-tuple-element.21), channel_id=1, source_target_pairs={{0,8},{8,16},{16,24},{24,32},{32,40},{40,48},{48,56},{56,64},{64,7... | collective-permute-start | bytes 884744 | tf_op jit(solution)/shard_map/ppermute | solution.py:112
  55.1 1.8 %shard_map.61 = (f32[128,1152]{1,0:T(8,128)S(1)}, f32[128,1152]{1,0:T(8,128)S(1)}, f32[128,1152]{1,0:T(8,128)S(1)}, f32[128,1152]{1,0:T(8,128)S(1)}, bf16[256,1152]{1,0:T(8,128)(2,1)S(1)}) custom-call(f32[1]{0:T(128)S(6)} %copy.6.stretch, f32[1]{0:T(128)S(6)} %copy.7.offset_term, bf16[128,1152]{1,0:T(8,128)(2,1)S(1)} %copy-done.2, ...), custom_call_target="tpu_custom_call" | custom-call | flops 1207959552 | tf_op jit(solution)/shard_map/pallas_call | solution.py:72
  56.9 3.7 %collective-permute-start.9 = (bf16[256,1152]{1,0:T(8,128)(2,1)S(1)}, bf16[256,1152]{1,0:T(8,128)(2,1)S(1)}, u32[]{:S(2)}, u32[]{:S(2)}) collective-permute-start(bf16[256,1152]{1,0:T(8,128)(2,1)S(1)} %get-tuple-element.26), channel_id=1, source_target_pairs={{0,1},{1,0},{2,3},{3,2},{4,5},{5,4},{6,7},{7,6},{8,9},{9,8},{10,11... | collective-permute-start | bytes 1769480 | tf_op jit(solution)/shard_map/ppermute | solution.py:120
  60.6 3.1 %collective-permute-done.6 = bf16[128,1152]{1,0:T(8,128)(2,1)S(1)} collective-permute-done((bf16[128,1152]{1,0:T(8,128)(2,1)S(1)}, bf16[128,1152]{1,0:T(8,128)(2,1)S(1)}, u32[]{:S(2)}, u32[]{:S(2)}) %collective-permute-start.6) | collective-permute-done | bytes 294944 | tf_op jit(solution)/shard_map/ppermute | solution.py:107
  63.7 6.3 %collective-permute-done.7 = bf16[128,1152]{1,0:T(8,128)(2,1)S(1)} collective-permute-done((bf16[128,1152]{1,0:T(8,128)(2,1)S(1)}, bf16[128,1152]{1,0:T(8,128)(2,1)S(1)}, u32[]{:S(2)}, u32[]{:S(2)}) %collective-permute-start.7) | collective-permute-done | bytes 294944 | tf_op jit(solution)/shard_map/ppermute | solution.py:112
  70.0 0.1 add_convert_fusion.1
  70.0 7.7 %collective-permute-start.8 = (bf16[128,1152]{1,0:T(8,128)(2,1)S(1)}, bf16[128,1152]{1,0:T(8,128)(2,1)S(1)}, u32[]{:S(2)}, u32[]{:S(2)}) collective-permute-start(bf16[128,1152]{1,0:T(8,128)(2,1)S(1)} %add_convert_fusion.1), channel_id=1, source_target_pairs={{0,6},{1,7},{2,4},{3,5},{4,2},{5,3},{6,0},{7,1},{8,14},{9,15},{10,... | collective-permute-start | bytes 884744 | tf_op jit(solution)/shard_map/ppermute | solution.py:125
  77.7 0.0 collective-permute-done.9
  77.7 0.1 add_convert_fusion
  77.8 2.9 %collective-permute-start.10 = (bf16[128,1152]{1,0:T(8,128)(2,1)S(1)}, bf16[128,1152]{1,0:T(8,128)(2,1)S(1)}, u32[]{:S(2)}, u32[]{:S(2)}) collective-permute-start(bf16[128,1152]{1,0:T(8,128)(2,1)S(1)} %add_convert_fusion), channel_id=1, source_target_pairs={{0,2},{1,3},{2,0},{3,1},{4,6},{5,7},{6,4},{7,5},{8,10},{9,11},{10,... | collective-permute-start | bytes 884744 | tf_op jit(solution)/shard_map/ppermute | solution.py:124
  80.7 3.1 %collective-permute-done.8 = bf16[128,1152]{1,0:T(8,128)(2,1)S(1)} collective-permute-done((bf16[128,1152]{1,0:T(8,128)(2,1)S(1)}, bf16[128,1152]{1,0:T(8,128)(2,1)S(1)}, u32[]{:S(2)}, u32[]{:S(2)}) %collective-permute-start.8) | collective-permute-done | bytes 294944 | tf_op jit(solution)/shard_map/ppermute | solution.py:125
  83.8 0.9 %convert_add_fusion.1 = f32[128,1152]{1,0:T(8,128)} fusion(bf16[128,1152]{1,0:T(8,128)(2,1)S(1)} %collective-permute-done.8, f32[128,1152]{1,0:T(8,128)S(1)} %get-tuple-element.19, bf16[128,1152]{1,0:T(8,128)(2,1)S(1)} %collective-permute-done.6), kind=kLoop, calls=%fused_computation.2 | loop fusion | flops 589824 | bytes 1769472 | tf_op jit(solution)/shard_map/add | solution.py:129
  84.7 2.9 %collective-permute-done.10 = bf16[128,1152]{1,0:T(8,128)(2,1)S(1)} collective-permute-done((bf16[128,1152]{1,0:T(8,128)(2,1)S(1)}, bf16[128,1152]{1,0:T(8,128)(2,1)S(1)}, u32[]{:S(2)}, u32[]{:S(2)}) %collective-permute-start.10) | collective-permute-done | bytes 294944 | tf_op jit(solution)/shard_map/ppermute | solution.py:124
  87.6 0.9 %convert_add_fusion = f32[128,1152]{1,0:T(8,128)} fusion(bf16[128,1152]{1,0:T(8,128)(2,1)S(1)} %collective-permute-done.10, f32[128,1152]{1,0:T(8,128)S(1)} %get-tuple-element.25, bf16[256,1152]{1,0:T(8,128)(2,1)S(1)} %collective-permute-done.9), kind=kLoop, calls=%fused_computation | loop fusion | flops 589824 | bytes 1769472 | tf_op jit(solution)/shard_map/add | solution.py:128
  (3 shorter events, 0.0 us)
Async XLA Ops:
  0.6 32.1 %collective-permute-start.4 = (bf16[128,1152]{1,0:T(8,128)(2,1)}, bf16[128,1152]{1,0:T(8,128)(2,1)S(1)}, u32[]{:S(2)}, u32[]{:S(2)}) collective-permute-start(bf16[128,1152]{1,0:T(8,128)(2,1)} %t0.5), channel_id=1, source_target_pairs={{0,2},{1,3},{2,0},{3,1},{4,6},{5,7},{6,4},{7,5},{8,10},{9,11},{10,... | collective-permute-start | bytes 884744 | tf_op jit(solution)/shard_map/ppermute | solution.py:96
  9.1 25.5 %collective-permute-start = (bf16[128,1152]{1,0:T(8,128)(2,1)}, bf16[128,1152]{1,0:T(8,128)(2,1)S(1)}, u32[]{:S(2)}, u32[]{:S(2)}) collective-permute-start(bf16[128,1152]{1,0:T(8,128)(2,1)} %images.1), channel_id=1, source_target_pairs={{0,6},{1,7},{2,4},{3,5},{4,2},{5,3},{6,0},{7,1},{8,14},{9,15},{10,... | collective-permute-start | bytes 884744 | tf_op jit(solution)/shard_map/ppermute | solution.py:93
  19.5 28.7 %collective-permute-start.1 = (bf16[128,1152]{1,0:T(8,128)(2,1)}, bf16[128,1152]{1,0:T(8,128)(2,1)S(1)}, u32[]{:S(2)}, u32[]{:S(2)}) collective-permute-start(bf16[128,1152]{1,0:T(8,128)(2,1)} %images.1), channel_id=1, source_target_pairs={{0,1016},{8,0},{16,8},{24,16},{32,24},{40,32},{48,40},{56,48},{64,... | collective-permute-start | bytes 884744 | tf_op jit(solution)/shard_map/ppermute | solution.py:97
  29.5 18.7 %collective-permute-start.3 = (bf16[128,1152]{1,0:T(8,128)(2,1)}, bf16[128,1152]{1,0:T(8,128)(2,1)S(1)}, u32[]{:S(2)}, u32[]{:S(2)}) collective-permute-start(bf16[128,1152]{1,0:T(8,128)(2,1)} %t0.5), channel_id=1, source_target_pairs={{0,1},{1,0},{2,3},{3,2},{4,5},{5,4},{6,7},{7,6},{8,9},{9,8},{10,11... | collective-permute-start | bytes 884744 | tf_op jit(solution)/shard_map/ppermute | solution.py:94
  32.7 15.5 %collective-permute-start.5 = (bf16[128,1152]{1,0:T(8,128)(2,1)S(1)}, bf16[128,1152]{1,0:T(8,128)(2,1)S(1)}, u32[]{:S(2)}, u32[]{:S(2)}) collective-permute-start(bf16[128,1152]{1,0:T(8,128)(2,1)S(1)} %collective-permute-done.4.t2), channel_id=1, source_target_pairs={{0,1},{1,0},{2,3},{3,2},{4,5},{5,4},{6,7},{7,6},{8,9},{9,8},{10,11... | collective-permute-start | bytes 884744 | tf_op jit(solution)/shard_map/ppermute | solution.py:99
  34.6 17.7 %collective-permute-start.2 = (bf16[128,1152]{1,0:T(8,128)(2,1)S(1)}, bf16[128,1152]{1,0:T(8,128)(2,1)S(1)}, u32[]{:S(2)}, u32[]{:S(2)}) collective-permute-start(bf16[128,1152]{1,0:T(8,128)(2,1)S(1)} %collective-permute-done.across), channel_id=1, source_target_pairs={{0,1016},{8,0},{16,8},{24,16},{32,24},{40,32},{48,40},{56,48},{64,... | collective-permute-start | bytes 884744 | tf_op jit(solution)/shard_map/ppermute | solution.py:98
  48.3 1.0 %copy-start = (bf16[128,1152]{1,0:T(8,128)(2,1)S(1)}, bf16[128,1152]{1,0:T(8,128)(2,1)}, u32[]{:S(2)}) copy-start(bf16[128,1152]{1,0:T(8,128)(2,1)} %t0.5) | copy-start | bytes 884740
  49.2 3.2 %copy-start.1 = (bf16[128,1152]{1,0:T(8,128)(2,1)S(1)}, bf16[128,1152]{1,0:T(8,128)(2,1)}, u32[]{:S(2)}) copy-start(bf16[128,1152]{1,0:T(8,128)(2,1)} %t0.5) | copy-start | bytes 884740
  50.0 5.1 %copy-start.2 = (bf16[128,1152]{1,0:T(8,128)(2,1)S(1)}, bf16[128,1152]{1,0:T(8,128)(2,1)}, u32[]{:S(2)}) copy-start(bf16[128,1152]{1,0:T(8,128)(2,1)} %images.1) | copy-start | bytes 884740
  50.1 13.6 %collective-permute-start.6 = (bf16[128,1152]{1,0:T(8,128)(2,1)S(1)}, bf16[128,1152]{1,0:T(8,128)(2,1)S(1)}, u32[]{:S(2)}, u32[]{:S(2)}) collective-permute-start(bf16[128,1152]{1,0:T(8,128)(2,1)S(1)} %get-tuple-element.15), channel_id=1, source_target_pairs={{0,8},{8,16},{16,24},{24,32},{32,40},{40,48},{48,56},{56,64},{64,7... | collective-permute-start | bytes 884744 | tf_op jit(solution)/shard_map/ppermute | solution.py:107
  53.2 16.8 %collective-permute-start.7 = (bf16[128,1152]{1,0:T(8,128)(2,1)S(1)}, bf16[128,1152]{1,0:T(8,128)(2,1)S(1)}, u32[]{:S(2)}, u32[]{:S(2)}) collective-permute-start(bf16[128,1152]{1,0:T(8,128)(2,1)S(1)} %get-tuple-element.21), channel_id=1, source_target_pairs={{0,8},{8,16},{16,24},{24,32},{32,40},{40,48},{48,56},{56,64},{64,7... | collective-permute-start | bytes 884744 | tf_op jit(solution)/shard_map/ppermute | solution.py:112
  56.9 20.8 %collective-permute-start.9 = (bf16[256,1152]{1,0:T(8,128)(2,1)S(1)}, bf16[256,1152]{1,0:T(8,128)(2,1)S(1)}, u32[]{:S(2)}, u32[]{:S(2)}) collective-permute-start(bf16[256,1152]{1,0:T(8,128)(2,1)S(1)} %get-tuple-element.26), channel_id=1, source_target_pairs={{0,1},{1,0},{2,3},{3,2},{4,5},{5,4},{6,7},{7,6},{8,9},{9,8},{10,11... | collective-permute-start | bytes 1769480 | tf_op jit(solution)/shard_map/ppermute | solution.py:120
  70.0 13.8 %collective-permute-start.8 = (bf16[128,1152]{1,0:T(8,128)(2,1)S(1)}, bf16[128,1152]{1,0:T(8,128)(2,1)S(1)}, u32[]{:S(2)}, u32[]{:S(2)}) collective-permute-start(bf16[128,1152]{1,0:T(8,128)(2,1)S(1)} %add_convert_fusion.1), channel_id=1, source_target_pairs={{0,6},{1,7},{2,4},{3,5},{4,2},{5,3},{6,0},{7,1},{8,14},{9,15},{10,... | collective-permute-start | bytes 884744 | tf_op jit(solution)/shard_map/ppermute | solution.py:125
  77.8 9.8 %collective-permute-start.10 = (bf16[128,1152]{1,0:T(8,128)(2,1)S(1)}, bf16[128,1152]{1,0:T(8,128)(2,1)S(1)}, u32[]{:S(2)}, u32[]{:S(2)}) collective-permute-start(bf16[128,1152]{1,0:T(8,128)(2,1)S(1)} %add_convert_fusion), channel_id=1, source_target_pairs={{0,2},{1,3},{2,0},{3,1},{4,6},{5,7},{6,4},{7,5},{8,10},{9,11},{10,... | collective-permute-start | bytes 884744 | tf_op jit(solution)/shard_map/ppermute | solution.py:124

commit v6 on v5

--- a/solution.py
+++ b/solution.py
@@ -92,8 +92,7 @@
 
     images_across = lax.ppermute(images, "inner", across)
     texts_core = lax.ppermute(texts, "inner", other_core)
-    texts_out = texts
-    texts_beside = lax.ppermute(texts_out, "inner", beside)
+    texts_beside = lax.ppermute(texts, "inner", beside)
     guests = lax.ppermute(images, "outer", to_previous)
     guests_across = lax.ppermute(images_across, "outer", to_previous)
     texts_beside_core = lax.ppermute(texts_beside, "inner", other_core)
@@ -105,7 +104,6 @@
         guests_kernel, guests_outs, 2 * block, stretch, offset_term, guests, *all_texts
     )
     back = lax.ppermute(guests_part, "outer", to_next)
-    guests_across, guests_part = lax.optimization_barrier((guests_across, guests_part))
     last_coef, last_part = local_call(
         guests_kernel, guests_outs, 2 * block, stretch, offset_term, guests_across, *all_texts
     )
@@ -118,13 +116,12 @@
         guests_coef, last_coef, *all_texts,
     )
     from_core = lax.ppermute(for_core, "inner", other_core)
-    back, own_across, back_across = lax.optimization_barrier((back, own_across, back_across))
+    own, own_across, back_across = lax.optimization_barrier((own, own_across, back_across))
     mine = mine + from_core[rows:].astype(F32)
     sent = (far + from_core[:rows].astype(F32)).astype(BF16)
+    across_sent = (own_across + back_across.astype(F32)).astype(BF16)
     from_beside = lax.ppermute(sent, "inner", beside)
-    from_across = lax.ppermute(
-        (own_across + back_across.astype(F32)).astype(BF16), "inner", across
-    )
+    from_across = lax.ppermute(across_sent, "inner", across)
     grad_text = mine + from_beside.astype(F32)
     grad_image = own + back.astype(F32) + from_across.astype(F32)
     return grad_image, grad_text

time: 88.9 us -> 83.9 us (0.944)
  starting transfers between devices: 64.5 us -> 53.8 us
  waiting for transfers between devices: 15.6 us -> 20.5 us
    ppermute x2, starting transfers between devices: 16.1 us -> 6.64 us  [the longest x1 4.72 us: per_device(): from_across = lax.ppermute(across_sent, 'inner', across)]
    ppermute x1, starting transfers between devices: 10 us -> 3.06 us  [per_device(): guests = lax.ppermute(images, 'outer', to_previous)]
    ppermute x1, starting transfers between devices: 10.4 us -> 16.9 us  [per_device(): images_across = lax.ppermute(images, 'inner', across)]
    ppermute x1, waiting for transfers between devices: 0.01 us -> 5.64 us  [per_device(): images_across = lax.ppermute(images, 'inner', across)]
    ppermute x1, waiting for transfers between devices: 6.32 us -> 2.24 us  [per_device(): back_across = lax.ppermute(last_part, 'outer', to_next)]
    ppermute x2, waiting for transfers between devices: 3.08 us -> 6.63 us  [the longest x1 6.63 us: per_device(): from_across = lax.ppermute(across_sent, 'inner', across)]
    ppermute x1, waiting for transfers between devices: 2.88 us -> 0.01 us  [per_device(): from_beside = lax.ppermute(sent, 'inner', beside)]
    ppermute x1, waiting for transfers between devices: 0.01 us -> 2.17 us  [per_device(): guests = lax.ppermute(images, 'outer', to_previous)]
where the time goes in v6:
time: 83.9 us; the launch traced here: 82.7 us
  starting transfers between devices  53.8 us (64%)
  waiting for transfers between devices  20.5 us (24%)
  Pallas kernels  3.4 us (4%)
  between operations  2.11 us (3%)
  other arithmetic  1.89 us (2%)
  local copies, waits for them, and re-layouts  0.96 us (1%)
    ppermute x1, starting transfers between devices, per_device(): images_across = lax.ppermute(images, 'inner', across)  16.9 us
    ppermute x1, starting transfers between devices, per_device(): guests_across = lax.ppermute(images_across, 'outer', to_previous)  12.7 us
    ppermute x1, waiting for transfers between devices, per_device(): from_across = lax.ppermute(across_sent, 'inner', across)  6.63 us
    ppermute x1, waiting for transfers between devices, per_device(): images_across = lax.ppermute(images, 'inner', across)  5.64 us
    ppermute x1, starting transfers between devices, per_device(): from_across = lax.ppermute(across_sent, 'inner', across)  4.72 us
    ppermute x1, waiting for transfers between devices, per_device(): back = lax.ppermute(guests_part, 'outer', to_next)  3.84 us
    pallas_call x3, Pallas kernels, local_call(): pl.pallas_call(kernel, out_shape=[jax.ShapeDtypeStruct(shape, dtype) for...  3.4 us
    ppermute x1, starting transfers between devices, per_device(): guests = lax.ppermute(images, 'outer', to_previous)  3.06 us
  transfers between devices with their start and end apart: 11, of which 5 were waited for; matrix products, arithmetic and copies ran while one was open for 1% of the time, Pallas kernels for 4%

profile of v6, /device:TPU:1, one launch (start us, length us, event | category | flops | bytes accessed | tf_op | source)
XLA Modules:
  0.0 82.7 jit_solution(15769637336001508999)
XLA Ops:
  0.6 16.9 %collective-permute-start = (bf16[128,1152]{1,0:T(8,128)(2,1)}, bf16[128,1152]{1,0:T(8,128)(2,1)S(1)}, u32[]{:S(2)}, u32[]{:S(2)}) collective-permute-start(bf16[128,1152]{1,0:T(8,128)(2,1)} %images.1), channel_id=1, source_target_pairs={{0,6},{1,7},{2,4},{3,5},{4,2},{5,3},{6,0},{7,1},{8,14},{9,15},{10,... | collective-permute-start | bytes 884744 | tf_op jit(solution)/shard_map/ppermute | solution.py:93
  17.6 1.9 %collective-permute-start.4 = (bf16[128,1152]{1,0:T(8,128)(2,1)}, bf16[128,1152]{1,0:T(8,128)(2,1)S(1)}, u32[]{:S(2)}, u32[]{:S(2)}) collective-permute-start(bf16[128,1152]{1,0:T(8,128)(2,1)} %t0.5), channel_id=1, source_target_pairs={{0,2},{1,3},{2,0},{3,1},{4,6},{5,7},{6,4},{7,5},{8,10},{9,11},{10,... | collective-permute-start | bytes 884744 | tf_op jit(solution)/shard_map/ppermute | solution.py:95
  19.5 2.9 %collective-permute-start.3 = (bf16[128,1152]{1,0:T(8,128)(2,1)}, bf16[128,1152]{1,0:T(8,128)(2,1)S(1)}, u32[]{:S(2)}, u32[]{:S(2)}) collective-permute-start(bf16[128,1152]{1,0:T(8,128)(2,1)} %t0.5), channel_id=1, source_target_pairs={{0,1},{1,0},{2,3},{3,2},{4,5},{5,4},{6,7},{7,6},{8,9},{9,8},{10,11... | collective-permute-start | bytes 884744 | tf_op jit(solution)/shard_map/ppermute | solution.py:94
  22.4 5.6 %collective-permute-done.across = bf16[128,1152]{1,0:T(8,128)(2,1)S(1)} collective-permute-done((bf16[128,1152]{1,0:T(8,128)(2,1)}, bf16[128,1152]{1,0:T(8,128)(2,1)S(1)}, u32[]{:S(2)}, u32[]{:S(2)}) %collective-permute-start) | collective-permute-done | bytes 294944 | tf_op jit(solution)/shard_map/ppermute | solution.py:93
  28.0 12.7 %collective-permute-start.2 = (bf16[128,1152]{1,0:T(8,128)(2,1)S(1)}, bf16[128,1152]{1,0:T(8,128)(2,1)S(1)}, u32[]{:S(2)}, u32[]{:S(2)}) collective-permute-start(bf16[128,1152]{1,0:T(8,128)(2,1)S(1)} %collective-permute-done.across), channel_id=1, source_target_pairs={{0,1016},{8,0},{16,8},{24,16},{32,24},{40,32},{48,40},{56,48},{64,... | collective-permute-start | bytes 884744 | tf_op jit(solution)/shard_map/ppermute | solution.py:97
  40.7 0.0 collective-permute-done.4.t2
  40.7 2.7 %collective-permute-start.5 = (bf16[128,1152]{1,0:T(8,128)(2,1)S(1)}, bf16[128,1152]{1,0:T(8,128)(2,1)S(1)}, u32[]{:S(2)}, u32[]{:S(2)}) collective-permute-start(bf16[128,1152]{1,0:T(8,128)(2,1)S(1)} %collective-permute-done.4.t2), channel_id=1, source_target_pairs={{0,1},{1,0},{2,3},{3,2},{4,5},{5,4},{6,7},{7,6},{8,9},{9,8},{10,11... | collective-permute-start | bytes 884744 | tf_op jit(solution)/shard_map/ppermute | solution.py:98
  43.5 3.1 %collective-permute-start.1 = (bf16[128,1152]{1,0:T(8,128)(2,1)}, bf16[128,1152]{1,0:T(8,128)(2,1)S(1)}, u32[]{:S(2)}, u32[]{:S(2)}) collective-permute-start(bf16[128,1152]{1,0:T(8,128)(2,1)} %images.1), channel_id=1, source_target_pairs={{0,1016},{8,0},{16,8},{24,16},{32,24},{40,32},{48,40},{56,48},{64,... | collective-permute-start | bytes 884744 | tf_op jit(solution)/shard_map/ppermute | solution.py:96
  47.8 0.0 collective-permute-done.3.t1
  47.8 0.0 collective-permute-done.2.left.last
  47.9 0.0 collective-permute-done.5.t3
  47.9 1.0 %copy-done = bf16[128,1152]{1,0:T(8,128)(2,1)S(1)} copy-done((bf16[128,1152]{1,0:T(8,128)(2,1)S(1)}, bf16[128,1152]{1,0:T(8,128)(2,1)}, u32[]{:S(2)}) %copy-start) | copy-done | bytes 294936
  48.8 0.8 shard_map.60
  49.7 0.0 copy-start.2
  49.7 2.4 %collective-permute-start.6 = (bf16[128,1152]{1,0:T(8,128)(2,1)S(1)}, bf16[128,1152]{1,0:T(8,128)(2,1)S(1)}, u32[]{:S(2)}, u32[]{:S(2)}) collective-permute-start(bf16[128,1152]{1,0:T(8,128)(2,1)S(1)} %get-tuple-element.18), channel_id=1, source_target_pairs={{0,8},{8,16},{16,24},{24,32},{32,40},{40,48},{48,56},{56,64},{64,7... | collective-permute-start | bytes 884744 | tf_op jit(solution)/shard_map/ppermute | solution.py:110
  52.0 2.2 %collective-permute-done.1.left.guests = bf16[128,1152]{1,0:T(8,128)(2,1)S(1)} collective-permute-done((bf16[128,1152]{1,0:T(8,128)(2,1)}, bf16[128,1152]{1,0:T(8,128)(2,1)S(1)}, u32[]{:S(2)}, u32[]{:S(2)}) %collective-permute-start.1) | collective-permute-done | bytes 294944 | tf_op jit(solution)/shard_map/ppermute | solution.py:96
  54.2 0.0 copy-done.1
  54.2 0.8 shard_map.59
  55.0 1.8 %shard_map.61 = (f32[128,1152]{1,0:T(8,128)S(1)}, f32[128,1152]{1,0:T(8,128)S(1)}, f32[128,1152]{1,0:T(8,128)S(1)}, f32[128,1152]{1,0:T(8,128)S(1)}, bf16[256,1152]{1,0:T(8,128)(2,1)S(1)}) custom-call(f32[1]{0:T(128)S(6)} %copy.6.stretch, f32[1]{0:T(128)S(6)} %copy.7.offset_term, bf16[128,1152]{1,0:T(8,128)(2,1)S(1)} %copy-done.2, ...), custom_call_target="tpu_custom_call" | custom-call | flops 1207959552 | tf_op jit(solution)/shard_map/pallas_call | solution.py:72
  56.8 2.7 %collective-permute-start.9 = (bf16[256,1152]{1,0:T(8,128)(2,1)S(1)}, bf16[256,1152]{1,0:T(8,128)(2,1)S(1)}, u32[]{:S(2)}, u32[]{:S(2)}) collective-permute-start(bf16[256,1152]{1,0:T(8,128)(2,1)S(1)} %get-tuple-element.24), channel_id=1, source_target_pairs={{0,1},{1,0},{2,3},{3,2},{4,5},{5,4},{6,7},{7,6},{8,9},{9,8},{10,11... | collective-permute-start | bytes 1769480 | tf_op jit(solution)/shard_map/ppermute | solution.py:118
  59.5 1.9 %collective-permute-start.7 = (bf16[128,1152]{1,0:T(8,128)(2,1)S(1)}, bf16[128,1152]{1,0:T(8,128)(2,1)S(1)}, u32[]{:S(2)}, u32[]{:S(2)}) collective-permute-start(bf16[128,1152]{1,0:T(8,128)(2,1)S(1)} %get-tuple-element.20), channel_id=1, source_target_pairs={{0,8},{8,16},{16,24},{24,32},{32,40},{40,48},{48,56},{56,64},{64,7... | collective-permute-start | bytes 884744 | tf_op jit(solution)/shard_map/ppermute | solution.py:106
  61.5 2.2 %collective-permute-done.6 = bf16[128,1152]{1,0:T(8,128)(2,1)S(1)} collective-permute-done((bf16[128,1152]{1,0:T(8,128)(2,1)S(1)}, bf16[128,1152]{1,0:T(8,128)(2,1)S(1)}, u32[]{:S(2)}, u32[]{:S(2)}) %collective-permute-start.6) | collective-permute-done | bytes 294944 | tf_op jit(solution)/shard_map/ppermute | solution.py:110
  63.7 0.1 add_convert_fusion.1
  63.7 4.7 %collective-permute-start.8 = (bf16[128,1152]{1,0:T(8,128)(2,1)S(1)}, bf16[128,1152]{1,0:T(8,128)(2,1)S(1)}, u32[]{:S(2)}, u32[]{:S(2)}) collective-permute-start(bf16[128,1152]{1,0:T(8,128)(2,1)S(1)} %add_convert_fusion.1), channel_id=1, source_target_pairs={{0,6},{1,7},{2,4},{3,5},{4,2},{5,3},{6,0},{7,1},{8,14},{9,15},{10,... | collective-permute-start | bytes 884744 | tf_op jit(solution)/shard_map/ppermute | solution.py:124
  68.5 0.0 collective-permute-done.9
  68.5 0.1 add_convert_fusion
  68.5 1.9 %collective-permute-start.10 = (bf16[128,1152]{1,0:T(8,128)(2,1)S(1)}, bf16[128,1152]{1,0:T(8,128)(2,1)S(1)}, u32[]{:S(2)}, u32[]{:S(2)}) collective-permute-start(bf16[128,1152]{1,0:T(8,128)(2,1)S(1)} %add_convert_fusion), channel_id=1, source_target_pairs={{0,2},{1,3},{2,0},{3,1},{4,6},{5,7},{6,4},{7,5},{8,10},{9,11},{10,... | collective-permute-start | bytes 884744 | tf_op jit(solution)/shard_map/ppermute | solution.py:123
  70.5 3.8 %collective-permute-done.7 = bf16[128,1152]{1,0:T(8,128)(2,1)S(1)} collective-permute-done((bf16[128,1152]{1,0:T(8,128)(2,1)S(1)}, bf16[128,1152]{1,0:T(8,128)(2,1)S(1)}, u32[]{:S(2)}, u32[]{:S(2)}) %collective-permute-start.7) | collective-permute-done | bytes 294944 | tf_op jit(solution)/shard_map/ppermute | solution.py:106
  74.3 6.6 %collective-permute-done.8 = bf16[128,1152]{1,0:T(8,128)(2,1)S(1)} collective-permute-done((bf16[128,1152]{1,0:T(8,128)(2,1)S(1)}, bf16[128,1152]{1,0:T(8,128)(2,1)S(1)}, u32[]{:S(2)}, u32[]{:S(2)}) %collective-permute-start.8) | collective-permute-done | bytes 294944 | tf_op jit(solution)/shard_map/ppermute | solution.py:124
  80.9 0.9 %convert_add_fusion.1 = f32[128,1152]{1,0:T(8,128)} fusion(bf16[128,1152]{1,0:T(8,128)(2,1)S(1)} %collective-permute-done.8, f32[128,1152]{1,0:T(8,128)S(1)} %get-tuple-element.19, bf16[128,1152]{1,0:T(8,128)(2,1)S(1)} %collective-permute-done.7), kind=kLoop, calls=%fused_computation.2 | loop fusion | flops 589824 | bytes 1769472 | tf_op jit(solution)/shard_map/add | solution.py:126
  81.8 0.0 collective-permute-done.10
  81.8 0.9 %convert_add_fusion = f32[128,1152]{1,0:T(8,128)} fusion(bf16[128,1152]{1,0:T(8,128)(2,1)S(1)} %collective-permute-done.10, f32[128,1152]{1,0:T(8,128)S(1)} %get-tuple-element.23, bf16[256,1152]{1,0:T(8,128)(2,1)S(1)} %collective-permute-done.9), kind=kLoop, calls=%fused_computation | loop fusion | flops 589824 | bytes 1769472 | tf_op jit(solution)/shard_map/add | solution.py:125
  (3 shorter events, 0.0 us)
Async XLA Ops:
  0.6 27.4 %collective-permute-start = (bf16[128,1152]{1,0:T(8,128)(2,1)}, bf16[128,1152]{1,0:T(8,128)(2,1)S(1)}, u32[]{:S(2)}, u32[]{:S(2)}) collective-permute-start(bf16[128,1152]{1,0:T(8,128)(2,1)} %images.1), channel_id=1, source_target_pairs={{0,6},{1,7},{2,4},{3,5},{4,2},{5,3},{6,0},{7,1},{8,14},{9,15},{10,... | collective-permute-start | bytes 884744 | tf_op jit(solution)/shard_map/ppermute | solution.py:93
  17.6 23.1 %collective-permute-start.4 = (bf16[128,1152]{1,0:T(8,128)(2,1)}, bf16[128,1152]{1,0:T(8,128)(2,1)S(1)}, u32[]{:S(2)}, u32[]{:S(2)}) collective-permute-start(bf16[128,1152]{1,0:T(8,128)(2,1)} %t0.5), channel_id=1, source_target_pairs={{0,2},{1,3},{2,0},{3,1},{4,6},{5,7},{6,4},{7,5},{8,10},{9,11},{10,... | collective-permute-start | bytes 884744 | tf_op jit(solution)/shard_map/ppermute | solution.py:95
  19.5 28.3 %collective-permute-start.3 = (bf16[128,1152]{1,0:T(8,128)(2,1)}, bf16[128,1152]{1,0:T(8,128)(2,1)S(1)}, u32[]{:S(2)}, u32[]{:S(2)}) collective-permute-start(bf16[128,1152]{1,0:T(8,128)(2,1)} %t0.5), channel_id=1, source_target_pairs={{0,1},{1,0},{2,3},{3,2},{4,5},{5,4},{6,7},{7,6},{8,9},{9,8},{10,11... | collective-permute-start | bytes 884744 | tf_op jit(solution)/shard_map/ppermute | solution.py:94
  28.0 19.8 %collective-permute-start.2 = (bf16[128,1152]{1,0:T(8,128)(2,1)S(1)}, bf16[128,1152]{1,0:T(8,128)(2,1)S(1)}, u32[]{:S(2)}, u32[]{:S(2)}) collective-permute-start(bf16[128,1152]{1,0:T(8,128)(2,1)S(1)} %collective-permute-done.across), channel_id=1, source_target_pairs={{0,1016},{8,0},{16,8},{24,16},{32,24},{40,32},{48,40},{56,48},{64,... | collective-permute-start | bytes 884744 | tf_op jit(solution)/shard_map/ppermute | solution.py:97
  40.7 7.1 %collective-permute-start.5 = (bf16[128,1152]{1,0:T(8,128)(2,1)S(1)}, bf16[128,1152]{1,0:T(8,128)(2,1)S(1)}, u32[]{:S(2)}, u32[]{:S(2)}) collective-permute-start(bf16[128,1152]{1,0:T(8,128)(2,1)S(1)} %collective-permute-done.4.t2), channel_id=1, source_target_pairs={{0,1},{1,0},{2,3},{3,2},{4,5},{5,4},{6,7},{7,6},{8,9},{9,8},{10,11... | collective-permute-start | bytes 884744 | tf_op jit(solution)/shard_map/ppermute | solution.py:98
  43.5 10.7 %collective-permute-start.1 = (bf16[128,1152]{1,0:T(8,128)(2,1)}, bf16[128,1152]{1,0:T(8,128)(2,1)S(1)}, u32[]{:S(2)}, u32[]{:S(2)}) collective-permute-start(bf16[128,1152]{1,0:T(8,128)(2,1)} %images.1), channel_id=1, source_target_pairs={{0,1016},{8,0},{16,8},{24,16},{32,24},{40,32},{48,40},{56,48},{64,... | collective-permute-start | bytes 884744 | tf_op jit(solution)/shard_map/ppermute | solution.py:96
  47.9 1.0 %copy-start = (bf16[128,1152]{1,0:T(8,128)(2,1)S(1)}, bf16[128,1152]{1,0:T(8,128)(2,1)}, u32[]{:S(2)}) copy-start(bf16[128,1152]{1,0:T(8,128)(2,1)} %t0.5) | copy-start | bytes 884740
  48.8 5.4 %copy-start.1 = (bf16[128,1152]{1,0:T(8,128)(2,1)S(1)}, bf16[128,1152]{1,0:T(8,128)(2,1)}, u32[]{:S(2)}) copy-start(bf16[128,1152]{1,0:T(8,128)(2,1)} %t0.5) | copy-start | bytes 884740
  49.7 5.4 %copy-start.2 = (bf16[128,1152]{1,0:T(8,128)(2,1)S(1)}, bf16[128,1152]{1,0:T(8,128)(2,1)}, u32[]{:S(2)}) copy-start(bf16[128,1152]{1,0:T(8,128)(2,1)} %images.1) | copy-start | bytes 884740
  49.7 14.0 %collective-permute-start.6 = (bf16[128,1152]{1,0:T(8,128)(2,1)S(1)}, bf16[128,1152]{1,0:T(8,128)(2,1)S(1)}, u32[]{:S(2)}, u32[]{:S(2)}) collective-permute-start(bf16[128,1152]{1,0:T(8,128)(2,1)S(1)} %get-tuple-element.18), channel_id=1, source_target_pairs={{0,8},{8,16},{16,24},{24,32},{32,40},{40,48},{48,56},{56,64},{64,7... | collective-permute-start | bytes 884744 | tf_op jit(solution)/shard_map/ppermute | solution.py:110
  56.8 11.7 %collective-permute-start.9 = (bf16[256,1152]{1,0:T(8,128)(2,1)S(1)}, bf16[256,1152]{1,0:T(8,128)(2,1)S(1)}, u32[]{:S(2)}, u32[]{:S(2)}) collective-permute-start(bf16[256,1152]{1,0:T(8,128)(2,1)S(1)} %get-tuple-element.24), channel_id=1, source_target_pairs={{0,1},{1,0},{2,3},{3,2},{4,5},{5,4},{6,7},{7,6},{8,9},{9,8},{10,11... | collective-permute-start | bytes 1769480 | tf_op jit(solution)/shard_map/ppermute | solution.py:118
  59.5 14.8 %collective-permute-start.7 = (bf16[128,1152]{1,0:T(8,128)(2,1)S(1)}, bf16[128,1152]{1,0:T(8,128)(2,1)S(1)}, u32[]{:S(2)}, u32[]{:S(2)}) collective-permute-start(bf16[128,1152]{1,0:T(8,128)(2,1)S(1)} %get-tuple-element.20), channel_id=1, source_target_pairs={{0,8},{8,16},{16,24},{24,32},{32,40},{40,48},{48,56},{56,64},{64,7... | collective-permute-start | bytes 884744 | tf_op jit(solution)/shard_map/ppermute | solution.py:106
  63.7 17.2 %collective-permute-start.8 = (bf16[128,1152]{1,0:T(8,128)(2,1)S(1)}, bf16[128,1152]{1,0:T(8,128)(2,1)S(1)}, u32[]{:S(2)}, u32[]{:S(2)}) collective-permute-start(bf16[128,1152]{1,0:T(8,128)(2,1)S(1)} %add_convert_fusion.1), channel_id=1, source_target_pairs={{0,6},{1,7},{2,4},{3,5},{4,2},{5,3},{6,0},{7,1},{8,14},{9,15},{10,... | collective-permute-start | bytes 884744 | tf_op jit(solution)/shard_map/ppermute | solution.py:124
  68.5 13.3 %collective-permute-start.10 = (bf16[128,1152]{1,0:T(8,128)(2,1)S(1)}, bf16[128,1152]{1,0:T(8,128)(2,1)S(1)}, u32[]{:S(2)}, u32[]{:S(2)}) collective-permute-start(bf16[128,1152]{1,0:T(8,128)(2,1)S(1)} %add_convert_fusion), channel_id=1, source_target_pairs={{0,2},{1,3},{2,0},{3,1},{4,6},{5,7},{6,4},{7,5},{8,10},{9,11},{10,... | collective-permute-start | bytes 884744 | tf_op jit(solution)/shard_map/ppermute | solution.py:123

commit v7 on v6

--- a/solution.py
+++ b/solution.py
@@ -37,9 +37,8 @@
     part[...] = jnp.dot(c, texts, preferred_element_type=F32).astype(BF16)
 
 
-def rest_kernel(
-    stretch, offset_term, images, across, guests, last, guests_coef, last_coef, t0, t1, t2, t3,
-    own, own_across, mine, far, for_core,
+def own_kernel(
+    stretch, offset_term, images, across, t0, t1, t2, t3, coef_out, own, own_across
 ):
     rows = images.shape[0]
     texts = stack(t0, t1, t2, t3)
@@ -52,11 +51,18 @@
         (-stretch[0] * jax.nn.sigmoid(-scores)).astype(BF16),
         (stretch[0] * jax.nn.sigmoid(scores)).astype(BF16),
     )
+    coef_out[...] = coef
     image_grads = jnp.dot(coef, texts, preferred_element_type=F32)
     own[...] = image_grads[:rows]
     own_across[...] = image_grads[rows:]
+
+
+def texts_kernel(
+    images, across, guests, last, own_coef, guests_coef, last_coef, mine, far, for_core
+):
+    rows = images.shape[0]
     text_grads = lax.dot_general(
-        jnp.concatenate([coef, guests_coef[...], last_coef[...]], axis=0),
+        stack(own_coef, guests_coef, last_coef),
         stack(images, across, guests, last),
         BY_COLUMN,
         preferred_element_type=F32,
@@ -67,16 +73,31 @@
     for_core[:rows, :] = text_grads[3 * rows :].astype(BF16)
 
 
-def local_call(kernel, outs, flops, stretch, offset_term, *arrays):
+def copy_kernel(given, taken):
+    taken[...] = given[...]
+
+
+def in_vmem(array):
+    vmem = pl.BlockSpec(memory_space=pltpu.VMEM)
+    return pl.pallas_call(
+        copy_kernel,
+        out_shape=jax.ShapeDtypeStruct(array.shape, array.dtype),
+        in_specs=[vmem],
+        out_specs=vmem,
+        compiler_params=pltpu.CompilerParams(vmem_limit_bytes=24 * 1024 * 1024),
+    )(array)
+
+
+def local_call(kernel, outs, flops, scalars, *arrays):
     vmem = pl.BlockSpec(memory_space=pltpu.VMEM)
     return pl.pallas_call(
         kernel,
         out_shape=[jax.ShapeDtypeStruct(shape, dtype) for shape, dtype in outs],
-        in_specs=[pl.BlockSpec(memory_space=pltpu.SMEM)] * 2 + [vmem] * len(arrays),
+        in_specs=[pl.BlockSpec(memory_space=pltpu.SMEM)] * len(scalars) + [vmem] * len(arrays),
         out_specs=[vmem] * len(outs),
         compiler_params=pltpu.CompilerParams(vmem_limit_bytes=24 * 1024 * 1024),
         cost_estimate=pl.CostEstimate(flops=flops, bytes_accessed=0, transcendentals=0),
-    )(stretch, offset_term, *arrays)
+    )(*scalars, *arrays)
 
 
 def per_device(images, texts, stretch, offset_term):
@@ -94,26 +115,36 @@
     texts_core = lax.ppermute(texts, "inner", other_core)
     texts_beside = lax.ppermute(texts, "inner", beside)
     guests = lax.ppermute(images, "outer", to_previous)
+    texts_here = in_vmem(texts)
+    images_across, texts_here = lax.optimization_barrier((images_across, texts_here))
     guests_across = lax.ppermute(images_across, "outer", to_previous)
     texts_beside_core = lax.ppermute(texts_beside, "inner", other_core)
-    all_texts = (texts, texts_core, texts_beside, texts_beside_core)
+    all_texts = (texts_here, texts_core, texts_beside, texts_beside_core)
 
     block = rows * width * 4 * rows * 2
+    scalars = (stretch, offset_term)
     guests_outs = [((rows, 4 * rows), BF16), ((rows, width), BF16)]
+    last_coef, last_part = local_call(
+        guests_kernel, guests_outs, 2 * block, scalars, guests_across, *all_texts
+    )
+    back_across = lax.ppermute(last_part, "outer", to_next)
+    last_coef, images_across = lax.optimization_barrier((last_coef, images_across))
+    own_coef, own, own_across = local_call(
+        own_kernel,
+        [((2 * rows, 4 * rows), BF16)] + [((rows, width), F32)] * 2,
+        4 * block,
+        scalars, images, images_across, *all_texts,
+    )
+    guests, own_coef = lax.optimization_barrier((guests, own_coef))
     guests_coef, guests_part = local_call(
-        guests_kernel, guests_outs, 2 * block, stretch, offset_term, guests, *all_texts
+        guests_kernel, guests_outs, 2 * block, scalars, guests, *all_texts
     )
     back = lax.ppermute(guests_part, "outer", to_next)
-    last_coef, last_part = local_call(
-        guests_kernel, guests_outs, 2 * block, stretch, offset_term, guests_across, *all_texts
-    )
-    back_across = lax.ppermute(last_part, "outer", to_next)
-    own, own_across, mine, far, for_core = local_call(
-        rest_kernel,
-        [((rows, width), F32)] * 4 + [((2 * rows, width), BF16)],
-        8 * block,
-        stretch, offset_term, images, images_across, guests, guests_across,
-        guests_coef, last_coef, *all_texts,
+    mine, far, for_core = local_call(
+        texts_kernel,
+        [((rows, width), F32)] * 2 + [((2 * rows, width), BF16)],
+        4 * block,
+        (), images, images_across, guests, guests_across, own_coef, guests_coef, last_coef,
     )
     from_core = lax.ppermute(for_core, "inner", other_core)
     own, own_across, back_across = lax.optimization_barrier((own, own_across, back_across))

time: 83.9 us -> 82.9 us (0.988)
  waiting for transfers between devices: 20.5 us -> 19.3 us
    ppermute x1, waiting for transfers between devices: 5.64 us -> 4.65 us  [per_device(): images_across = lax.ppermute(images, 'inner', across)]
    pallas_call x3 -> x4, Pallas kernels: 3.4 us -> 3.6 us  [local_call(): pl.pallas_call(kernel, out_shape=[jax.ShapeDtypeStruct(shape, dtype) for...]
where the time goes in v7:
time: 82.9 us; the launch traced here: 81.8 us
  starting transfers between devices  53.9 us (65%)
  waiting for transfers between devices  19.3 us (23%)
  Pallas kernels  3.62 us (4%)
  between operations  2.11 us (3%)
  other arithmetic  1.89 us (2%)
  local copies, waits for them, and re-layouts  0.96 us (1%)
    ppermute x1, starting transfers between devices, per_device(): images_across = lax.ppermute(images, 'inner', across)  16.9 us
    ppermute x1, starting transfers between devices, per_device(): guests_across = lax.ppermute(images_across, 'outer', to_previous)  12.7 us
    ppermute x1, waiting for transfers between devices, per_device(): from_across = lax.ppermute(across_sent, 'inner', across)  6.16 us
    ppermute x1, starting transfers between devices, per_device(): from_across = lax.ppermute(across_sent, 'inner', across)  4.94 us
    ppermute x1, waiting for transfers between devices, per_device(): images_across = lax.ppermute(images, 'inner', across)  4.65 us
    ppermute x1, waiting for transfers between devices, per_device(): back = lax.ppermute(guests_part, 'outer', to_next)  4.47 us
    pallas_call x4, Pallas kernels, local_call(): pl.pallas_call(kernel, out_shape=[jax.ShapeDtypeStruct(shape, dtype) for...  3.6 us
    ppermute x1, starting transfers between devices, per_device(): guests = lax.ppermute(images, 'outer', to_previous)  3.06 us
  transfers between devices with their start and end apart: 11, of which 5 were waited for; matrix products, arithmetic and copies ran while one was open for 1% of the time, Pallas kernels for 4%

profile of v7, /device:TPU:1, one launch (start us, length us, event | category | flops | bytes accessed | tf_op | source)
XLA Modules:
  0.0 81.8 jit_solution(5327907171790714560)
XLA Ops:
  0.6 16.9 %collective-permute-start = (bf16[128,1152]{1,0:T(8,128)(2,1)}, bf16[128,1152]{1,0:T(8,128)(2,1)S(1)}, u32[]{:S(2)}, u32[]{:S(2)}) collective-permute-start(bf16[128,1152]{1,0:T(8,128)(2,1)} %images.3), channel_id=1, source_target_pairs={{0,6},{1,7},{2,4},{3,5},{4,2},{5,3},{6,0},{7,1},{8,14},{9,15},{10,... | collective-permute-start | bytes 884744 | tf_op jit(solution)/shard_map/ppermute | solution.py:114
  17.6 1.9 %collective-permute-start.3 = (bf16[128,1152]{1,0:T(8,128)(2,1)}, bf16[128,1152]{1,0:T(8,128)(2,1)S(1)}, u32[]{:S(2)}, u32[]{:S(2)}) collective-permute-start(bf16[128,1152]{1,0:T(8,128)(2,1)} %given.1), channel_id=1, source_target_pairs={{0,2},{1,3},{2,0},{3,1},{4,6},{5,7},{6,4},{7,5},{8,10},{9,11},{10,... | collective-permute-start | bytes 884744 | tf_op jit(solution)/shard_map/ppermute | solution.py:116
  19.5 2.9 %collective-permute-start.2 = (bf16[128,1152]{1,0:T(8,128)(2,1)}, bf16[128,1152]{1,0:T(8,128)(2,1)S(1)}, u32[]{:S(2)}, u32[]{:S(2)}) collective-permute-start(bf16[128,1152]{1,0:T(8,128)(2,1)} %given.1), channel_id=1, source_target_pairs={{0,1},{1,0},{2,3},{3,2},{4,5},{5,4},{6,7},{7,6},{8,9},{9,8},{10,11... | collective-permute-start | bytes 884744 | tf_op jit(solution)/shard_map/ppermute | solution.py:115
  22.4 0.0 copy-start
  22.4 1.0 %copy-done = bf16[128,1152]{1,0:T(8,128)(2,1)S(1)} copy-done((bf16[128,1152]{1,0:T(8,128)(2,1)S(1)}, bf16[128,1152]{1,0:T(8,128)(2,1)}, u32[]{:S(2)}) %copy-start) | copy-done | bytes 294936
  23.4 4.6 %collective-permute-done.across = bf16[128,1152]{1,0:T(8,128)(2,1)S(1)} collective-permute-done((bf16[128,1152]{1,0:T(8,128)(2,1)}, bf16[128,1152]{1,0:T(8,128)(2,1)S(1)}, u32[]{:S(2)}, u32[]{:S(2)}) %collective-permute-start) | collective-permute-done | bytes 294944 | tf_op jit(solution)/shard_map/ppermute | solution.py:114
  28.0 12.7 %collective-permute-start.1 = (bf16[128,1152]{1,0:T(8,128)(2,1)S(1)}, bf16[128,1152]{1,0:T(8,128)(2,1)S(1)}, u32[]{:S(2)}, u32[]{:S(2)}) collective-permute-start(bf16[128,1152]{1,0:T(8,128)(2,1)S(1)} %collective-permute-done.across), channel_id=1, source_target_pairs={{0,1016},{8,0},{16,8},{24,16},{32,24},{40,32},{48,40},{56,48},{64,... | collective-permute-start | bytes 884744 | tf_op jit(solution)/shard_map/ppermute | solution.py:120
  40.7 0.0 collective-permute-done.3.t2
  40.7 2.7 %collective-permute-start.4 = (bf16[128,1152]{1,0:T(8,128)(2,1)S(1)}, bf16[128,1152]{1,0:T(8,128)(2,1)S(1)}, u32[]{:S(2)}, u32[]{:S(2)}) collective-permute-start(bf16[128,1152]{1,0:T(8,128)(2,1)S(1)} %collective-permute-done.3.t2), channel_id=1, source_target_pairs={{0,1},{1,0},{2,3},{3,2},{4,5},{5,4},{6,7},{7,6},{8,9},{9,8},{10,11... | collective-permute-start | bytes 884744 | tf_op jit(solution)/shard_map/ppermute | solution.py:121
  43.5 3.1 %collective-permute-start.6 = (bf16[128,1152]{1,0:T(8,128)(2,1)S(1)}, bf16[128,1152]{1,0:T(8,128)(2,1)S(1)}, u32[]{:S(2)}, u32[]{:S(2)}) collective-permute-start(bf16[128,1152]{1,0:T(8,128)(2,1)S(1)} %copy-done.1), channel_id=1, source_target_pairs={{0,1016},{8,0},{16,8},{24,16},{32,24},{40,32},{48,40},{56,48},{64,... | collective-permute-start | bytes 884744 | tf_op jit(solution)/shard_map/ppermute | solution.py:117
  47.8 0.0 collective-permute-done.2.t1
  47.9 0.0 collective-permute-done.1.left.last
  47.9 0.0 collective-permute-done.4.t3
  47.9 0.8 %shard_map.60 = (bf16[128,512]{1,0:T(8,128)(2,1)S(1)}, bf16[128,1152]{1,0:T(8,128)(2,1)S(1)}) custom-call(f32[1]{0:T(128)S(6)} %copy.6.stretch, f32[1]{0:T(128)S(6)} %copy.7.offset_term, bf16[128,1152]{1,0:T(8,128)(2,1)S(1)} %collective-permute-done.1.left.last, bf16[128,1152]{1,0:T(8,128)(2,1)S(1)} %shard_map.59.t0, ...), custom_call_target="tpu_custom_call" | custom-call | flops 301989888 | tf_op jit(solution)/shard_map/pallas_call | solution.py:93
  48.7 2.2 %collective-permute-start.5 = (bf16[128,1152]{1,0:T(8,128)(2,1)S(1)}, bf16[128,1152]{1,0:T(8,128)(2,1)S(1)}, u32[]{:S(2)}, u32[]{:S(2)}) collective-permute-start(bf16[128,1152]{1,0:T(8,128)(2,1)S(1)} %get-tuple-element.27), channel_id=1, source_target_pairs={{0,8},{8,16},{16,24},{24,32},{32,40},{40,48},{48,56},{56,64},{64,7... | collective-permute-start | bytes 884744 | tf_op jit(solution)/shard_map/ppermute | solution.py:130
  50.9 1.1 %shard_map.61 = (bf16[256,512]{1,0:T(8,128)(2,1)S(1)}, f32[128,1152]{1,0:T(8,128)S(1)}, f32[128,1152]{1,0:T(8,128)S(1)}) custom-call(f32[1]{0:T(128)S(6)} %copy.6.stretch, f32[1]{0:T(128)S(6)} %copy.7.offset_term, bf16[128,1152]{1,0:T(8,128)(2,1)S(1)} %copy-done.1, bf16[128,1152]{1,0:T(8,128)(2,1)S(1)} %collective-permute-done.across, ...), custom_call_target="tpu_custom_call" | custom-call | flops 603979776 | tf_op jit(solution)/shard_map/pallas_call | solution.py:93
  52.0 2.0 %collective-permute-done.6.left.guests = bf16[128,1152]{1,0:T(8,128)(2,1)S(1)} collective-permute-done((bf16[128,1152]{1,0:T(8,128)(2,1)S(1)}, bf16[128,1152]{1,0:T(8,128)(2,1)S(1)}, u32[]{:S(2)}, u32[]{:S(2)}) %collective-permute-start.6) | collective-permute-done | bytes 294944 | tf_op jit(solution)/shard_map/ppermute | solution.py:117
  54.0 0.8 %shard_map.62 = (bf16[128,512]{1,0:T(8,128)(2,1)S(1)}, bf16[128,1152]{1,0:T(8,128)(2,1)S(1)}) custom-call(f32[1]{0:T(128)S(6)} %copy.6.stretch, f32[1]{0:T(128)S(6)} %copy.7.offset_term, bf16[128,1152]{1,0:T(8,128)(2,1)S(1)} %collective-permute-done.6.left.guests, bf16[128,1152]{1,0:T(8,128)(2,1)S(1)} %shard_map.59.t0, ...), custom_call_target="tpu_custom_call" | custom-call | flops 301989888 | tf_op jit(solution)/shard_map/pallas_call | solution.py:93
  54.8 0.9 %shard_map.63 = (f32[128,1152]{1,0:T(8,128)S(1)}, f32[128,1152]{1,0:T(8,128)S(1)}, bf16[256,1152]{1,0:T(8,128)(2,1)S(1)}) custom-call(bf16[128,1152]{1,0:T(8,128)(2,1)S(1)} %copy-done.1, bf16[128,1152]{1,0:T(8,128)(2,1)S(1)} %collective-permute-done.across, bf16[128,1152]{1,0:T(8,128)(2,1)S(1)} %collective-permute-done.6.left.guests, ...), custom_call_target="tpu_custom_call" | custom-call | flops 603979776 | tf_op jit(solution)/shard_map/pallas_call | solution.py:93
  55.7 2.7 %collective-permute-start.9 = (bf16[256,1152]{1,0:T(8,128)(2,1)S(1)}, bf16[256,1152]{1,0:T(8,128)(2,1)S(1)}, u32[]{:S(2)}, u32[]{:S(2)}) collective-permute-start(bf16[256,1152]{1,0:T(8,128)(2,1)S(1)} %get-tuple-element.38), channel_id=1, source_target_pairs={{0,1},{1,0},{2,3},{3,2},{4,5},{5,4},{6,7},{7,6},{8,9},{9,8},{10,11... | collective-permute-start | bytes 1769480 | tf_op jit(solution)/shard_map/ppermute | solution.py:149
  58.4 1.9 %collective-permute-start.7 = (bf16[128,1152]{1,0:T(8,128)(2,1)S(1)}, bf16[128,1152]{1,0:T(8,128)(2,1)S(1)}, u32[]{:S(2)}, u32[]{:S(2)}) collective-permute-start(bf16[128,1152]{1,0:T(8,128)(2,1)S(1)} %get-tuple-element.31), channel_id=1, source_target_pairs={{0,8},{8,16},{16,24},{24,32},{32,40},{40,48},{48,56},{56,64},{64,7... | collective-permute-start | bytes 884744 | tf_op jit(solution)/shard_map/ppermute | solution.py:142
  60.4 2.0 %collective-permute-done.5 = bf16[128,1152]{1,0:T(8,128)(2,1)S(1)} collective-permute-done((bf16[128,1152]{1,0:T(8,128)(2,1)S(1)}, bf16[128,1152]{1,0:T(8,128)(2,1)S(1)}, u32[]{:S(2)}, u32[]{:S(2)}) %collective-permute-start.5) | collective-permute-done | bytes 294944 | tf_op jit(solution)/shard_map/ppermute | solution.py:130
  62.4 0.1 add_convert_fusion.1
  62.4 4.9 %collective-permute-start.8 = (bf16[128,1152]{1,0:T(8,128)(2,1)S(1)}, bf16[128,1152]{1,0:T(8,128)(2,1)S(1)}, u32[]{:S(2)}, u32[]{:S(2)}) collective-permute-start(bf16[128,1152]{1,0:T(8,128)(2,1)S(1)} %add_convert_fusion.1), channel_id=1, source_target_pairs={{0,6},{1,7},{2,4},{3,5},{4,2},{5,3},{6,0},{7,1},{8,14},{9,15},{10,... | collective-permute-start | bytes 884744 | tf_op jit(solution)/shard_map/ppermute | solution.py:155
  67.4 0.0 collective-permute-done.9
  67.4 0.1 add_convert_fusion
  67.4 1.9 %collective-permute-start.10 = (bf16[128,1152]{1,0:T(8,128)(2,1)S(1)}, bf16[128,1152]{1,0:T(8,128)(2,1)S(1)}, u32[]{:S(2)}, u32[]{:S(2)}) collective-permute-start(bf16[128,1152]{1,0:T(8,128)(2,1)S(1)} %add_convert_fusion), channel_id=1, source_target_pairs={{0,2},{1,3},{2,0},{3,1},{4,6},{5,7},{6,4},{7,5},{8,10},{9,11},{10,... | collective-permute-start | bytes 884744 | tf_op jit(solution)/shard_map/ppermute | solution.py:154
  69.4 4.5 %collective-permute-done.7 = bf16[128,1152]{1,0:T(8,128)(2,1)S(1)} collective-permute-done((bf16[128,1152]{1,0:T(8,128)(2,1)S(1)}, bf16[128,1152]{1,0:T(8,128)(2,1)S(1)}, u32[]{:S(2)}, u32[]{:S(2)}) %collective-permute-start.7) | collective-permute-done | bytes 294944 | tf_op jit(solution)/shard_map/ppermute | solution.py:142
  73.8 6.2 %collective-permute-done.8 = bf16[128,1152]{1,0:T(8,128)(2,1)S(1)} collective-permute-done((bf16[128,1152]{1,0:T(8,128)(2,1)S(1)}, bf16[128,1152]{1,0:T(8,128)(2,1)S(1)}, u32[]{:S(2)}, u32[]{:S(2)}) %collective-permute-start.8) | collective-permute-done | bytes 294944 | tf_op jit(solution)/shard_map/ppermute | solution.py:155
  80.0 0.9 %convert_add_fusion.1 = f32[128,1152]{1,0:T(8,128)} fusion(bf16[128,1152]{1,0:T(8,128)(2,1)S(1)} %collective-permute-done.8, f32[128,1152]{1,0:T(8,128)S(1)} %get-tuple-element.28, bf16[128,1152]{1,0:T(8,128)(2,1)S(1)} %collective-permute-done.7), kind=kLoop, calls=%fused_computation.2 | loop fusion | flops 589824 | bytes 1769472 | tf_op jit(solution)/shard_map/add | solution.py:157
  80.9 0.0 collective-permute-done.10
  80.9 0.9 %convert_add_fusion = f32[128,1152]{1,0:T(8,128)} fusion(bf16[128,1152]{1,0:T(8,128)(2,1)S(1)} %collective-permute-done.10, f32[128,1152]{1,0:T(8,128)S(1)} %get-tuple-element.37, bf16[256,1152]{1,0:T(8,128)(2,1)S(1)} %collective-permute-done.9), kind=kLoop, calls=%fused_computation | loop fusion | flops 589824 | bytes 1769472 | tf_op jit(solution)/shard_map/add | solution.py:156
  (3 shorter events, 0.0 us)
Async XLA Ops:
  0.6 27.4 %collective-permute-start = (bf16[128,1152]{1,0:T(8,128)(2,1)}, bf16[128,1152]{1,0:T(8,128)(2,1)S(1)}, u32[]{:S(2)}, u32[]{:S(2)}) collective-permute-start(bf16[128,1152]{1,0:T(8,128)(2,1)} %images.3), channel_id=1, source_target_pairs={{0,6},{1,7},{2,4},{3,5},{4,2},{5,3},{6,0},{7,1},{8,14},{9,15},{10,... | collective-permute-start | bytes 884744 | tf_op jit(solution)/shard_map/ppermute | solution.py:114
  17.6 23.1 %collective-permute-start.3 = (bf16[128,1152]{1,0:T(8,128)(2,1)}, bf16[128,1152]{1,0:T(8,128)(2,1)S(1)}, u32[]{:S(2)}, u32[]{:S(2)}) collective-permute-start(bf16[128,1152]{1,0:T(8,128)(2,1)} %given.1), channel_id=1, source_target_pairs={{0,2},{1,3},{2,0},{3,1},{4,6},{5,7},{6,4},{7,5},{8,10},{9,11},{10,... | collective-permute-start | bytes 884744 | tf_op jit(solution)/shard_map/ppermute | solution.py:116
  19.5 28.3 %collective-permute-start.2 = (bf16[128,1152]{1,0:T(8,128)(2,1)}, bf16[128,1152]{1,0:T(8,128)(2,1)S(1)}, u32[]{:S(2)}, u32[]{:S(2)}) collective-permute-start(bf16[128,1152]{1,0:T(8,128)(2,1)} %given.1), channel_id=1, source_target_pairs={{0,1},{1,0},{2,3},{3,2},{4,5},{5,4},{6,7},{7,6},{8,9},{9,8},{10,11... | collective-permute-start | bytes 884744 | tf_op jit(solution)/shard_map/ppermute | solution.py:115
  22.4 1.0 %copy-start = (bf16[128,1152]{1,0:T(8,128)(2,1)S(1)}, bf16[128,1152]{1,0:T(8,128)(2,1)}, u32[]{:S(2)}) copy-start(bf16[128,1152]{1,0:T(8,128)(2,1)} %given.1) | copy-start | bytes 884740
  23.3 20.1 %copy-start.1 = (bf16[128,1152]{1,0:T(8,128)(2,1)S(1)}, bf16[128,1152]{1,0:T(8,128)(2,1)}, u32[]{:S(2)}) copy-start(bf16[128,1152]{1,0:T(8,128)(2,1)} %images.3) | copy-start | bytes 884740
  28.0 19.8 %collective-permute-start.1 = (bf16[128,1152]{1,0:T(8,128)(2,1)S(1)}, bf16[128,1152]{1,0:T(8,128)(2,1)S(1)}, u32[]{:S(2)}, u32[]{:S(2)}) collective-permute-start(bf16[128,1152]{1,0:T(8,128)(2,1)S(1)} %collective-permute-done.across), channel_id=1, source_target_pairs={{0,1016},{8,0},{16,8},{24,16},{32,24},{40,32},{48,40},{56,48},{64,... | collective-permute-start | bytes 884744 | tf_op jit(solution)/shard_map/ppermute | solution.py:120
  40.7 7.1 %collective-permute-start.4 = (bf16[128,1152]{1,0:T(8,128)(2,1)S(1)}, bf16[128,1152]{1,0:T(8,128)(2,1)S(1)}, u32[]{:S(2)}, u32[]{:S(2)}) collective-permute-start(bf16[128,1152]{1,0:T(8,128)(2,1)S(1)} %collective-permute-done.3.t2), channel_id=1, source_target_pairs={{0,1},{1,0},{2,3},{3,2},{4,5},{5,4},{6,7},{7,6},{8,9},{9,8},{10,11... | collective-permute-start | bytes 884744 | tf_op jit(solution)/shard_map/ppermute | solution.py:121
  43.5 10.5 %collective-permute-start.6 = (bf16[128,1152]{1,0:T(8,128)(2,1)S(1)}, bf16[128,1152]{1,0:T(8,128)(2,1)S(1)}, u32[]{:S(2)}, u32[]{:S(2)}) collective-permute-start(bf16[128,1152]{1,0:T(8,128)(2,1)S(1)} %copy-done.1), channel_id=1, source_target_pairs={{0,1016},{8,0},{16,8},{24,16},{32,24},{40,32},{48,40},{56,48},{64,... | collective-permute-start | bytes 884744 | tf_op jit(solution)/shard_map/ppermute | solution.py:117
  48.7 13.7 %collective-permute-start.5 = (bf16[128,1152]{1,0:T(8,128)(2,1)S(1)}, bf16[128,1152]{1,0:T(8,128)(2,1)S(1)}, u32[]{:S(2)}, u32[]{:S(2)}) collective-permute-start(bf16[128,1152]{1,0:T(8,128)(2,1)S(1)} %get-tuple-element.27), channel_id=1, source_target_pairs={{0,8},{8,16},{16,24},{24,32},{32,40},{40,48},{48,56},{56,64},{64,7... | collective-permute-start | bytes 884744 | tf_op jit(solution)/shard_map/ppermute | solution.py:130
  55.7 11.7 %collective-permute-start.9 = (bf16[256,1152]{1,0:T(8,128)(2,1)S(1)}, bf16[256,1152]{1,0:T(8,128)(2,1)S(1)}, u32[]{:S(2)}, u32[]{:S(2)}) collective-permute-start(bf16[256,1152]{1,0:T(8,128)(2,1)S(1)} %get-tuple-element.38), channel_id=1, source_target_pairs={{0,1},{1,0},{2,3},{3,2},{4,5},{5,4},{6,7},{7,6},{8,9},{9,8},{10,11... | collective-permute-start | bytes 1769480 | tf_op jit(solution)/shard_map/ppermute | solution.py:149
  58.4 15.4 %collective-permute-start.7 = (bf16[128,1152]{1,0:T(8,128)(2,1)S(1)}, bf16[128,1152]{1,0:T(8,128)(2,1)S(1)}, u32[]{:S(2)}, u32[]{:S(2)}) collective-permute-start(bf16[128,1152]{1,0:T(8,128)(2,1)S(1)} %get-tuple-element.31), channel_id=1, source_target_pairs={{0,8},{8,16},{16,24},{24,32},{32,40},{40,48},{48,56},{56,64},{64,7... | collective-permute-start | bytes 884744 | tf_op jit(solution)/shard_map/ppermute | solution.py:142
  62.4 17.6 %collective-permute-start.8 = (bf16[128,1152]{1,0:T(8,128)(2,1)S(1)}, bf16[128,1152]{1,0:T(8,128)(2,1)S(1)}, u32[]{:S(2)}, u32[]{:S(2)}) collective-permute-start(bf16[128,1152]{1,0:T(8,128)(2,1)S(1)} %add_convert_fusion.1), channel_id=1, source_target_pairs={{0,6},{1,7},{2,4},{3,5},{4,2},{5,3},{6,0},{7,1},{8,14},{9,15},{10,... | collective-permute-start | bytes 884744 | tf_op jit(solution)/shard_map/ppermute | solution.py:155
  67.4 13.5 %collective-permute-start.10 = (bf16[128,1152]{1,0:T(8,128)(2,1)S(1)}, bf16[128,1152]{1,0:T(8,128)(2,1)S(1)}, u32[]{:S(2)}, u32[]{:S(2)}) collective-permute-start(bf16[128,1152]{1,0:T(8,128)(2,1)S(1)} %add_convert_fusion), channel_id=1, source_target_pairs={{0,2},{1,3},{2,0},{3,1},{4,6},{5,7},{6,4},{7,5},{8,10},{9,11},{10,... | collective-permute-start | bytes 884744 | tf_op jit(solution)/shard_map/ppermute | solution.py:154

commit v8 on v7

--- a/solution.py
+++ b/solution.py
@@ -73,19 +73,20 @@
     for_core[:rows, :] = text_grads[3 * rows :].astype(BF16)
 
 
-def copy_kernel(given, taken):
+def copy_kernel(stretch, offset_term, given, taken):
+    del stretch, offset_term
     taken[...] = given[...]
 
 
-def in_vmem(array):
+def in_vmem(stretch, offset_term, array):
     vmem = pl.BlockSpec(memory_space=pltpu.VMEM)
     return pl.pallas_call(
         copy_kernel,
         out_shape=jax.ShapeDtypeStruct(array.shape, array.dtype),
-        in_specs=[vmem],
+        in_specs=[pl.BlockSpec(memory_space=pltpu.SMEM)] * 2 + [vmem],
         out_specs=vmem,
         compiler_params=pltpu.CompilerParams(vmem_limit_bytes=24 * 1024 * 1024),
-    )(array)
+    )(stretch, offset_term, array)
 
 
 def local_call(kernel, outs, flops, scalars, *arrays):
@@ -115,7 +116,7 @@
     texts_core = lax.ppermute(texts, "inner", other_core)
     texts_beside = lax.ppermute(texts, "inner", beside)
     guests = lax.ppermute(images, "outer", to_previous)
-    texts_here = in_vmem(texts)
+    texts_here = in_vmem(stretch, offset_term, texts)
     images_across, texts_here = lax.optimization_barrier((images_across, texts_here))
     guests_across = lax.ppermute(images_across, "outer", to_previous)
     texts_beside_core = lax.ppermute(texts_beside, "inner", other_core)

time: 82.9 us -> 82.8 us (level)
    ppermute x1, waiting for transfers between devices: 4.47 us -> 7.45 us  [per_device(): back = lax.ppermute(guests_part, 'outer', to_next)]
    ppermute x1, waiting for transfers between devices: 1.99 us -> 3.28 us  [per_device(): guests = lax.ppermute(images, 'outer', to_previous)]
    ppermute x1, waiting for transfers between devices: 4.65 us -> 3.36 us  [per_device(): images_across = lax.ppermute(images, 'inner', across)]
    ppermute x1, waiting for transfers between devices: 2.02 us -> 0.83 us  [per_device(): back_across = lax.ppermute(last_part, 'outer', to_next)]
    ppermute x1, waiting for transfers between devices: 6.16 us -> 5.04 us  [per_device(): from_across = lax.ppermute(across_sent, 'inner', across)]
where the time goes in v8:
time: 82.8 us; the launch traced here: 81.9 us
  starting transfers between devices  53.3 us (64%)
  waiting for transfers between devices  20 us (24%)
  Pallas kernels  3.63 us (4%)
  between operations  2.1 us (3%)
  other arithmetic  1.89 us (2%)
  local copies, waits for them, and re-layouts  0.96 us (1%)
    ppermute x1, starting transfers between devices, per_device(): images_across = lax.ppermute(images, 'inner', across)  16.9 us
    ppermute x1, starting transfers between devices, per_device(): guests_across = lax.ppermute(images_across, 'outer', to_previous)  12.7 us
    ppermute x1, waiting for transfers between devices, per_device(): back = lax.ppermute(guests_part, 'outer', to_next)  7.45 us
    ppermute x1, waiting for transfers between devices, per_device(): from_across = lax.ppermute(across_sent, 'inner', across)  5.04 us
    ppermute x1, starting transfers between devices, per_device(): from_across = lax.ppermute(across_sent, 'inner', across)  4.32 us
    pallas_call x4, Pallas kernels, local_call(): pl.pallas_call(kernel, out_shape=[jax.ShapeDtypeStruct(shape, dtype) for...  3.61 us
    ppermute x1, waiting for transfers between devices, per_device(): images_across = lax.ppermute(images, 'inner', across)  3.36 us
    ppermute x1, waiting for transfers between devices, per_device(): guests = lax.ppermute(images, 'outer', to_previous)  3.28 us
  transfers between devices with their start and end apart: 11, of which 5 were waited for; matrix products, arithmetic and copies ran while one was open for 1% of the time, Pallas kernels for 4%

profile of v8, /device:TPU:1, one launch (start us, length us, event | category | flops | bytes accessed | tf_op | source)
XLA Modules:
  0.0 81.9 jit_solution(3110081257940574911)
XLA Ops:
  0.6 16.9 %collective-permute-start = (bf16[128,1152]{1,0:T(8,128)(2,1)}, bf16[128,1152]{1,0:T(8,128)(2,1)S(1)}, u32[]{:S(2)}, u32[]{:S(2)}) collective-permute-start(bf16[128,1152]{1,0:T(8,128)(2,1)} %images.3), channel_id=1, source_target_pairs={{0,6},{1,7},{2,4},{3,5},{4,2},{5,3},{6,0},{7,1},{8,14},{9,15},{10,... | collective-permute-start | bytes 884744 | tf_op jit(solution)/shard_map/ppermute | solution.py:115
  17.6 1.9 %collective-permute-start.3 = (bf16[128,1152]{1,0:T(8,128)(2,1)}, bf16[128,1152]{1,0:T(8,128)(2,1)S(1)}, u32[]{:S(2)}, u32[]{:S(2)}) collective-permute-start(bf16[128,1152]{1,0:T(8,128)(2,1)} %given.1), channel_id=1, source_target_pairs={{0,2},{1,3},{2,0},{3,1},{4,6},{5,7},{6,4},{7,5},{8,10},{9,11},{10,... | collective-permute-start | bytes 884744 | tf_op jit(solution)/shard_map/ppermute | solution.py:117
  19.5 2.9 %collective-permute-start.2 = (bf16[128,1152]{1,0:T(8,128)(2,1)}, bf16[128,1152]{1,0:T(8,128)(2,1)S(1)}, u32[]{:S(2)}, u32[]{:S(2)}) collective-permute-start(bf16[128,1152]{1,0:T(8,128)(2,1)} %given.1), channel_id=1, source_target_pairs={{0,1},{1,0},{2,3},{3,2},{4,5},{5,4},{6,7},{7,6},{8,9},{9,8},{10,11... | collective-permute-start | bytes 884744 | tf_op jit(solution)/shard_map/ppermute | solution.py:116
  23.7 1.0 %copy-done = bf16[128,1152]{1,0:T(8,128)(2,1)S(1)} copy-done((bf16[128,1152]{1,0:T(8,128)(2,1)S(1)}, bf16[128,1152]{1,0:T(8,128)(2,1)}, u32[]{:S(2)}) %copy-start) | copy-done | bytes 294936
  24.7 3.4 %collective-permute-done.across = bf16[128,1152]{1,0:T(8,128)(2,1)S(1)} collective-permute-done((bf16[128,1152]{1,0:T(8,128)(2,1)}, bf16[128,1152]{1,0:T(8,128)(2,1)S(1)}, u32[]{:S(2)}, u32[]{:S(2)}) %collective-permute-start) | collective-permute-done | bytes 294944 | tf_op jit(solution)/shard_map/ppermute | solution.py:115
  28.0 12.7 %collective-permute-start.1 = (bf16[128,1152]{1,0:T(8,128)(2,1)S(1)}, bf16[128,1152]{1,0:T(8,128)(2,1)S(1)}, u32[]{:S(2)}, u32[]{:S(2)}) collective-permute-start(bf16[128,1152]{1,0:T(8,128)(2,1)S(1)} %collective-permute-done.across), channel_id=1, source_target_pairs={{0,1016},{8,0},{16,8},{24,16},{32,24},{40,32},{48,40},{56,48},{64,... | collective-permute-start | bytes 884744 | tf_op jit(solution)/shard_map/ppermute | solution.py:121
  40.7 0.0 collective-permute-done.3.t2
  40.7 2.7 %collective-permute-start.4 = (bf16[128,1152]{1,0:T(8,128)(2,1)S(1)}, bf16[128,1152]{1,0:T(8,128)(2,1)S(1)}, u32[]{:S(2)}, u32[]{:S(2)}) collective-permute-start(bf16[128,1152]{1,0:T(8,128)(2,1)S(1)} %collective-permute-done.3.t2), channel_id=1, source_target_pairs={{0,1},{1,0},{2,3},{3,2},{4,5},{5,4},{6,7},{7,6},{8,9},{9,8},{10,11... | collective-permute-start | bytes 884744 | tf_op jit(solution)/shard_map/ppermute | solution.py:122
  43.5 0.0 copy-done.1
  43.5 3.1 %collective-permute-start.6 = (bf16[128,1152]{1,0:T(8,128)(2,1)S(1)}, bf16[128,1152]{1,0:T(8,128)(2,1)S(1)}, u32[]{:S(2)}, u32[]{:S(2)}) collective-permute-start(bf16[128,1152]{1,0:T(8,128)(2,1)S(1)} %copy-done.1), channel_id=1, source_target_pairs={{0,1016},{8,0},{16,8},{24,16},{32,24},{40,32},{48,40},{56,48},{64,... | collective-permute-start | bytes 884744 | tf_op jit(solution)/shard_map/ppermute | solution.py:118
  46.5 0.0 collective-permute-done.2.t1
  46.6 0.0 collective-permute-done.1.left.last
  46.6 0.0 collective-permute-done.4.t3
  46.6 0.8 %shard_map.60 = (bf16[128,512]{1,0:T(8,128)(2,1)S(1)}, bf16[128,1152]{1,0:T(8,128)(2,1)S(1)}) custom-call(f32[1]{0:T(128)S(6)} %copy.6.stretch, f32[1]{0:T(128)S(6)} %copy.7.offset_term, bf16[128,1152]{1,0:T(8,128)(2,1)S(1)} %collective-permute-done.1.left.last, bf16[128,1152]{1,0:T(8,128)(2,1)S(1)} %shard_map.59.t0, ...), custom_call_target="tpu_custom_call" | custom-call | flops 301989888 | tf_op jit(solution)/shard_map/pallas_call | solution.py:94
  47.4 2.2 %collective-permute-start.5 = (bf16[128,1152]{1,0:T(8,128)(2,1)S(1)}, bf16[128,1152]{1,0:T(8,128)(2,1)S(1)}, u32[]{:S(2)}, u32[]{:S(2)}) collective-permute-start(bf16[128,1152]{1,0:T(8,128)(2,1)S(1)} %get-tuple-element.27), channel_id=1, source_target_pairs={{0,8},{8,16},{16,24},{24,32},{32,40},{40,48},{48,56},{56,64},{64,7... | collective-permute-start | bytes 884744 | tf_op jit(solution)/shard_map/ppermute | solution.py:131
  49.6 1.1 %shard_map.61 = (bf16[256,512]{1,0:T(8,128)(2,1)S(1)}, f32[128,1152]{1,0:T(8,128)S(1)}, f32[128,1152]{1,0:T(8,128)S(1)}) custom-call(f32[1]{0:T(128)S(6)} %copy.6.stretch, f32[1]{0:T(128)S(6)} %copy.7.offset_term, bf16[128,1152]{1,0:T(8,128)(2,1)S(1)} %copy-done.1, bf16[128,1152]{1,0:T(8,128)(2,1)S(1)} %collective-permute-done.across, ...), custom_call_target="tpu_custom_call" | custom-call | flops 603979776 | tf_op jit(solution)/shard_map/pallas_call | solution.py:94
  50.7 3.3 %collective-permute-done.6.left.guests = bf16[128,1152]{1,0:T(8,128)(2,1)S(1)} collective-permute-done((bf16[128,1152]{1,0:T(8,128)(2,1)S(1)}, bf16[128,1152]{1,0:T(8,128)(2,1)S(1)}, u32[]{:S(2)}, u32[]{:S(2)}) %collective-permute-start.6) | collective-permute-done | bytes 294944 | tf_op jit(solution)/shard_map/ppermute | solution.py:118
  54.0 0.8 %shard_map.62 = (bf16[128,512]{1,0:T(8,128)(2,1)S(1)}, bf16[128,1152]{1,0:T(8,128)(2,1)S(1)}) custom-call(f32[1]{0:T(128)S(6)} %copy.6.stretch, f32[1]{0:T(128)S(6)} %copy.7.offset_term, bf16[128,1152]{1,0:T(8,128)(2,1)S(1)} %collective-permute-done.6.left.guests, bf16[128,1152]{1,0:T(8,128)(2,1)S(1)} %shard_map.59.t0, ...), custom_call_target="tpu_custom_call" | custom-call | flops 301989888 | tf_op jit(solution)/shard_map/pallas_call | solution.py:94
  54.8 0.9 %shard_map.63 = (f32[128,1152]{1,0:T(8,128)S(1)}, f32[128,1152]{1,0:T(8,128)S(1)}, bf16[256,1152]{1,0:T(8,128)(2,1)S(1)}) custom-call(bf16[128,1152]{1,0:T(8,128)(2,1)S(1)} %copy-done.1, bf16[128,1152]{1,0:T(8,128)(2,1)S(1)} %collective-permute-done.across, bf16[128,1152]{1,0:T(8,128)(2,1)S(1)} %collective-permute-done.6.left.guests, ...), custom_call_target="tpu_custom_call" | custom-call | flops 603979776 | tf_op jit(solution)/shard_map/pallas_call | solution.py:94
  55.7 2.7 %collective-permute-start.9 = (bf16[256,1152]{1,0:T(8,128)(2,1)S(1)}, bf16[256,1152]{1,0:T(8,128)(2,1)S(1)}, u32[]{:S(2)}, u32[]{:S(2)}) collective-permute-start(bf16[256,1152]{1,0:T(8,128)(2,1)S(1)} %get-tuple-element.38), channel_id=1, source_target_pairs={{0,1},{1,0},{2,3},{3,2},{4,5},{5,4},{6,7},{7,6},{8,9},{9,8},{10,11... | collective-permute-start | bytes 1769480 | tf_op jit(solution)/shard_map/ppermute | solution.py:150
  58.4 1.9 %collective-permute-start.7 = (bf16[128,1152]{1,0:T(8,128)(2,1)S(1)}, bf16[128,1152]{1,0:T(8,128)(2,1)S(1)}, u32[]{:S(2)}, u32[]{:S(2)}) collective-permute-start(bf16[128,1152]{1,0:T(8,128)(2,1)S(1)} %get-tuple-element.31), channel_id=1, source_target_pairs={{0,8},{8,16},{16,24},{24,32},{32,40},{40,48},{48,56},{56,64},{64,7... | collective-permute-start | bytes 884744 | tf_op jit(solution)/shard_map/ppermute | solution.py:143
  60.4 0.8 %collective-permute-done.5 = bf16[128,1152]{1,0:T(8,128)(2,1)S(1)} collective-permute-done((bf16[128,1152]{1,0:T(8,128)(2,1)S(1)}, bf16[128,1152]{1,0:T(8,128)(2,1)S(1)}, u32[]{:S(2)}, u32[]{:S(2)}) %collective-permute-start.5) | collective-permute-done | bytes 294944 | tf_op jit(solution)/shard_map/ppermute | solution.py:131
  61.2 0.1 add_convert_fusion.1
  61.2 4.3 %collective-permute-start.8 = (bf16[128,1152]{1,0:T(8,128)(2,1)S(1)}, bf16[128,1152]{1,0:T(8,128)(2,1)S(1)}, u32[]{:S(2)}, u32[]{:S(2)}) collective-permute-start(bf16[128,1152]{1,0:T(8,128)(2,1)S(1)} %add_convert_fusion.1), channel_id=1, source_target_pairs={{0,6},{1,7},{2,4},{3,5},{4,2},{5,3},{6,0},{7,1},{8,14},{9,15},{10,... | collective-permute-start | bytes 884744 | tf_op jit(solution)/shard_map/ppermute | solution.py:156
  65.6 0.0 collective-permute-done.9
  65.6 0.1 add_convert_fusion
  65.6 1.9 %collective-permute-start.10 = (bf16[128,1152]{1,0:T(8,128)(2,1)S(1)}, bf16[128,1152]{1,0:T(8,128)(2,1)S(1)}, u32[]{:S(2)}, u32[]{:S(2)}) collective-permute-start(bf16[128,1152]{1,0:T(8,128)(2,1)S(1)} %add_convert_fusion), channel_id=1, source_target_pairs={{0,2},{1,3},{2,0},{3,1},{4,6},{5,7},{6,4},{7,5},{8,10},{9,11},{10,... | collective-permute-start | bytes 884744 | tf_op jit(solution)/shard_map/ppermute | solution.py:155
  67.6 7.5 %collective-permute-done.7 = bf16[128,1152]{1,0:T(8,128)(2,1)S(1)} collective-permute-done((bf16[128,1152]{1,0:T(8,128)(2,1)S(1)}, bf16[128,1152]{1,0:T(8,128)(2,1)S(1)}, u32[]{:S(2)}, u32[]{:S(2)}) %collective-permute-start.7) | collective-permute-done | bytes 294944 | tf_op jit(solution)/shard_map/ppermute | solution.py:143
  75.0 5.0 %collective-permute-done.8 = bf16[128,1152]{1,0:T(8,128)(2,1)S(1)} collective-permute-done((bf16[128,1152]{1,0:T(8,128)(2,1)S(1)}, bf16[128,1152]{1,0:T(8,128)(2,1)S(1)}, u32[]{:S(2)}, u32[]{:S(2)}) %collective-permute-start.8) | collective-permute-done | bytes 294944 | tf_op jit(solution)/shard_map/ppermute | solution.py:156
  80.1 0.9 %convert_add_fusion.1 = f32[128,1152]{1,0:T(8,128)} fusion(bf16[128,1152]{1,0:T(8,128)(2,1)S(1)} %collective-permute-done.8, f32[128,1152]{1,0:T(8,128)S(1)} %get-tuple-element.28, bf16[128,1152]{1,0:T(8,128)(2,1)S(1)} %collective-permute-done.7), kind=kLoop, calls=%fused_computation.2 | loop fusion | flops 589824 | bytes 1769472 | tf_op jit(solution)/shard_map/add | solution.py:158
  81.0 0.0 collective-permute-done.10
  81.0 0.9 %convert_add_fusion = f32[128,1152]{1,0:T(8,128)} fusion(bf16[128,1152]{1,0:T(8,128)(2,1)S(1)} %collective-permute-done.10, f32[128,1152]{1,0:T(8,128)S(1)} %get-tuple-element.37, bf16[256,1152]{1,0:T(8,128)(2,1)S(1)} %collective-permute-done.9), kind=kLoop, calls=%fused_computation | loop fusion | flops 589824 | bytes 1769472 | tf_op jit(solution)/shard_map/add | solution.py:157
  (3 shorter events, 0.0 us)
Async XLA Ops:
  0.6 27.4 %collective-permute-start = (bf16[128,1152]{1,0:T(8,128)(2,1)}, bf16[128,1152]{1,0:T(8,128)(2,1)S(1)}, u32[]{:S(2)}, u32[]{:S(2)}) collective-permute-start(bf16[128,1152]{1,0:T(8,128)(2,1)} %images.3), channel_id=1, source_target_pairs={{0,6},{1,7},{2,4},{3,5},{4,2},{5,3},{6,0},{7,1},{8,14},{9,15},{10,... | collective-permute-start | bytes 884744 | tf_op jit(solution)/shard_map/ppermute | solution.py:115
  17.6 23.1 %collective-permute-start.3 = (bf16[128,1152]{1,0:T(8,128)(2,1)}, bf16[128,1152]{1,0:T(8,128)(2,1)S(1)}, u32[]{:S(2)}, u32[]{:S(2)}) collective-permute-start(bf16[128,1152]{1,0:T(8,128)(2,1)} %given.1), channel_id=1, source_target_pairs={{0,2},{1,3},{2,0},{3,1},{4,6},{5,7},{6,4},{7,5},{8,10},{9,11},{10,... | collective-permute-start | bytes 884744 | tf_op jit(solution)/shard_map/ppermute | solution.py:117
  19.5 27.0 %collective-permute-start.2 = (bf16[128,1152]{1,0:T(8,128)(2,1)}, bf16[128,1152]{1,0:T(8,128)(2,1)S(1)}, u32[]{:S(2)}, u32[]{:S(2)}) collective-permute-start(bf16[128,1152]{1,0:T(8,128)(2,1)} %given.1), channel_id=1, source_target_pairs={{0,1},{1,0},{2,3},{3,2},{4,5},{5,4},{6,7},{7,6},{8,9},{9,8},{10,11... | collective-permute-start | bytes 884744 | tf_op jit(solution)/shard_map/ppermute | solution.py:116
  23.7 1.0 %copy-start = (bf16[128,1152]{1,0:T(8,128)(2,1)S(1)}, bf16[128,1152]{1,0:T(8,128)(2,1)}, u32[]{:S(2)}) copy-start(bf16[128,1152]{1,0:T(8,128)(2,1)} %given.1) | copy-start | bytes 884740
  24.6 18.8 %copy-start.1 = (bf16[128,1152]{1,0:T(8,128)(2,1)S(1)}, bf16[128,1152]{1,0:T(8,128)(2,1)}, u32[]{:S(2)}) copy-start(bf16[128,1152]{1,0:T(8,128)(2,1)} %images.3) | copy-start | bytes 884740
  28.0 18.5 %collective-permute-start.1 = (bf16[128,1152]{1,0:T(8,128)(2,1)S(1)}, bf16[128,1152]{1,0:T(8,128)(2,1)S(1)}, u32[]{:S(2)}, u32[]{:S(2)}) collective-permute-start(bf16[128,1152]{1,0:T(8,128)(2,1)S(1)} %collective-permute-done.across), channel_id=1, source_target_pairs={{0,1016},{8,0},{16,8},{24,16},{32,24},{40,32},{48,40},{56,48},{64,... | collective-permute-start | bytes 884744 | tf_op jit(solution)/shard_map/ppermute | solution.py:121
  40.7 5.8 %collective-permute-start.4 = (bf16[128,1152]{1,0:T(8,128)(2,1)S(1)}, bf16[128,1152]{1,0:T(8,128)(2,1)S(1)}, u32[]{:S(2)}, u32[]{:S(2)}) collective-permute-start(bf16[128,1152]{1,0:T(8,128)(2,1)S(1)} %collective-permute-done.3.t2), channel_id=1, source_target_pairs={{0,1},{1,0},{2,3},{3,2},{4,5},{5,4},{6,7},{7,6},{8,9},{9,8},{10,11... | collective-permute-start | bytes 884744 | tf_op jit(solution)/shard_map/ppermute | solution.py:122
  43.5 10.5 %collective-permute-start.6 = (bf16[128,1152]{1,0:T(8,128)(2,1)S(1)}, bf16[128,1152]{1,0:T(8,128)(2,1)S(1)}, u32[]{:S(2)}, u32[]{:S(2)}) collective-permute-start(bf16[128,1152]{1,0:T(8,128)(2,1)S(1)} %copy-done.1), channel_id=1, source_target_pairs={{0,1016},{8,0},{16,8},{24,16},{32,24},{40,32},{48,40},{56,48},{64,... | collective-permute-start | bytes 884744 | tf_op jit(solution)/shard_map/ppermute | solution.py:118
  47.4 13.8 %collective-permute-start.5 = (bf16[128,1152]{1,0:T(8,128)(2,1)S(1)}, bf16[128,1152]{1,0:T(8,128)(2,1)S(1)}, u32[]{:S(2)}, u32[]{:S(2)}) collective-permute-start(bf16[128,1152]{1,0:T(8,128)(2,1)S(1)} %get-tuple-element.27), channel_id=1, source_target_pairs={{0,8},{8,16},{16,24},{24,32},{32,40},{40,48},{48,56},{56,64},{64,7... | collective-permute-start | bytes 884744 | tf_op jit(solution)/shard_map/ppermute | solution.py:131
  55.7 9.9 %collective-permute-start.9 = (bf16[256,1152]{1,0:T(8,128)(2,1)S(1)}, bf16[256,1152]{1,0:T(8,128)(2,1)S(1)}, u32[]{:S(2)}, u32[]{:S(2)}) collective-permute-start(bf16[256,1152]{1,0:T(8,128)(2,1)S(1)} %get-tuple-element.38), channel_id=1, source_target_pairs={{0,1},{1,0},{2,3},{3,2},{4,5},{5,4},{6,7},{7,6},{8,9},{9,8},{10,11... | collective-permute-start | bytes 1769480 | tf_op jit(solution)/shard_map/ppermute | solution.py:150
  58.4 16.6 %collective-permute-start.7 = (bf16[128,1152]{1,0:T(8,128)(2,1)S(1)}, bf16[128,1152]{1,0:T(8,128)(2,1)S(1)}, u32[]{:S(2)}, u32[]{:S(2)}) collective-permute-start(bf16[128,1152]{1,0:T(8,128)(2,1)S(1)} %get-tuple-element.31), channel_id=1, source_target_pairs={{0,8},{8,16},{16,24},{24,32},{32,40},{40,48},{48,56},{56,64},{64,7... | collective-permute-start | bytes 884744 | tf_op jit(solution)/shard_map/ppermute | solution.py:143
  61.2 18.8 %collective-permute-start.8 = (bf16[128,1152]{1,0:T(8,128)(2,1)S(1)}, bf16[128,1152]{1,0:T(8,128)(2,1)S(1)}, u32[]{:S(2)}, u32[]{:S(2)}) collective-permute-start(bf16[128,1152]{1,0:T(8,128)(2,1)S(1)} %add_convert_fusion.1), channel_id=1, source_target_pairs={{0,6},{1,7},{2,4},{3,5},{4,2},{5,3},{6,0},{7,1},{8,14},{9,15},{10,... | collective-permute-start | bytes 884744 | tf_op jit(solution)/shard_map/ppermute | solution.py:156
  65.6 15.3 %collective-permute-start.10 = (bf16[128,1152]{1,0:T(8,128)(2,1)S(1)}, bf16[128,1152]{1,0:T(8,128)(2,1)S(1)}, u32[]{:S(2)}, u32[]{:S(2)}) collective-permute-start(bf16[128,1152]{1,0:T(8,128)(2,1)S(1)} %add_convert_fusion), channel_id=1, source_target_pairs={{0,2},{1,3},{2,0},{3,1},{4,6},{5,7},{6,4},{7,5},{8,10},{9,11},{10,... | collective-permute-start | bytes 884744 | tf_op jit(solution)/shard_map/ppermute | solution.py:155
